TPU v7x, 32 devices: a whole 2x2x4 slice. The times are simulated.
32 devices in a mesh: groups: 2 (over y), phi: 4 (over z), gz: 2 (over x), row: 2 (over core).
Axes of the slice: x: 2, y: 2, z: 4, core: 2. Of those that a mesh axis runs over, the one named last changes fastest.
Arguments:
- field: float32 [6, 16, 32, 256], P('groups', 'row', 'phi', 'gz'), parts along dimension 0, may hold values from -900 to 900
- velocity: float32 [6, 16, 32, 256], P('groups', 'row', 'phi', 'gz'), parts along dimension 0, may hold values from -4 to 4
- basis: float32 [16, 3, 16, 32, 256], P('groups', None, 'row', 'phi', 'gz'), parts along dimension 0, may hold values from -200 to 200
- wall_region: int32 [64, 256], P(('groups', 'phi'), 'gz'), parts along dimension 0, may hold values from 0 to 7
- wall_conductance: float32 [16], P('groups'), parts along dimension 0, may hold values from 0.1 to 10
Outputs:
- next_vector: float32 [6, 16, 32, 256], P('groups', 'row', 'phi', 'gz'), parts along dimension 0
- hessenberg: float32 [18], P('groups'), parts along dimension 0
There are 2 independent parts, one for each index of `groups`. A program takes and returns all parts, laid end to end along the dimension named above; each array names one. Nothing has to cross between parts.
All inputs are finite; a program needn't handle non-finite values.
Results may differ from a plain program's by a relative error of at most 0.00015.
Values sent between devices are 32-bit elements; how exact they have to be, the bound alone decides.
No kernel may reach another device: no remote copies, remote signals or barrier semaphores. Data moves between devices by JAX's collectives and lax.ppermute only.
A program may use at most 64 MiB of HBM per device.

v0:
```python
import jax
import jax.numpy as jnp
from jax import lax
from jax.sharding import PartitionSpec as P

advect_step = 0.2
diffuse_step = 0.1
epsilon = 1e-06


def with_halo(block, sides, width, periodic):
    for axis, dim in sides:
        count = lax.axis_size(axis)
        forward = [(i, i + 1) for i in range(count - 1)]
        if periodic:
            forward.append((count - 1, 0))
        backward = [(target, source) for source, target in forward]
        low = lax.ppermute(
            lax.slice_in_dim(block, block.shape[dim] - width, None, axis=dim), axis, forward
        )
        high = lax.ppermute(lax.slice_in_dim(block, 0, width, axis=dim), axis, backward)
        block = jnp.concatenate([low, block, high], axis=dim)
    return block


def from_behind(value, axis, steps):
    count = lax.axis_size(axis)
    pairs = [(source, (source + steps) % count) for source in range(count)]
    return lax.ppermute(value, axis, pairs)


def cell_part(padded, radial_step, azimuth_step, axial_step):
    radial_count = padded.shape[1] - 2
    azimuth_count = padded.shape[2] - 2
    axial_count = padded.shape[3] - 2
    return padded[
        :,
        1 + radial_step : 1 + radial_step + radial_count,
        1 + azimuth_step : 1 + azimuth_step + azimuth_count,
        1 + axial_step : 1 + axial_step + axial_count,
    ]


def velocity_terms(padded_velocity):
    center = cell_part(padded_velocity, 0, 0, 0)
    radial_grad = 0.5 * (cell_part(padded_velocity, 1, 0, 0) - cell_part(padded_velocity, -1, 0, 0))
    azimuth_grad = 0.5 * (
        cell_part(padded_velocity, 0, 1, 0) - cell_part(padded_velocity, 0, -1, 0)
    )
    axial_grad = 0.5 * (cell_part(padded_velocity, 0, 0, 1) - cell_part(padded_velocity, 0, 0, -1))
    return (center, radial_grad, azimuth_grad, axial_grad)


def tendency(padded, motion, radius):
    center_speed, radial_grad, azimuth_grad, axial_grad = motion
    center = cell_part(padded, 0, 0, 0)
    outward = cell_part(padded, 1, 0, 0)
    inward = cell_part(padded, -1, 0, 0)
    forward = cell_part(padded, 0, 1, 0)
    behind = cell_part(padded, 0, -1, 0)
    above_cell = cell_part(padded, 0, 0, 1)
    below_cell = cell_part(padded, 0, 0, -1)
    radial_speed = center_speed[0]
    azimuth_speed = center_speed[1]
    axial_speed = center_speed[2]
    upwind = (
        jnp.maximum(radial_speed, 0.0) * (center - inward)
        + jnp.minimum(radial_speed, 0.0) * (outward - center)
        + jnp.maximum(azimuth_speed, 0.0) * (center - behind)
        + jnp.minimum(azimuth_speed, 0.0) * (forward - center)
        + jnp.maximum(axial_speed, 0.0) * (center - below_cell)
        + jnp.minimum(axial_speed, 0.0) * (above_cell - center)
    )
    stretch = center[0] * radial_grad + center[1] * azimuth_grad + center[2] * axial_grad
    induction = stretch - upwind
    bending = (center[1] * radial_speed - azimuth_speed * center[0]) / radius
    laplace = (
        ((radius + 0.5) * (outward - center) - (radius - 0.5) * (center - inward)) / radius
        + (forward + behind - 2.0 * center)
        + (above_cell + below_cell - 2.0 * center)
    )
    turning = 0.5 * (forward - behind)
    inverse_square = 1.0 / (radius * radius)
    diffuse_radial = laplace[0] - center[0] * inverse_square - 2.0 * turning[1] / radius
    diffuse_azimuth = laplace[1] - center[1] * inverse_square + 2.0 * turning[0] / radius
    diffuse_axial = laplace[2]
    radial_rate = advect_step * induction[0] + diffuse_step * diffuse_radial
    azimuth_rate = advect_step * (induction[1] + bending) + diffuse_step * diffuse_azimuth
    axial_rate = advect_step * induction[2] + diffuse_step * diffuse_axial
    return jnp.stack([radial_rate, azimuth_rate, axial_rate])


def extend_local(fields, flip_signs, wall_factors):
    half_turn = lax.axis_size("phi") // 2
    beside_all = with_halo(fields, (("phi", 2),), 1, True)
    padded = with_halo(beside_all, (("row", 1), ("gz", 3)), 1, False)
    opposite = from_behind(beside_all[:, 0], "phi", half_turn)
    axis_layer = jnp.pad(opposite * flip_signs[:, None, None], ((0, 0), (0, 0), (1, 1)))
    middle = padded[:, 1:-1]
    inner_side = padded[:, 0]
    outer_side = padded[:, -1]
    wall_layer = jnp.pad(fields[:, -1] * wall_factors, ((0, 0), (1, 1), (1, 1)))
    row_position = lax.axis_index("row")
    inner_layer = jnp.where(row_position == 0, axis_layer, inner_side)
    outer_layer = jnp.where(row_position == lax.axis_size("row") - 1, wall_layer, outer_side)
    return jnp.concatenate([inner_layer[:, None], middle, outer_layer[:, None]], axis=1)


def remainder_energy(remaining):
    return lax.psum(jnp.sum(remaining * remaining), ("phi", "gz", "row"))


def local(field, velocity, basis, wall_region, wall_conductance):
    regions = wall_conductance.shape[0]
    one_hot = (
        wall_region[None, :, :] == jnp.arange(regions, dtype=jnp.int32)[:, None, None]
    ).astype(jnp.float32)
    conductance = jnp.sum(one_hot * wall_conductance[:, None, None], axis=0)
    reflect = 1.0 - 2.0 * conductance / (1.0 + conductance)
    field_wall = jnp.broadcast_to(reflect[None], (3,) + reflect.shape)
    unity = jnp.ones_like(reflect)
    velocity_wall = jnp.stack([-unity, unity, unity])
    flip_signs = jnp.array([-1.0, -1.0, 1.0], dtype=jnp.float32)
    radial_cells = field.shape[1]
    radius = (
        (lax.axis_index("row") * radial_cells + jnp.arange(radial_cells, dtype=jnp.int32)).astype(
            jnp.float32
        )
        + 0.5
    )[:, None, None]
    joined = extend_local(
        jnp.concatenate([field, velocity], axis=0),
        jnp.concatenate([flip_signs, flip_signs]),
        jnp.concatenate([field_wall, velocity_wall], axis=0),
    )
    motion = velocity_terms(joined[3:])
    section_one = field + tendency(joined[:3], motion, radius)
    second = 0.75 * field + 0.25 * (
        section_one + tendency(extend_local(section_one, flip_signs, field_wall), motion, radius)
    )
    advanced = field / 3.0 + 2.0 / 3.0 * (
        second + tendency(extend_local(second, flip_signs, field_wall), motion, radius)
    )
    cell_count = float(
        field.size * lax.axis_size("phi") * lax.axis_size("gz") * lax.axis_size("row")
    )
    vectors = basis.shape[0]
    remaining = advanced
    weights = []
    squares = lax.psum(jnp.sum(basis * basis, axis=(1, 2, 3, 4)), ("phi", "gz", "row"))
    for position in range(vectors):
        vector = basis[position]
        weight = lax.psum(jnp.sum(vector * remaining), ("phi", "gz", "row")) / squares[position]
        weights.append(weight)
        remaining = remaining - weight * vector
    energy = remainder_energy(remaining)
    spread = jnp.sqrt(energy / cell_count + epsilon)
    return (remaining / spread, jnp.concatenate([jnp.stack(weights), spread[None]]))


def solution(mesh):
    return jax.shard_map(
        local,
        mesh=mesh,
        in_specs=(
            P("groups", "row", "phi", "gz"),
            P("groups", "row", "phi", "gz"),
            P("groups", None, "row", "phi", "gz"),
            P(("groups", "phi"), "gz"),
            P("groups"),
        ),
        out_specs=(P("groups", "row", "phi", "gz"), P("groups")),
        check_vma=False,
    )
```

profile of v0, /device:TPU:0, one launch (start us, length us, event | category | flops | bytes accessed | tf_op | source)
XLA Modules:
  0.0 375.5 jit_solution(6699828556092457907)
XLA Ops:
  0.6 1.0 fusion.115
  1.7 5.1 %collective-permute-start.1 = (f32[6,8,1,128]{3,2,0,1:T(1,128)S(1)}, f32[6,8,1,128]{3,2,0,1:T(1,128)S(1)}, u32[]{:S(2)}, u32[]{:S(2)}) collective-permute-start(f32[6,8,1,128]{3,2,0,1:T(1,128)S(1)} %get-tuple-element.63), channel_id=1, source_target_pairs={{4,0},{8,4},{12,8},{0,12},{5,1},{9,5},{13,9},{1,13},{6,2},{10,6},{... | collective-permute-start | bytes 73736 | tf_op jit(solution)/shard_map/ppermute | solution.py:21
  6.9 0.6 copy-done.3
  7.8 1.3 multiply_reduce_fusion
  9.2 3.2 collective-permute-done
  12.5 1.3 collective-permute-start.3
  13.8 3.0 collective-permute-start.2
  17.9 3.4 collective-permute-start.4
  21.4 1.3 collective-permute-start.5
  22.8 13.7 %collective-permute-done.5 = f32[6,10,10,1]{3,2,0,1:T(8,128)S(1)} collective-permute-done((f32[6,10,10,1]{3,2,0,1:T(8,128)S(1)}, f32[6,10,10,1]{3,2,0,1:T(8,128)S(1)}, u32[]{:S(2)}, u32[]{:S(2)}) %collective-permute-start.5) | collective-permute-done | bytes 2432 | tf_op jit(solution)/shard_map/ppermute | solution.py:21
  36.7 0.7 pad_maximum_fusion
  38.3 3.8 %collective-permute-start.8 = (f32[3,8,1,128]{3,2,0,1:T(1,128)S(1)}, f32[3,8,1,128]{3,2,0,1:T(1,128)S(1)}, u32[]{:S(2)}, u32[]{:S(2)}) collective-permute-start(f32[3,8,1,128]{3,2,0,1:T(1,128)S(1)} %get-tuple-element.83), channel_id=1, source_target_pairs={{4,0},{8,4},{12,8},{0,12},{5,1},{9,5},{13,9},{1,13},{6,2},{10,6},{... | collective-permute-start | bytes 36872 | tf_op jit(solution)/shard_map/ppermute | solution.py:21
  42.1 1.7 collective-permute-done.7
  43.9 1.3 collective-permute-start.10
  45.2 1.3 collective-permute-start.11
  46.5 0.8 collective-permute-start.9
  47.2 1.0 collective-permute-done.11
  48.4 1.5 collective-permute-start.12
  49.9 1.3 collective-permute-start.13
  51.4 4.0 %collective-permute-done.12 = f32[3,10,10,1]{3,2,0,1:T(8,128)S(1)} collective-permute-done((f32[3,10,10,1]{3,2,0,1:T(8,128)S(1)}, f32[3,10,10,1]{3,2,0,1:T(8,128)S(1)}, u32[]{:S(2)}, u32[]{:S(2)}) %collective-permute-start.12) | collective-permute-done | bytes 1232 | tf_op jit(solution)/shard_map/ppermute | solution.py:18
  55.5 4.1 %collective-permute-done.13 = f32[3,10,10,1]{3,2,0,1:T(8,128)S(1)} collective-permute-done((f32[3,10,10,1]{3,2,0,1:T(8,128)S(1)}, f32[3,10,10,1]{3,2,0,1:T(8,128)S(1)}, u32[]{:S(2)}, u32[]{:S(2)}) %collective-permute-start.13) | collective-permute-done | bytes 1232 | tf_op jit(solution)/shard_map/ppermute | solution.py:21
  60.7 3.4 collective-permute-start.14
  64.7 1.7 collective-permute-done.14
  66.3 1.5 collective-permute-done.15
  67.8 1.3 collective-permute-start.17
  69.1 1.3 collective-permute-start.18
  70.5 1.1 collective-permute-start.16
  71.6 0.7 collective-permute-done.18
  72.4 1.5 collective-permute-start.19
  73.9 1.3 collective-permute-start.20
  75.6 3.9 %collective-permute-done.19 = f32[3,10,10,1]{3,2,0,1:T(8,128)S(1)} collective-permute-done((f32[3,10,10,1]{3,2,0,1:T(8,128)S(1)}, f32[3,10,10,1]{3,2,0,1:T(8,128)S(1)}, u32[]{:S(2)}, u32[]{:S(2)}) %collective-permute-start.19) | collective-permute-done | bytes 1232 | tf_op jit(solution)/shard_map/ppermute | solution.py:18
  79.5 4.1 %collective-permute-done.20 = f32[3,10,10,1]{3,2,0,1:T(8,128)S(1)} collective-permute-done((f32[3,10,10,1]{3,2,0,1:T(8,128)S(1)}, f32[3,10,10,1]{3,2,0,1:T(8,128)S(1)}, u32[]{:S(2)}, u32[]{:S(2)}) %collective-permute-start.20) | collective-permute-done | bytes 1232 | tf_op jit(solution)/shard_map/ppermute | solution.py:21
  84.9 0.9 copy-done.1
  85.8 0.6 fusion.54
  86.4 30.2 %all-reduce.6 = (f32[]{:T(128)}, f32[8]{0:T(128)S(1)}) all-reduce(f32[]{:T(128)} %get-tuple-element.12, f32[8]{0:T(128)S(1)} %multiply_reduce_fusion), channel_id=1, replica_groups=mesh['groups'=2,'phi'=4,'gz'=2,'row'=2] {'phi','gz','row'}, use_global_device_ids=true, to_apply=%region_2.3 | all-reduce | flops 9 | bytes 72 | tf_op jit(solution)/shard_map/psum | solution.py:153
  116.6 0.7 fusion.118
  119.1 30.1 %psum.72 = f32[]{:T(128)} all-reduce(f32[]{:T(128)} %fusion.52), channel_id=1, replica_groups=mesh['groups'=2,'phi'=4,'gz'=2,'row'=2] {'phi','gz','row'}, use_global_device_ids=true, to_apply=%region_6.7 | all-reduce | flops 1 | bytes 8 | tf_op jit(solution)/shard_map/psum | solution.py:153
  150.5 0.6 fusion.50
  151.2 30.1 %psum.73 = f32[]{:T(128)} all-reduce(f32[]{:T(128)} %get-tuple-element.10), channel_id=1, replica_groups=mesh['groups'=2,'phi'=4,'gz'=2,'row'=2] {'phi','gz','row'}, use_global_device_ids=true, to_apply=%region_8.9 | all-reduce | flops 1 | bytes 8 | tf_op jit(solution)/shard_map/psum | solution.py:153
  183.2 30.1 %psum.74 = f32[]{:T(128)} all-reduce(f32[]{:T(128)} %fusion.48), channel_id=1, replica_groups=mesh['groups'=2,'phi'=4,'gz'=2,'row'=2] {'phi','gz','row'}, use_global_device_ids=true, to_apply=%region_10.11 | all-reduce | flops 1 | bytes 8 | tf_op jit(solution)/shard_map/psum | solution.py:153
  214.6 0.6 fusion.46
  215.2 30.1 %psum.75 = f32[]{:T(128)} all-reduce(f32[]{:T(128)} %get-tuple-element.8), channel_id=1, replica_groups=mesh['groups'=2,'phi'=4,'gz'=2,'row'=2] {'phi','gz','row'}, use_global_device_ids=true, to_apply=%region_12.13 | all-reduce | flops 1 | bytes 8 | tf_op jit(solution)/shard_map/psum | solution.py:153
  247.2 30.1 %psum.76 = f32[]{:T(128)} all-reduce(f32[]{:T(128)} %fusion.44), channel_id=1, replica_groups=mesh['groups'=2,'phi'=4,'gz'=2,'row'=2] {'phi','gz','row'}, use_global_device_ids=true, to_apply=%region_14.15 | all-reduce | flops 1 | bytes 8 | tf_op jit(solution)/shard_map/psum | solution.py:153
  278.7 0.6 fusion.42
  279.3 30.1 %psum.77 = f32[]{:T(128)} all-reduce(f32[]{:T(128)} %get-tuple-element.6), channel_id=1, replica_groups=mesh['groups'=2,'phi'=4,'gz'=2,'row'=2] {'phi','gz','row'}, use_global_device_ids=true, to_apply=%region_16.17 | all-reduce | flops 1 | bytes 8 | tf_op jit(solution)/shard_map/psum | solution.py:153
  311.4 30.1 %psum.78 = f32[]{:T(128)} all-reduce(f32[]{:T(128)} %fusion.40), channel_id=1, replica_groups=mesh['groups'=2,'phi'=4,'gz'=2,'row'=2] {'phi','gz','row'}, use_global_device_ids=true, to_apply=%region_18.19 | all-reduce | flops 1 | bytes 8 | tf_op jit(solution)/shard_map/psum | solution.py:153
  343.5 30.1 %psum.79 = f32[]{:T(128)} all-reduce(f32[]{:T(128)} %get-tuple-element.4), channel_id=1, replica_groups=mesh['groups'=2,'phi'=4,'gz'=2,'row'=2] {'phi','gz','row'}, use_global_device_ids=true, to_apply=%region_20.21 | all-reduce | flops 1 | bytes 8 | tf_op jit(solution)/shard_map/psum | solution.py:110
  374.3 0.7 broadcast_divide_fusion
  (87 shorter events, 10.4 us)
Async XLA Ops:
  0.6 6.2 %copy-start.2 = (f32[3,8,8,128]{3,2,1,0:T(8,128)S(1)}, f32[3,8,8,128]{3,2,1,0:T(8,128)}, u32[]{:S(2)}) copy-start(f32[3,8,8,128]{3,2,1,0:T(8,128)} %param.7) | copy-start | bytes 294916
  1.6 5.2 %copy-start = (f32[3,8,8,128]{3,2,1,0:T(8,128)S(1)}, f32[3,8,8,128]{3,2,1,0:T(8,128)}, u32[]{:S(2)}) copy-start(f32[3,8,8,128]{3,2,1,0:T(8,128)} %param.6) | copy-start | bytes 294916
  1.7 7.5 %collective-permute-start.1 = (f32[6,8,1,128]{3,2,0,1:T(1,128)S(1)}, f32[6,8,1,128]{3,2,0,1:T(1,128)S(1)}, u32[]{:S(2)}, u32[]{:S(2)}) collective-permute-start(f32[6,8,1,128]{3,2,0,1:T(1,128)S(1)} %get-tuple-element.63), channel_id=1, source_target_pairs={{4,0},{8,4},{12,8},{0,12},{5,1},{9,5},{13,9},{1,13},{6,2},{10,6},{... | collective-permute-start | bytes 73736 | tf_op jit(solution)/shard_map/ppermute | solution.py:21
  6.8 5.6 %collective-permute-start = (f32[6,8,1,128]{3,2,0,1:T(1,128)S(1)}, f32[6,8,1,128]{3,2,0,1:T(1,128)S(1)}, u32[]{:S(2)}, u32[]{:S(2)}) collective-permute-start(f32[6,8,1,128]{3,2,0,1:T(1,128)S(1)} %get-tuple-element.62), channel_id=1, source_target_pairs={{0,4},{4,8},{8,12},{12,0},{1,5},{5,9},{9,13},{13,1},{2,6},{6,10},{... | collective-permute-start | bytes 73736 | tf_op jit(solution)/shard_map/ppermute | solution.py:18
  6.8 0.7 copy-start.3
  6.9 0.7 copy-start.6
  12.5 4.6 %collective-permute-start.3 = (f32[6,1,10,128]{3,2,0,1:T(8,128)S(1)}, f32[6,1,10,128]{3,2,0,1:T(8,128)S(1)}, u32[]{:S(2)}, u32[]{:S(2)}) collective-permute-start(f32[6,1,10,128]{3,2,0,1:T(8,128)S(1)} %get-tuple-element.51), channel_id=1, source_target_pairs={{1,0},{3,2},{5,4},{7,6},{9,8},{11,10},{13,12},{15,14},{17,16},{19,... | collective-permute-start | bytes 92168 | tf_op jit(solution)/shard_map/ppermute | solution.py:21
  13.8 3.9 %collective-permute-start.2 = (f32[6,1,10,128]{3,2,0,1:T(8,128)S(1)}, f32[6,1,10,128]{3,2,0,1:T(8,128)S(1)}, u32[]{:S(2)}, u32[]{:S(2)}) collective-permute-start(f32[6,1,10,128]{3,2,0,1:T(8,128)S(1)} %get-tuple-element.50), channel_id=1, source_target_pairs={{0,1},{2,3},{4,5},{6,7},{8,9},{10,11},{12,13},{14,15},{16,17},{18,... | collective-permute-start | bytes 92168 | tf_op jit(solution)/shard_map/ppermute | solution.py:18
  16.8 5.9 %collective-permute-start.6 = (f32[6,10,128]{2,1,0:T(8,128)S(1)}, f32[6,10,128]{2,1,0:T(8,128)S(1)}, u32[]{:S(2)}, u32[]{:S(2)}) collective-permute-start(f32[6,10,128]{2,1,0:T(8,128)S(1)} %bitcast.204), channel_id=1, source_target_pairs={{0,8},{4,12},{8,0},{12,4},{1,9},{5,13},{9,1},{13,5},{2,10},{6,14},... | collective-permute-start | bytes 92168 | tf_op jit(solution)/shard_map/ppermute | solution.py:29
  17.9 4.8 %copy-start.5 = (f32[6]{0:T(128)S(1)}, f32[6]{0:T(128)}, u32[]{:S(2)}) copy-start(f32[6]{0:T(128)} %constant.67) | copy-start | bytes 76
  17.9 18.8 %collective-permute-start.4 = (f32[6,10,10,1]{3,2,0,1:T(8,128)S(1)}, f32[6,10,10,1]{3,2,0,1:T(8,128)S(1)}, u32[]{:S(2)}, u32[]{:S(2)}) collective-permute-start(f32[6,10,10,1]{3,2,0,1:T(8,128)S(1)} %get-tuple-element.31), channel_id=1, source_target_pairs={{0,2},{1,3},{4,6},{5,7},{8,10},{9,11},{12,14},{13,15},{16,18},{17,... | collective-permute-start | bytes 7208 | tf_op jit(solution)/shard_map/ppermute | solution.py:18
  21.4 15.1 %collective-permute-start.5 = (f32[6,10,10,1]{3,2,0,1:T(8,128)S(1)}, f32[6,10,10,1]{3,2,0,1:T(8,128)S(1)}, u32[]{:S(2)}, u32[]{:S(2)}) collective-permute-start(f32[6,10,10,1]{3,2,0,1:T(8,128)S(1)} %get-tuple-element.32), channel_id=1, source_target_pairs={{2,0},{3,1},{6,4},{7,5},{10,8},{11,9},{14,12},{15,13},{18,16},{19,... | collective-permute-start | bytes 7208 | tf_op jit(solution)/shard_map/ppermute | solution.py:21
  38.2 5.5 %collective-permute-start.7 = (f32[3,8,1,128]{3,2,0,1:T(1,128)S(1)}, f32[3,8,1,128]{3,2,0,1:T(1,128)S(1)}, u32[]{:S(2)}, u32[]{:S(2)}) collective-permute-start(f32[3,8,1,128]{3,2,0,1:T(1,128)S(1)} %get-tuple-element.82), channel_id=1, source_target_pairs={{0,4},{4,8},{8,12},{12,0},{1,5},{5,9},{9,13},{13,1},{2,6},{6,10},{... | collective-permute-start | bytes 36872 | tf_op jit(solution)/shard_map/ppermute | solution.py:18
  38.3 5.5 %collective-permute-start.8 = (f32[3,8,1,128]{3,2,0,1:T(1,128)S(1)}, f32[3,8,1,128]{3,2,0,1:T(1,128)S(1)}, u32[]{:S(2)}, u32[]{:S(2)}) collective-permute-start(f32[3,8,1,128]{3,2,0,1:T(1,128)S(1)} %get-tuple-element.83), channel_id=1, source_target_pairs={{4,0},{8,4},{12,8},{0,12},{5,1},{9,5},{13,9},{1,13},{6,2},{10,6},{... | collective-permute-start | bytes 36872 | tf_op jit(solution)/shard_map/ppermute | solution.py:21
  43.9 3.4 collective-permute-start.10
  45.2 3.1 collective-permute-start.11
  46.5 4.9 %collective-permute-start.9 = (f32[3,10,128]{2,1,0:T(8,128)S(1)}, f32[3,10,128]{2,1,0:T(8,128)S(1)}, u32[]{:S(2)}, u32[]{:S(2)}) collective-permute-start(f32[3,10,128]{2,1,0:T(8,128)S(1)} %get-tuple-element.56), channel_id=1, source_target_pairs={{0,8},{4,12},{8,0},{12,4},{1,9},{5,13},{9,1},{13,5},{2,10},{6,14},... | collective-permute-start | bytes 46088 | tf_op jit(solution)/shard_map/ppermute | solution.py:29
  48.4 3.0 copy-start.4
  48.4 7.1 %collective-permute-start.12 = (f32[3,10,10,1]{3,2,0,1:T(8,128)S(1)}, f32[3,10,10,1]{3,2,0,1:T(8,128)S(1)}, u32[]{:S(2)}, u32[]{:S(2)}) collective-permute-start(f32[3,10,10,1]{3,2,0,1:T(8,128)S(1)} %get-tuple-element.48), channel_id=1, source_target_pairs={{0,2},{1,3},{4,6},{5,7},{8,10},{9,11},{12,14},{13,15},{16,18},{17,... | collective-permute-start | bytes 3608 | tf_op jit(solution)/shard_map/ppermute | solution.py:18
  49.9 9.8 %collective-permute-start.13 = (f32[3,10,10,1]{3,2,0,1:T(8,128)S(1)}, f32[3,10,10,1]{3,2,0,1:T(8,128)S(1)}, u32[]{:S(2)}, u32[]{:S(2)}) collective-permute-start(f32[3,10,10,1]{3,2,0,1:T(8,128)S(1)} %get-tuple-element.49), channel_id=1, source_target_pairs={{2,0},{3,1},{6,4},{7,5},{10,8},{11,9},{14,12},{15,13},{18,16},{19,... | collective-permute-start | bytes 3608 | tf_op jit(solution)/shard_map/ppermute | solution.py:21
  60.7 5.6 %collective-permute-start.14 = (f32[3,8,1,128]{3,2,0,1:T(1,128)S(1)}, f32[3,8,1,128]{3,2,0,1:T(1,128)S(1)}, u32[]{:S(2)}, u32[]{:S(2)}) collective-permute-start(f32[3,8,1,128]{3,2,0,1:T(1,128)S(1)} %get-tuple-element.77), channel_id=1, source_target_pairs={{0,4},{4,8},{8,12},{12,0},{1,5},{5,9},{9,13},{13,1},{2,6},{6,10},{... | collective-permute-start | bytes 36872 | tf_op jit(solution)/shard_map/ppermute | solution.py:18
  64.1 3.7 collective-permute-start.15
  67.8 3.7 collective-permute-start.17
  69.1 3.1 collective-permute-start.18
  70.5 5.1 %collective-permute-start.16 = (f32[3,10,128]{2,1,0:T(8,128)S(1)}, f32[3,10,128]{2,1,0:T(8,128)S(1)}, u32[]{:S(2)}, u32[]{:S(2)}) collective-permute-start(f32[3,10,128]{2,1,0:T(8,128)S(1)} %bitcast.205), channel_id=1, source_target_pairs={{0,8},{4,12},{8,0},{12,4},{1,9},{5,13},{9,1},{13,5},{2,10},{6,14},... | collective-permute-start | bytes 46088 | tf_op jit(solution)/shard_map/ppermute | solution.py:29
  72.4 7.1 %collective-permute-start.19 = (f32[3,10,10,1]{3,2,0,1:T(8,128)S(1)}, f32[3,10,10,1]{3,2,0,1:T(8,128)S(1)}, u32[]{:S(2)}, u32[]{:S(2)}) collective-permute-start(f32[3,10,10,1]{3,2,0,1:T(8,128)S(1)} %get-tuple-element.46), channel_id=1, source_target_pairs={{0,2},{1,3},{4,6},{5,7},{8,10},{9,11},{12,14},{13,15},{16,18},{17,... | collective-permute-start | bytes 3608 | tf_op jit(solution)/shard_map/ppermute | solution.py:18
  73.9 9.8 %collective-permute-start.20 = (f32[3,10,10,1]{3,2,0,1:T(8,128)S(1)}, f32[3,10,10,1]{3,2,0,1:T(8,128)S(1)}, u32[]{:S(2)}, u32[]{:S(2)}) collective-permute-start(f32[3,10,10,1]{3,2,0,1:T(8,128)S(1)} %get-tuple-element.47), channel_id=1, source_target_pairs={{2,0},{3,1},{6,4},{7,5},{10,8},{11,9},{14,12},{15,13},{18,16},{19,... | collective-permute-start | bytes 3608 | tf_op jit(solution)/shard_map/ppermute | solution.py:21
  84.6 1.1 copy-start.1
where the time goes:
time: 376 us
  blocking collectives  271 us (72%)
  waiting for transfers between devices  40.8 us (11%)
  starting transfers between devices  34.5 us (9%)
  other arithmetic  13.4 us (4%)
  between operations  12.3 us (3%)
    psum x8, blocking collectives, local(): lax.psum(jnp.sum(vector * remaining), ('phi', 'gz', 'row'))  241 us
    psum x1, blocking collectives, remainder_energy(): return lax.psum(jnp.sum(remaining * remaining), ('phi', 'gz', 'row'))  30.1 us
    ppermute x9, waiting for transfers between devices, with_halo(): lax.ppermute(lax.slice_in_dim(block, 0, width, axis=dim), axis, backward)  25.2 us
    ppermute x9, starting transfers between devices, with_halo(): lax.ppermute(lax.slice_in_dim(block, 0, width, axis=dim), axis, backward)  17.2 us
    ppermute x9, starting transfers between devices, with_halo(): lax.ppermute(lax.slice_in_dim(block, block.shape[dim] - width, None, axis...  15.4 us
    ppermute x9, waiting for transfers between devices, with_halo(): lax.ppermute(lax.slice_in_dim(block, block.shape[dim] - width, None, axis...  15.1 us
  transfers between devices with their start and end apart: 21, of which 14 were waited for; matrix products, arithmetic and copies ran while one was open for 1% of the time, Pallas kernels for 0%

commit v1 on v0

--- a/solution.py
+++ b/solution.py
@@ -106,8 +106,11 @@
     return jnp.concatenate([inner_layer[:, None], middle, outer_layer[:, None]], axis=1)
 
 
-def remainder_energy(remaining):
-    return lax.psum(jnp.sum(remaining * remaining), ("phi", "gz", "row"))
+def summed_over_part(values):
+    axes = ("phi", "gz", "row")
+    count = lax.axis_size(axes)
+    copies = jnp.broadcast_to(values[None], (count,) + values.shape)
+    return jnp.sum(lax.all_to_all(copies, axes, 0, 0, tiled=True), axis=0)
 
 
 def local(field, velocity, basis, wall_region, wall_conductance):
@@ -145,17 +148,24 @@
         field.size * lax.axis_size("phi") * lax.axis_size("gz") * lax.axis_size("row")
     )
     vectors = basis.shape[0]
-    remaining = advanced
+    everything = jnp.concatenate([basis, advanced[None]], axis=0)
+    flat = everything.reshape(vectors + 1, -1)
+    partial = lax.dot_general(
+        flat, flat, (((1,), (1,)), ((), ())), precision=lax.Precision.HIGHEST
+    )
+    gram = summed_over_part(partial)
     weights = []
-    squares = lax.psum(jnp.sum(basis * basis, axis=(1, 2, 3, 4)), ("phi", "gz", "row"))
+    pending = gram[vectors, :vectors]
     for position in range(vectors):
-        vector = basis[position]
-        weight = lax.psum(jnp.sum(vector * remaining), ("phi", "gz", "row")) / squares[position]
+        weight = pending[position] / gram[position, position]
         weights.append(weight)
-        remaining = remaining - weight * vector
-    energy = remainder_energy(remaining)
+        pending = pending - weight * gram[:vectors, position]
+    factors = jnp.stack(weights)
+    remaining = advanced - jnp.sum(factors[:, None, None, None, None] * basis, axis=0)
+    signed = jnp.concatenate([-factors, jnp.ones((1,), jnp.float32)])
+    energy = jnp.maximum(jnp.sum(signed[:, None] * signed[None, :] * gram), 0.0)
     spread = jnp.sqrt(energy / cell_count + epsilon)
-    return (remaining / spread, jnp.concatenate([jnp.stack(weights), spread[None]]))
+    return (remaining / spread, jnp.concatenate([factors, spread[None]]))
 
 
 def solution(mesh):

time: 376 us -> 124 us (0.33)
  blocking collectives: 271 us -> 11.4 us
  local copies, waits for them, and re-layouts: 3.49 us -> 7.69 us
    psum x9 -> x0, blocking collectives: 271 us -> none  [the longest x8 241 us: local(): lax.psum(jnp.sum(vector * remaining), ('phi', 'gz', 'row'))]
    all_to_all x0 -> x1, blocking collectives: none -> 11.4 us  [summed_over_part(): return jnp.sum(lax.all_to_all(copies, axes, 0, 0, tiled=True), axis=0)]
    reduce_sum x10 -> x3, other arithmetic: 6.97 us -> 0.82 us  [the longest x1 0.67 us: local(): energy = jnp.maximum(jnp.sum(signed[:, None] * signed[None, :] * gram), 0.0)]
    mul x0 -> x7, other arithmetic: none -> 5.34 us  [local(): pending = pending - weight * gram[:vectors, position]]
    slice x1 -> x8, local copies, waits for them, and re-layouts: 0.66 us -> 5.23 us  [local(): weight = pending[position] / gram[position, position]]
  transfers between devices with their start and end apart: 21 -> 21, of which waited for: 14 -> 14; matrix products, arithmetic and copies ran while one was open for 1% -> 2% of each run, Pallas kernels for 0% -> 0%
where the time goes in v1:
time: 124 us
  waiting for transfers between devices  41.5 us (33%)
  starting transfers between devices  34.5 us (28%)
  other arithmetic  13.6 us (11%)
  between operations  12.7 us (10%)
  blocking collectives  11.4 us (9%)
  local copies, waits for them, and re-layouts  7.69 us (6%)
  matrix products  2.23 us (2%)
    ppermute x9, waiting for transfers between devices, with_halo(): lax.ppermute(lax.slice_in_dim(block, 0, width, axis=dim), axis, backward)  25.2 us
    ppermute x9, starting transfers between devices, with_halo(): lax.ppermute(lax.slice_in_dim(block, 0, width, axis=dim), axis, backward)  17.2 us
    ppermute x9, waiting for transfers between devices, with_halo(): lax.ppermute(lax.slice_in_dim(block, block.shape[dim] - width, None, axis...  15.7 us
    ppermute x9, starting transfers between devices, with_halo(): lax.ppermute(lax.slice_in_dim(block, block.shape[dim] - width, None, axis...  15.4 us
    all_to_all x1, blocking collectives, summed_over_part(): return jnp.sum(lax.all_to_all(copies, axes, 0, 0, tiled=True), axis=0)  11.4 us
    mul x7, other arithmetic, local(): pending = pending - weight * gram[:vectors, position]  5.34 us
    slice x8, local copies, waits for them, and re-layouts, local(): weight = pending[position] / gram[position, position]  5.23 us
  transfers between devices with their start and end apart: 21, of which 14 were waited for; matrix products, arithmetic and copies ran while one was open for 2% of the time, Pallas kernels for 0%

profile of v1, /device:TPU:0, one launch (start us, length us, event | category | flops | bytes accessed | tf_op | source)
XLA Modules:
  0.0 123.6 jit_solution(5012122268320136660)
XLA Ops:
  0.7 1.0 fusion.110
  1.7 5.1 %collective-permute-start.1 = (f32[6,8,1,128]{3,2,0,1:T(1,128)S(1)}, f32[6,8,1,128]{3,2,0,1:T(1,128)S(1)}, u32[]{:S(2)}, u32[]{:S(2)}) collective-permute-start(f32[6,8,1,128]{3,2,0,1:T(1,128)S(1)} %get-tuple-element.51), channel_id=1, source_target_pairs={{4,0},{8,4},{12,8},{0,12},{5,1},{9,5},{13,9},{1,13},{6,2},{10,6},{... | collective-permute-start | bytes 73736 | tf_op jit(solution)/shard_map/ppermute | solution.py:21
  6.9 0.9 maximum_bitcast_fusion.8
  8.6 3.9 %collective-permute-done = f32[6,8,1,128]{3,2,0,1:T(1,128)S(1)} collective-permute-done((f32[6,8,1,128]{3,2,0,1:T(1,128)S(1)}, f32[6,8,1,128]{3,2,0,1:T(1,128)S(1)}, u32[]{:S(2)}, u32[]{:S(2)}) %collective-permute-start) | collective-permute-done | bytes 24608 | tf_op jit(solution)/shard_map/ppermute | solution.py:18
  12.5 1.3 %collective-permute-start.3 = (f32[6,1,10,128]{3,2,0,1:T(8,128)S(1)}, f32[6,1,10,128]{3,2,0,1:T(8,128)S(1)}, u32[]{:S(2)}, u32[]{:S(2)}) collective-permute-start(f32[6,1,10,128]{3,2,0,1:T(8,128)S(1)} %get-tuple-element.39), channel_id=1, source_target_pairs={{1,0},{3,2},{5,4},{7,6},{9,8},{11,10},{13,12},{15,14},{17,16},{19,... | collective-permute-start | bytes 92168 | tf_op jit(solution)/shard_map/ppermute | solution.py:21
  13.8 3.0 %collective-permute-start.2 = (f32[6,1,10,128]{3,2,0,1:T(8,128)S(1)}, f32[6,1,10,128]{3,2,0,1:T(8,128)S(1)}, u32[]{:S(2)}, u32[]{:S(2)}) collective-permute-start(f32[6,1,10,128]{3,2,0,1:T(8,128)S(1)} %get-tuple-element.38), channel_id=1, source_target_pairs={{0,1},{2,3},{4,5},{6,7},{8,9},{10,11},{12,13},{14,15},{16,17},{18,... | collective-permute-start | bytes 92168 | tf_op jit(solution)/shard_map/ppermute | solution.py:18
  18.0 3.4 %collective-permute-start.4 = (f32[6,10,10,1]{3,2,0,1:T(8,128)S(1)}, f32[6,10,10,1]{3,2,0,1:T(8,128)S(1)}, u32[]{:S(2)}, u32[]{:S(2)}) collective-permute-start(f32[6,10,10,1]{3,2,0,1:T(8,128)S(1)} %get-tuple-element.19), channel_id=1, source_target_pairs={{0,2},{1,3},{4,6},{5,7},{8,10},{9,11},{12,14},{13,15},{16,18},{17,... | collective-permute-start | bytes 7208 | tf_op jit(solution)/shard_map/ppermute | solution.py:18
  21.4 1.3 %collective-permute-start.5 = (f32[6,10,10,1]{3,2,0,1:T(8,128)S(1)}, f32[6,10,10,1]{3,2,0,1:T(8,128)S(1)}, u32[]{:S(2)}, u32[]{:S(2)}) collective-permute-start(f32[6,10,10,1]{3,2,0,1:T(8,128)S(1)} %get-tuple-element.20), channel_id=1, source_target_pairs={{2,0},{3,1},{6,4},{7,5},{10,8},{11,9},{14,12},{15,13},{18,16},{19,... | collective-permute-start | bytes 7208 | tf_op jit(solution)/shard_map/ppermute | solution.py:21
  22.8 13.7 %collective-permute-done.5 = f32[6,10,10,1]{3,2,0,1:T(8,128)S(1)} collective-permute-done((f32[6,10,10,1]{3,2,0,1:T(8,128)S(1)}, f32[6,10,10,1]{3,2,0,1:T(8,128)S(1)}, u32[]{:S(2)}, u32[]{:S(2)}) %collective-permute-start.5) | collective-permute-done | bytes 2432 | tf_op jit(solution)/shard_map/ppermute | solution.py:21
  36.8 0.7 pad_maximum_fusion
  38.9 3.8 %collective-permute-start.8 = (f32[3,8,1,128]{3,2,0,1:T(1,128)S(1)}, f32[3,8,1,128]{3,2,0,1:T(1,128)S(1)}, u32[]{:S(2)}, u32[]{:S(2)}) collective-permute-start(f32[3,8,1,128]{3,2,0,1:T(1,128)S(1)} %get-tuple-element.71), channel_id=1, source_target_pairs={{4,0},{8,4},{12,8},{0,12},{5,1},{9,5},{13,9},{1,13},{6,2},{10,6},{... | collective-permute-start | bytes 36872 | tf_op jit(solution)/shard_map/ppermute | solution.py:21
  42.8 1.7 %collective-permute-done.7 = f32[3,8,1,128]{3,2,0,1:T(1,128)S(1)} collective-permute-done((f32[3,8,1,128]{3,2,0,1:T(1,128)S(1)}, f32[3,8,1,128]{3,2,0,1:T(1,128)S(1)}, u32[]{:S(2)}, u32[]{:S(2)}) %collective-permute-start.7) | collective-permute-done | bytes 12320 | tf_op jit(solution)/shard_map/ppermute | solution.py:18
  44.5 1.3 %collective-permute-start.10 = (f32[3,1,10,128]{3,2,0,1:T(8,128)S(1)}, f32[3,1,10,128]{3,2,0,1:T(8,128)S(1)}, u32[]{:S(2)}, u32[]{:S(2)}) collective-permute-start(f32[3,1,10,128]{3,2,0,1:T(8,128)S(1)} %get-tuple-element.45), channel_id=1, source_target_pairs={{0,1},{2,3},{4,5},{6,7},{8,9},{10,11},{12,13},{14,15},{16,17},{18,... | collective-permute-start | bytes 46088 | tf_op jit(solution)/shard_map/ppermute | solution.py:18
  45.8 1.3 %collective-permute-start.11 = (f32[3,1,10,128]{3,2,0,1:T(8,128)S(1)}, f32[3,1,10,128]{3,2,0,1:T(8,128)S(1)}, u32[]{:S(2)}, u32[]{:S(2)}) collective-permute-start(f32[3,1,10,128]{3,2,0,1:T(8,128)S(1)} %get-tuple-element.46), channel_id=1, source_target_pairs={{1,0},{3,2},{5,4},{7,6},{9,8},{11,10},{13,12},{15,14},{17,16},{19,... | collective-permute-start | bytes 46088 | tf_op jit(solution)/shard_map/ppermute | solution.py:21
  47.1 0.8 collective-permute-start.9
  47.9 1.0 collective-permute-done.11
  49.0 1.5 %collective-permute-start.12 = (f32[3,10,10,1]{3,2,0,1:T(8,128)S(1)}, f32[3,10,10,1]{3,2,0,1:T(8,128)S(1)}, u32[]{:S(2)}, u32[]{:S(2)}) collective-permute-start(f32[3,10,10,1]{3,2,0,1:T(8,128)S(1)} %get-tuple-element.36), channel_id=1, source_target_pairs={{0,2},{1,3},{4,6},{5,7},{8,10},{9,11},{12,14},{13,15},{16,18},{17,... | collective-permute-start | bytes 3608 | tf_op jit(solution)/shard_map/ppermute | solution.py:18
  50.5 1.3 %collective-permute-start.13 = (f32[3,10,10,1]{3,2,0,1:T(8,128)S(1)}, f32[3,10,10,1]{3,2,0,1:T(8,128)S(1)}, u32[]{:S(2)}, u32[]{:S(2)}) collective-permute-start(f32[3,10,10,1]{3,2,0,1:T(8,128)S(1)} %get-tuple-element.37), channel_id=1, source_target_pairs={{2,0},{3,1},{6,4},{7,5},{10,8},{11,9},{14,12},{15,13},{18,16},{19,... | collective-permute-start | bytes 3608 | tf_op jit(solution)/shard_map/ppermute | solution.py:21
  52.1 4.0 %collective-permute-done.12 = f32[3,10,10,1]{3,2,0,1:T(8,128)S(1)} collective-permute-done((f32[3,10,10,1]{3,2,0,1:T(8,128)S(1)}, f32[3,10,10,1]{3,2,0,1:T(8,128)S(1)}, u32[]{:S(2)}, u32[]{:S(2)}) %collective-permute-start.12) | collective-permute-done | bytes 1232 | tf_op jit(solution)/shard_map/ppermute | solution.py:18
  56.1 4.1 %collective-permute-done.13 = f32[3,10,10,1]{3,2,0,1:T(8,128)S(1)} collective-permute-done((f32[3,10,10,1]{3,2,0,1:T(8,128)S(1)}, f32[3,10,10,1]{3,2,0,1:T(8,128)S(1)}, u32[]{:S(2)}, u32[]{:S(2)}) %collective-permute-start.13) | collective-permute-done | bytes 1232 | tf_op jit(solution)/shard_map/ppermute | solution.py:21
  61.3 3.4 %collective-permute-start.14 = (f32[3,8,1,128]{3,2,0,1:T(1,128)S(1)}, f32[3,8,1,128]{3,2,0,1:T(1,128)S(1)}, u32[]{:S(2)}, u32[]{:S(2)}) collective-permute-start(f32[3,8,1,128]{3,2,0,1:T(1,128)S(1)} %get-tuple-element.65), channel_id=1, source_target_pairs={{0,4},{4,8},{8,12},{12,0},{1,5},{5,9},{9,13},{13,1},{2,6},{6,10},{... | collective-permute-start | bytes 36872 | tf_op jit(solution)/shard_map/ppermute | solution.py:18
  65.3 1.7 %collective-permute-done.14 = f32[3,8,1,128]{3,2,0,1:T(1,128)S(1)} collective-permute-done((f32[3,8,1,128]{3,2,0,1:T(1,128)S(1)}, f32[3,8,1,128]{3,2,0,1:T(1,128)S(1)}, u32[]{:S(2)}, u32[]{:S(2)}) %collective-permute-start.14) | collective-permute-done | bytes 12320 | tf_op jit(solution)/shard_map/ppermute | solution.py:18
  66.9 1.5 %collective-permute-done.15 = f32[3,8,1,128]{3,2,0,1:T(1,128)S(1)} collective-permute-done((f32[3,8,1,128]{3,2,0,1:T(1,128)S(1)}, f32[3,8,1,128]{3,2,0,1:T(1,128)S(1)}, u32[]{:S(2)}, u32[]{:S(2)}) %collective-permute-start.15) | collective-permute-done | bytes 12320 | tf_op jit(solution)/shard_map/ppermute | solution.py:21
  68.5 1.3 %collective-permute-start.17 = (f32[3,1,10,128]{3,2,0,1:T(8,128)S(1)}, f32[3,1,10,128]{3,2,0,1:T(8,128)S(1)}, u32[]{:S(2)}, u32[]{:S(2)}) collective-permute-start(f32[3,1,10,128]{3,2,0,1:T(8,128)S(1)} %get-tuple-element.58), channel_id=1, source_target_pairs={{0,1},{2,3},{4,5},{6,7},{8,9},{10,11},{12,13},{14,15},{16,17},{18,... | collective-permute-start | bytes 46088 | tf_op jit(solution)/shard_map/ppermute | solution.py:18
  69.8 1.3 %collective-permute-start.18 = (f32[3,1,10,128]{3,2,0,1:T(8,128)S(1)}, f32[3,1,10,128]{3,2,0,1:T(8,128)S(1)}, u32[]{:S(2)}, u32[]{:S(2)}) collective-permute-start(f32[3,1,10,128]{3,2,0,1:T(8,128)S(1)} %get-tuple-element.59), channel_id=1, source_target_pairs={{1,0},{3,2},{5,4},{7,6},{9,8},{11,10},{13,12},{15,14},{17,16},{19,... | collective-permute-start | bytes 46088 | tf_op jit(solution)/shard_map/ppermute | solution.py:21
  71.1 1.1 collective-permute-start.16
  72.2 0.7 collective-permute-done.18
  73.0 1.5 %collective-permute-start.19 = (f32[3,10,10,1]{3,2,0,1:T(8,128)S(1)}, f32[3,10,10,1]{3,2,0,1:T(8,128)S(1)}, u32[]{:S(2)}, u32[]{:S(2)}) collective-permute-start(f32[3,10,10,1]{3,2,0,1:T(8,128)S(1)} %get-tuple-element.34), channel_id=1, source_target_pairs={{0,2},{1,3},{4,6},{5,7},{8,10},{9,11},{12,14},{13,15},{16,18},{17,... | collective-permute-start | bytes 3608 | tf_op jit(solution)/shard_map/ppermute | solution.py:18
  74.5 1.3 %collective-permute-start.20 = (f32[3,10,10,1]{3,2,0,1:T(8,128)S(1)}, f32[3,10,10,1]{3,2,0,1:T(8,128)S(1)}, u32[]{:S(2)}, u32[]{:S(2)}) collective-permute-start(f32[3,10,10,1]{3,2,0,1:T(8,128)S(1)} %get-tuple-element.35), channel_id=1, source_target_pairs={{2,0},{3,1},{6,4},{7,5},{10,8},{11,9},{14,12},{15,13},{18,16},{19,... | collective-permute-start | bytes 3608 | tf_op jit(solution)/shard_map/ppermute | solution.py:21
  76.2 3.9 %collective-permute-done.19 = f32[3,10,10,1]{3,2,0,1:T(8,128)S(1)} collective-permute-done((f32[3,10,10,1]{3,2,0,1:T(8,128)S(1)}, f32[3,10,10,1]{3,2,0,1:T(8,128)S(1)}, u32[]{:S(2)}, u32[]{:S(2)}) %collective-permute-start.19) | collective-permute-done | bytes 1232 | tf_op jit(solution)/shard_map/ppermute | solution.py:18
  80.1 4.1 %collective-permute-done.20 = f32[3,10,10,1]{3,2,0,1:T(8,128)S(1)} collective-permute-done((f32[3,10,10,1]{3,2,0,1:T(8,128)S(1)}, f32[3,10,10,1]{3,2,0,1:T(8,128)S(1)}, u32[]{:S(2)}, u32[]{:S(2)}) %collective-permute-start.20) | collective-permute-done | bytes 1232 | tf_op jit(solution)/shard_map/ppermute | solution.py:21
  85.6 2.2 %fusion.4 = f32[9,9]{1,0:T(8,128)S(1)} fusion(f32[1,3,8,8,128]{4,0,3,2,1:T(1,128)S(1)} %bitcast.140, f32[8,3,8,8,128]{4,0,3,2,1:T(8,128)S(1)} %copy.232), kind=kOutput, calls=%fused_computation.4 | convolution fusion | flops 24109056 | bytes 885060 | tf_op jit(solution)/shard_map/dot_general | solution.py:153
  87.8 11.4 %all_to_all.5 = f32[16,9,9]{2,1,0:T(8,128)S(1)} all-to-all(f32[16,9,9]{2,1,0:T(8,128)S(1)} %broadcast_in_dim.28), channel_id=1, replica_groups=mesh['groups'=2,'phi'=4,'gz'=2,'row'=2] {'phi','gz','row'}, dimensions={0} | all-to-all | bytes 10368 | tf_op jit(solution)/shard_map/all_to_all | solution.py:113
  99.3 0.7 fusion.113
  101.4 0.7 slice.610
  103.4 0.9 fusion.99
  106.2 0.9 fusion.98
  107.1 0.7 slice.616
  109.2 0.9 fusion.97
  110.0 0.7 slice.619
  112.0 0.9 fusion.96
  112.9 0.7 slice.622
  114.9 0.9 fusion.95
  115.8 0.7 slice.625
  117.8 0.9 fusion.94
  118.7 0.7 slice.628
  121.0 0.7 multiply_reduce_fusion.1
  123.0 0.7 subtract_divide_fusion
  (104 shorter events, 9.4 us)
Async XLA Ops:
  0.6 7.1 %copy-start.8 = (f32[8]{0:T(128)S(1)}, f32[8]{0:T(128)}, u32[]{:S(2)}) copy-start(f32[8]{0:T(128)} %param.10) | copy-start | bytes 100
  0.6 7.1 %copy-start.5 = (s32[8,128]{1,0:T(8,128)S(1)}, s32[8,128]{1,0:T(8,128)}, u32[]{:S(2)}) copy-start(s32[8,128]{1,0:T(8,128)} %param.9) | copy-start | bytes 12292
  0.7 7.5 %copy-start.1 = (f32[8,3,8,8,128]{4,3,2,1,0:T(8,128)S(1)}, f32[8,3,8,8,128]{4,3,2,1,0:T(8,128)}, u32[]{:S(2)}) copy-start(f32[8,3,8,8,128]{4,3,2,1,0:T(8,128)} %param.8) | copy-start | bytes 2359300
  1.7 6.9 %collective-permute-start.1 = (f32[6,8,1,128]{3,2,0,1:T(1,128)S(1)}, f32[6,8,1,128]{3,2,0,1:T(1,128)S(1)}, u32[]{:S(2)}, u32[]{:S(2)}) collective-permute-start(f32[6,8,1,128]{3,2,0,1:T(1,128)S(1)} %get-tuple-element.51), channel_id=1, source_target_pairs={{4,0},{8,4},{12,8},{0,12},{5,1},{9,5},{13,9},{1,13},{6,2},{10,6},{... | collective-permute-start | bytes 73736 | tf_op jit(solution)/shard_map/ppermute | solution.py:21
  6.9 5.6 %collective-permute-start = (f32[6,8,1,128]{3,2,0,1:T(1,128)S(1)}, f32[6,8,1,128]{3,2,0,1:T(1,128)S(1)}, u32[]{:S(2)}, u32[]{:S(2)}) collective-permute-start(f32[6,8,1,128]{3,2,0,1:T(1,128)S(1)} %get-tuple-element.50), channel_id=1, source_target_pairs={{0,4},{4,8},{8,12},{12,0},{1,5},{5,9},{9,13},{13,1},{2,6},{6,10},{... | collective-permute-start | bytes 73736 | tf_op jit(solution)/shard_map/ppermute | solution.py:18
  8.1 8.9 %copy-start = (f32[3,8,8,128]{3,2,1,0:T(8,128)S(1)}, f32[3,8,8,128]{3,2,1,0:T(8,128)}, u32[]{:S(2)}) copy-start(f32[3,8,8,128]{3,2,1,0:T(8,128)} %param.6) | copy-start | bytes 294916
  12.5 4.6 %collective-permute-start.3 = (f32[6,1,10,128]{3,2,0,1:T(8,128)S(1)}, f32[6,1,10,128]{3,2,0,1:T(8,128)S(1)}, u32[]{:S(2)}, u32[]{:S(2)}) collective-permute-start(f32[6,1,10,128]{3,2,0,1:T(8,128)S(1)} %get-tuple-element.39), channel_id=1, source_target_pairs={{1,0},{3,2},{5,4},{7,6},{9,8},{11,10},{13,12},{15,14},{17,16},{19,... | collective-permute-start | bytes 92168 | tf_op jit(solution)/shard_map/ppermute | solution.py:21
  13.8 3.9 %collective-permute-start.2 = (f32[6,1,10,128]{3,2,0,1:T(8,128)S(1)}, f32[6,1,10,128]{3,2,0,1:T(8,128)S(1)}, u32[]{:S(2)}, u32[]{:S(2)}) collective-permute-start(f32[6,1,10,128]{3,2,0,1:T(8,128)S(1)} %get-tuple-element.38), channel_id=1, source_target_pairs={{0,1},{2,3},{4,5},{6,7},{8,9},{10,11},{12,13},{14,15},{16,17},{18,... | collective-permute-start | bytes 92168 | tf_op jit(solution)/shard_map/ppermute | solution.py:18
  16.8 5.9 %collective-permute-start.6 = (f32[6,10,128]{2,1,0:T(8,128)S(1)}, f32[6,10,128]{2,1,0:T(8,128)S(1)}, u32[]{:S(2)}, u32[]{:S(2)}) collective-permute-start(f32[6,10,128]{2,1,0:T(8,128)S(1)} %bitcast.141), channel_id=1, source_target_pairs={{0,8},{4,12},{8,0},{12,4},{1,9},{5,13},{9,1},{13,5},{2,10},{6,14},... | collective-permute-start | bytes 92168 | tf_op jit(solution)/shard_map/ppermute | solution.py:29
  17.8 5.0 %copy-start.7 = (f32[6]{0:T(128)S(1)}, f32[6]{0:T(128)}, u32[]{:S(2)}) copy-start(f32[6]{0:T(128)} %constant.69) | copy-start | bytes 76
  18.0 18.8 %collective-permute-start.4 = (f32[6,10,10,1]{3,2,0,1:T(8,128)S(1)}, f32[6,10,10,1]{3,2,0,1:T(8,128)S(1)}, u32[]{:S(2)}, u32[]{:S(2)}) collective-permute-start(f32[6,10,10,1]{3,2,0,1:T(8,128)S(1)} %get-tuple-element.19), channel_id=1, source_target_pairs={{0,2},{1,3},{4,6},{5,7},{8,10},{9,11},{12,14},{13,15},{16,18},{17,... | collective-permute-start | bytes 7208 | tf_op jit(solution)/shard_map/ppermute | solution.py:18
  21.4 15.1 %collective-permute-start.5 = (f32[6,10,10,1]{3,2,0,1:T(8,128)S(1)}, f32[6,10,10,1]{3,2,0,1:T(8,128)S(1)}, u32[]{:S(2)}, u32[]{:S(2)}) collective-permute-start(f32[6,10,10,1]{3,2,0,1:T(8,128)S(1)} %get-tuple-element.20), channel_id=1, source_target_pairs={{2,0},{3,1},{6,4},{7,5},{10,8},{11,9},{14,12},{15,13},{18,16},{19,... | collective-permute-start | bytes 7208 | tf_op jit(solution)/shard_map/ppermute | solution.py:21
  37.8 0.9 copy-start.2
  38.8 13.2 %copy-start.6 = (f32[3]{0:T(128)S(1)}, f32[3]{0:T(128)}, u32[]{:S(2)}) copy-start(f32[3]{0:T(128)} %constant.54.clone) | copy-start | bytes 40
  38.9 5.5 %collective-permute-start.7 = (f32[3,8,1,128]{3,2,0,1:T(1,128)S(1)}, f32[3,8,1,128]{3,2,0,1:T(1,128)S(1)}, u32[]{:S(2)}, u32[]{:S(2)}) collective-permute-start(f32[3,8,1,128]{3,2,0,1:T(1,128)S(1)} %get-tuple-element.70), channel_id=1, source_target_pairs={{0,4},{4,8},{8,12},{12,0},{1,5},{5,9},{9,13},{13,1},{2,6},{6,10},{... | collective-permute-start | bytes 36872 | tf_op jit(solution)/shard_map/ppermute | solution.py:18
  38.9 5.5 %collective-permute-start.8 = (f32[3,8,1,128]{3,2,0,1:T(1,128)S(1)}, f32[3,8,1,128]{3,2,0,1:T(1,128)S(1)}, u32[]{:S(2)}, u32[]{:S(2)}) collective-permute-start(f32[3,8,1,128]{3,2,0,1:T(1,128)S(1)} %get-tuple-element.71), channel_id=1, source_target_pairs={{4,0},{8,4},{12,8},{0,12},{5,1},{9,5},{13,9},{1,13},{6,2},{10,6},{... | collective-permute-start | bytes 36872 | tf_op jit(solution)/shard_map/ppermute | solution.py:21
  44.5 3.4 %collective-permute-start.10 = (f32[3,1,10,128]{3,2,0,1:T(8,128)S(1)}, f32[3,1,10,128]{3,2,0,1:T(8,128)S(1)}, u32[]{:S(2)}, u32[]{:S(2)}) collective-permute-start(f32[3,1,10,128]{3,2,0,1:T(8,128)S(1)} %get-tuple-element.45), channel_id=1, source_target_pairs={{0,1},{2,3},{4,5},{6,7},{8,9},{10,11},{12,13},{14,15},{16,17},{18,... | collective-permute-start | bytes 46088 | tf_op jit(solution)/shard_map/ppermute | solution.py:18
  45.8 3.1 %collective-permute-start.11 = (f32[3,1,10,128]{3,2,0,1:T(8,128)S(1)}, f32[3,1,10,128]{3,2,0,1:T(8,128)S(1)}, u32[]{:S(2)}, u32[]{:S(2)}) collective-permute-start(f32[3,1,10,128]{3,2,0,1:T(8,128)S(1)} %get-tuple-element.46), channel_id=1, source_target_pairs={{1,0},{3,2},{5,4},{7,6},{9,8},{11,10},{13,12},{15,14},{17,16},{19,... | collective-permute-start | bytes 46088 | tf_op jit(solution)/shard_map/ppermute | solution.py:21
  47.1 4.9 %collective-permute-start.9 = (f32[3,10,128]{2,1,0:T(8,128)S(1)}, f32[3,10,128]{2,1,0:T(8,128)S(1)}, u32[]{:S(2)}, u32[]{:S(2)}) collective-permute-start(f32[3,10,128]{2,1,0:T(8,128)S(1)} %get-tuple-element.44), channel_id=1, source_target_pairs={{0,8},{4,12},{8,0},{12,4},{1,9},{5,13},{9,1},{13,5},{2,10},{6,14},... | collective-permute-start | bytes 46088 | tf_op jit(solution)/shard_map/ppermute | solution.py:29
  49.0 7.1 %collective-permute-start.12 = (f32[3,10,10,1]{3,2,0,1:T(8,128)S(1)}, f32[3,10,10,1]{3,2,0,1:T(8,128)S(1)}, u32[]{:S(2)}, u32[]{:S(2)}) collective-permute-start(f32[3,10,10,1]{3,2,0,1:T(8,128)S(1)} %get-tuple-element.36), channel_id=1, source_target_pairs={{0,2},{1,3},{4,6},{5,7},{8,10},{9,11},{12,14},{13,15},{16,18},{17,... | collective-permute-start | bytes 3608 | tf_op jit(solution)/shard_map/ppermute | solution.py:18
  50.5 9.8 %collective-permute-start.13 = (f32[3,10,10,1]{3,2,0,1:T(8,128)S(1)}, f32[3,10,10,1]{3,2,0,1:T(8,128)S(1)}, u32[]{:S(2)}, u32[]{:S(2)}) collective-permute-start(f32[3,10,10,1]{3,2,0,1:T(8,128)S(1)} %get-tuple-element.37), channel_id=1, source_target_pairs={{2,0},{3,1},{6,4},{7,5},{10,8},{11,9},{14,12},{15,13},{18,16},{19,... | collective-permute-start | bytes 3608 | tf_op jit(solution)/shard_map/ppermute | solution.py:21
  61.3 5.6 %collective-permute-start.14 = (f32[3,8,1,128]{3,2,0,1:T(1,128)S(1)}, f32[3,8,1,128]{3,2,0,1:T(1,128)S(1)}, u32[]{:S(2)}, u32[]{:S(2)}) collective-permute-start(f32[3,8,1,128]{3,2,0,1:T(1,128)S(1)} %get-tuple-element.65), channel_id=1, source_target_pairs={{0,4},{4,8},{8,12},{12,0},{1,5},{5,9},{9,13},{13,1},{2,6},{6,10},{... | collective-permute-start | bytes 36872 | tf_op jit(solution)/shard_map/ppermute | solution.py:18
  64.7 3.7 %collective-permute-start.15 = (f32[3,8,1,128]{3,2,0,1:T(1,128)S(1)}, f32[3,8,1,128]{3,2,0,1:T(1,128)S(1)}, u32[]{:S(2)}, u32[]{:S(2)}) collective-permute-start(f32[3,8,1,128]{3,2,0,1:T(1,128)S(1)} %get-tuple-element.66), channel_id=1, source_target_pairs={{4,0},{8,4},{12,8},{0,12},{5,1},{9,5},{13,9},{1,13},{6,2},{10,6},{... | collective-permute-start | bytes 36872 | tf_op jit(solution)/shard_map/ppermute | solution.py:21
  68.5 3.7 %collective-permute-start.17 = (f32[3,1,10,128]{3,2,0,1:T(8,128)S(1)}, f32[3,1,10,128]{3,2,0,1:T(8,128)S(1)}, u32[]{:S(2)}, u32[]{:S(2)}) collective-permute-start(f32[3,1,10,128]{3,2,0,1:T(8,128)S(1)} %get-tuple-element.58), channel_id=1, source_target_pairs={{0,1},{2,3},{4,5},{6,7},{8,9},{10,11},{12,13},{14,15},{16,17},{18,... | collective-permute-start | bytes 46088 | tf_op jit(solution)/shard_map/ppermute | solution.py:18
  69.8 3.1 %collective-permute-start.18 = (f32[3,1,10,128]{3,2,0,1:T(8,128)S(1)}, f32[3,1,10,128]{3,2,0,1:T(8,128)S(1)}, u32[]{:S(2)}, u32[]{:S(2)}) collective-permute-start(f32[3,1,10,128]{3,2,0,1:T(8,128)S(1)} %get-tuple-element.59), channel_id=1, source_target_pairs={{1,0},{3,2},{5,4},{7,6},{9,8},{11,10},{13,12},{15,14},{17,16},{19,... | collective-permute-start | bytes 46088 | tf_op jit(solution)/shard_map/ppermute | solution.py:21
  71.1 5.1 %collective-permute-start.16 = (f32[3,10,128]{2,1,0:T(8,128)S(1)}, f32[3,10,128]{2,1,0:T(8,128)S(1)}, u32[]{:S(2)}, u32[]{:S(2)}) collective-permute-start(f32[3,10,128]{2,1,0:T(8,128)S(1)} %bitcast.142), channel_id=1, source_target_pairs={{0,8},{4,12},{8,0},{12,4},{1,9},{5,13},{9,1},{13,5},{2,10},{6,14},... | collective-permute-start | bytes 46088 | tf_op jit(solution)/shard_map/ppermute | solution.py:29
  73.0 7.1 %collective-permute-start.19 = (f32[3,10,10,1]{3,2,0,1:T(8,128)S(1)}, f32[3,10,10,1]{3,2,0,1:T(8,128)S(1)}, u32[]{:S(2)}, u32[]{:S(2)}) collective-permute-start(f32[3,10,10,1]{3,2,0,1:T(8,128)S(1)} %get-tuple-element.34), channel_id=1, source_target_pairs={{0,2},{1,3},{4,6},{5,7},{8,10},{9,11},{12,14},{13,15},{16,18},{17,... | collective-permute-start | bytes 3608 | tf_op jit(solution)/shard_map/ppermute | solution.py:18
  74.5 9.8 %collective-permute-start.20 = (f32[3,10,10,1]{3,2,0,1:T(8,128)S(1)}, f32[3,10,10,1]{3,2,0,1:T(8,128)S(1)}, u32[]{:S(2)}, u32[]{:S(2)}) collective-permute-start(f32[3,10,10,1]{3,2,0,1:T(8,128)S(1)} %get-tuple-element.35), channel_id=1, source_target_pairs={{2,0},{3,1},{6,4},{7,5},{10,8},{11,9},{14,12},{15,13},{18,16},{19,... | collective-permute-start | bytes 3608 | tf_op jit(solution)/shard_map/ppermute | solution.py:21
  99.3 4.1 %copy-start.3 = (f32[9,9]{1,0:T(8,128)}, f32[9,9]{1,0:T(8,128)S(1)}, u32[]{:S(2)}) copy-start(f32[9,9]{1,0:T(8,128)S(1)} %reduce_sum.37) | copy-start | bytes 976
  104.2 16.8 %copy-start.4 = (f32[9,9]{1,0:T(8,128)S(1)}, f32[9,9]{1,0:T(8,128)}, u32[]{:S(2)}) copy-start(f32[9,9]{1,0:T(8,128)} %copy-done.3) | copy-start | bytes 976

commit v2 on v0

v2 whole, which is shorter than its diff:
```python
import functools

import jax
import jax.numpy as jnp
import numpy as np
from jax import lax
from jax.experimental import pallas as pl
from jax.experimental.pallas import tpu as pltpu
from jax.sharding import PartitionSpec as P

advect = 0.2
diffuse = 0.1
epsilon = 1e-06
signs = (-1.0, -1.0, 1.0)
wall_signs = (-1.0, 1.0, 1.0)

tiles = 15
wall_row = 8 * tiles
corner_row = wall_row + 8
side_rows = corner_row + 24
low_corner = 8 * tiles
high_corner = low_corner + 24
radial_rows = high_corner + 24
window = 14
sub = 16


def row_of(component, w):
    return (component * window + w) * sub


def vmem(count):
    return [pl.BlockSpec(memory_space=pltpu.VMEM)] * count


def shape(*dims):
    return jax.ShapeDtypeStruct(dims, jnp.float32)


def lanes(rows):
    return lax.broadcasted_iota(jnp.int32, (rows, 128), 1)


def pack_kernel(fold, conductance, region, field, velocity, up, down, inner, outer, reflect, *corners):
    top = lax.axis_index("row").astype(jnp.float32)
    kinds = region[...]
    value = jnp.zeros(kinds.shape, jnp.float32)
    for kind in range(conductance.shape[0]):
        value = jnp.where(kinds == kind, conductance[kind], value)
    reflect[...] = 1.0 - 2.0 * value / (1.0 + value)

    def column(source, c, q):
        return source[pl.ds(c * 64 + q, 8, stride=8), :]

    def layer(source, c, r):
        return source[pl.ds(c * 64 + r * 8, 8), :]

    radius = lax.broadcasted_iota(jnp.int32, (8, 128), 0).astype(jnp.float32) + (top * 8.0 + 0.5)
    turn = diffuse / radius
    for out, (one, two, three), direction in ((up, (7, 6, 5), -1.0), (down, (0, 1, 2), 1.0)):
        for c in range(3):
            out[pl.ds(8 * c, 8), :] = column(field, c, one)
            out[pl.ds(8 * (3 + c), 8), :] = column(velocity, c, one)
            out[pl.ds(8 * (6 + c), 8), :] = column(field, c, two)
            out[pl.ds(8 * (9 + c), 8), :] = column(velocity, c, two)
        speed = column(velocity, 1, two)
        carry = diffuse + advect * jnp.maximum(-direction * speed, 0.0)
        stretch = (0.5 * advect * direction) * column(field, 1, two)
        far = [column(field, c, three) for c in range(3)]
        term = [carry * far[c] + stretch * column(velocity, c, three) for c in range(3)]
        term[0] = term[0] - (direction * turn) * far[1]
        term[1] = term[1] + (direction * turn) * far[0]
        for c in range(3):
            out[pl.ds(8 * (12 + c), 8), :] = term[c]
        out[pl.ds(wall_row, 1), :] = reflect[pl.ds(one, 1), :]
        out[pl.ds(wall_row + 1, 1), :] = reflect[pl.ds(two, 1), :]
    for side, (one, two) in ((0, (7, 6)), (1, (0, 1))):
        if fold:
            out, base = (down, up)[side], corner_row
        else:
            out, base = corners[side], 0
        for place, (r, q) in enumerate(((0, one), (0, two), (1, one))):
            out[pl.ds(base + 8 * place, 3), :] = field[pl.ds(r * 8 + q, 3, stride=64), :]
            out[pl.ds(base + 8 * place + 3, 3), :] = velocity[pl.ds(r * 8 + q, 3, stride=64), :]
    for out, (one, two, three), direction in ((inner, (0, 1, 2), 1.0), (outer, (7, 6, 5), -1.0)):
        middle = top * 8.0 + (two + 0.5)
        pull = diffuse * (middle + 0.5 * direction) / jnp.full((8, 128), middle)
        speed = layer(velocity, 0, two)
        carry = pull + advect * jnp.maximum(-direction * speed, 0.0)
        stretch = (0.5 * advect * direction) * layer(field, 0, two)
        for c in range(3):
            out[pl.ds(8 * c, 8), :] = layer(field, c, one)
            out[pl.ds(8 * (3 + c), 8), :] = layer(velocity, c, one)
            out[pl.ds(8 * (6 + c), 8), :] = layer(field, c, two)
            out[pl.ds(8 * (9 + c), 8), :] = layer(velocity, c, two)
            out[pl.ds(8 * (12 + c), 8), :] = carry * layer(field, c, three) + stretch * layer(
                velocity, c, three
            )


def radial_kernel(below, above, inner, outer, out):
    low_half = lax.axis_index("row") == 0
    for tile in range(tiles):
        rows = pl.ds(8 * tile, 8)
        out[rows, :] = jnp.where(low_half, outer[rows, :], inner[rows, :])
    for source, base in ((below, low_corner), (above, high_corner)):
        for place, (one, two, first) in enumerate(((7, 0, 0), (7, 0, 48), (6, 1, 0))):
            out[pl.ds(base + 8 * place, 6), :] = jnp.where(
                low_half,
                source[pl.ds(first + one, 6, stride=8), :],
                source[pl.ds(first + two, 6, stride=8), :],
            )


def window_kernel(
    fold, field, velocity, below, above, behind, across, reflect, *rest
):
    if fold:
        corner_low, corner_high, corner_base = above, below, corner_row
        walls, strip, cells = rest[0], rest[1], rest[2]
    else:
        corner_low, corner_high, corner_base = rest[0], rest[1], 0
        walls, strip, cells = rest[2], rest[3], rest[4]
    low_half = lax.axis_index("row") == 0
    nothing = jnp.zeros((8, 128), jnp.float32)
    empty = jnp.zeros((sub, 128), jnp.float32)
    for c in range(6):
        source = field if c < 3 else velocity
        sign = signs[c % 3]
        base = 64 * (c % 3)
        cells[pl.ds(row_of(c, 0), sub), :] = empty
        cells[pl.ds(row_of(c, window - 1), sub), :] = empty
        for r in range(8):
            cells[pl.ds(row_of(c, r + 3), 8), :] = source[pl.ds(base + 8 * r, 8), :]
        for w in range(1, window - 1):
            cells[pl.ds(row_of(c, w) + 8, 8), :] = nothing
        for w, first in ((2, 0), (1, 48)):
            place = pl.ds(first + 8 * c, 8)
            cells[pl.ds(row_of(c, w), 8), :] = jnp.where(
                low_half, sign * behind[place, :], across[place, :]
            )
            cells[pl.ds(row_of(c, 13 - w), 8), :] = jnp.where(low_half, across[place, :], 0.0)
        for depth in range(2):
            place = pl.ds(48 * depth + 8 * c, 8)
            cells[pl.ds(row_of(c, 3) + 15 - depth, 8, stride=sub), :] = below[place, :]
            cells[pl.ds(row_of(c, 3) + 8 + depth, 8, stride=sub), :] = above[place, :]
    flip = lax.broadcasted_iota(jnp.int32, (6, 128), 0)
    flip = jnp.where((flip == 2) | (flip == 5), 1.0, -1.0)
    for place, (w, step) in enumerate(((2, 0), (2, 1), (1, 0))):
        for axis_source, base, q in (
            (corner_low, low_corner, 15 - step),
            (corner_high, high_corner, 8 + step),
        ):
            ghost = flip * axis_source[pl.ds(corner_base + 8 * place, 6), :]
            other = across[pl.ds(base + 8 * place, 6), :]
            low = jnp.where(low_half, ghost, other)
            high = jnp.where(low_half, other, 0.0)
            for c in range(6):
                cells[pl.ds(row_of(c, w) + q, 1), :] = low[c : c + 1]
                cells[pl.ds(row_of(c, 13 - w) + q, 1), :] = high[c : c + 1]
    walls[pl.ds(0, 8), :] = reflect[...]
    walls[pl.ds(8, 8), :] = nothing
    walls[pl.ds(8, 2), :] = above[pl.ds(wall_row, 2), :]
    walls[pl.ds(15, 1), :] = below[pl.ds(wall_row, 1), :]
    walls[pl.ds(14, 1), :] = below[pl.ds(wall_row + 1, 1), :]
    slot = lanes(sub) // 8
    for c in range(6):
        packed = jnp.where(slot == 12, pltpu.roll(walls[...], 100, 1), 0.0)
        for w in range(1, window - 1):
            row = cells[pl.ds(row_of(c, w), sub), :]
            packed = jnp.where(slot == w - 1, pltpu.roll(row, (8 * (w - 1) + 4) % 128, 1), packed)
        strip[pl.ds(sub * c, sub), :] = packed


def back(value, axis, step=1):
    return pltpu.roll(value, step, axis)


def ahead(value, axis, step=1):
    return pltpu.roll(value, value.shape[axis] - step, axis)


def rate(center, sides, coefficients):
    inward, outward, before, after, under, over = sides
    pull_in, pull_out, pull_before, pull_after, pull_under, pull_over, keep, mix, turn = coefficients
    result = []
    for c in range(3):
        value = (
            (pull_in * inward[c] + pull_out * outward[c])
            + (pull_before * before[c] + pull_after * after[c])
            + (pull_under * under[c] + pull_over * over[c])
            + keep * center[c]
        )
        for d in range(3):
            value = value + mix[c][d] * center[d]
        result.append(value)
    result[0] = result[0] - turn * (after[1] - before[1])
    result[1] = result[1] + turn * (after[0] - before[0])
    return result


def coefficients_of(speed, sides, sense, inner_pull, outer_pull, bend, inverse_square, turn):
    inward, outward, before, after, under, over = sides
    radial, around, axial = speed
    around_here = sense * around
    pulls = (
        inner_pull + advect * jnp.maximum(radial, 0.0),
        outer_pull - advect * jnp.minimum(radial, 0.0),
        diffuse + advect * jnp.maximum(around_here, 0.0),
        diffuse - advect * jnp.minimum(around_here, 0.0),
        diffuse + advect * jnp.maximum(axial, 0.0),
        diffuse - advect * jnp.minimum(axial, 0.0),
    )
    keep = -6.0 * diffuse - advect * (jnp.abs(radial) + jnp.abs(around) + jnp.abs(axial))
    half = 0.5 * advect
    mix = []
    for c in range(3):
        mix.append(
            [
                half * (outward[c] - inward[c]),
                (half * sense) * (after[c] - before[c]),
                half * (over[c] - under[c]),
            ]
        )
    mix[0][0] = mix[0][0] - diffuse * inverse_square
    mix[1][1] = mix[1][1] - diffuse * inverse_square + bend * radial
    mix[1][0] = mix[1][0] - bend * around
    return pulls + (keep, mix, turn)


def stage_kernel(
    many, below, above, behind, across, walls, strip, *rest
):
    others = rest[: 2 if many else 1]
    (cells, basis, gram, message, advanced, first, second, edge_low, edge_high) = rest[len(others) :]
    top = lax.axis_index("row")
    low_half = top == 0
    place = lax.axis_index("gz")
    has_low = place > 0
    has_high = place < lax.axis_size("gz") - 1
    lane = lanes(sub)
    slot, inside = lane // 8, lane % 8
    mine = [strip[pl.ds(sub * c, sub), :] for c in range(6)]
    if many:
        from_low = [others[0][pl.ds(sub * c, sub), :] for c in range(6)]
        from_high = [others[1][pl.ds(sub * c, sub), :] for c in range(6)]
        strips = [
            [jnp.where(inside < 4, b, a) for a, b in zip(mine, from_low)],
            [jnp.where(inside < 4, a, b) for a, b in zip(mine, from_high)],
        ]
    else:
        other = [others[0][pl.ds(sub * c, sub), :] for c in range(6)]
        strips = [[jnp.where((inside < 4) == has_high, a, b) for a, b in zip(mine, other)]]

    number = (slot - 2).astype(jnp.float32) + top.astype(jnp.float32) * 8.0 + 0.5
    inverse = 1.0 / number
    strip_scalars = (
        jnp.where(number < 0.0, -1.0, 1.0),
        diffuse * (number - 0.5) * inverse,
        diffuse * (number + 0.5) * inverse,
        advect * inverse,
        inverse * inverse,
        diffuse * jnp.abs(inverse),
    )
    strip_wall = jnp.logical_and(slot == 10, top == 1)

    def strip_sides(values):
        return (
            [back(v, 1, 8) for v in values],
            [ahead(v, 1, 8) for v in values],
            [back(v, 0) for v in values],
            [ahead(v, 0) for v in values],
            [back(v, 1) for v in values],
            [ahead(v, 1) for v in values],
        )

    def walled(values, factors):
        return [jnp.where(strip_wall, f * back(v, 1, 8), v) for v, f in zip(values, factors)]

    levels = []
    flows = []
    for line in strips:
        factor = ahead(line[0], 1, 16)
        flow = walled(line[3:], wall_signs)
        flows.append(flow)
        table = coefficients_of(flow, strip_sides(flow), *strip_scalars)
        start = walled(line[:3], [factor] * 3)
        one = rate(start, strip_sides(start), table)
        one = walled([a + b for a, b in zip(start, one)], [factor] * 3)
        two = rate(one, strip_sides(one), table)
        two = [0.75 * s + 0.25 * (a + b) for s, a, b in zip(start, one, two)]
        levels.append((start, one, two))

    def store_edges(low_values, high_values):
        for c in range(3):
            edge_low[pl.ds(sub * c, sub), :] = jnp.where(has_low, low_values[c], 0.0)
            edge_high[pl.ds(sub * c, sub), :] = jnp.where(has_high, high_values[c], 0.0)

    def axial(value, c, w, size):
        low = pltpu.roll(edge_low[pl.ds(sub * c, size), :], (128 - (8 * (w - 1) + 3)) % 128, 1)
        high = pltpu.roll(edge_high[pl.ds(sub * c, size), :], (127 - (8 * (w - 1) + 4)) % 128, 1)
        at = lane[:size]
        return jnp.where(at == 0, low, back(value, 1)), jnp.where(at == 127, high, ahead(value, 1))

    def pick(low, high):
        return jnp.where(low_half, np.float32(low), np.float32(high))

    def scalars(w):
        options = []
        for half in range(2):
            r = half * 8 + (w - 3) + 0.5
            options.append(
                (
                    -1.0 if r < 0 else 1.0,
                    diffuse * (r - 0.5) / r,
                    diffuse * (r + 0.5) / r,
                    advect / r,
                    1.0 / (r * r),
                    diffuse / abs(r),
                )
            )
        return [pick(a, b) for a, b in zip(*options)]

    def read(source, c, w, size=sub):
        return source[pl.ds(row_of(c, w), size), :]

    for c in range(6):
        last = read(cells, c, 10)
        factor = walls[...] if c < 3 else wall_signs[c - 3]
        cells[pl.ds(row_of(c, 11), sub), :] = jnp.where(low_half, read(cells, c, 11), factor * last)

    flow_low, flow_high = flows[0], flows[-1]

    def flow_table(w, size):
        speed, sides = [], [[], [], [], [], [], []]
        for c in range(3):
            value = read(cells, 3 + c, w)
            low = pltpu.roll(jnp.where(has_low, flow_low[c], 0.0), (128 - (8 * (w - 1) + 3)) % 128, 1)
            high = pltpu.roll(jnp.where(has_high, flow_high[c], 0.0), (127 - (8 * (w - 1) + 4)) % 128, 1)
            under = jnp.where(lane == 0, low, back(value, 1))
            over = jnp.where(lane == 127, high, ahead(value, 1))
            for side, part in zip(
                sides,
                (
                    read(cells, 3 + c, w - 1),
                    read(cells, 3 + c, w + 1),
                    back(value, 0),
                    ahead(value, 0),
                    under,
                    over,
                ),
            ):
                side.append(part[:size])
            speed.append(value[:size])
        return coefficients_of(speed, sides, *scalars(w))

    def field_rate(source, w, size):
        center, sides = [], [[], [], [], [], [], []]
        for c in range(3):
            value = read(source, c, w)
            under, over = axial(value[:size], c, w, size)
            for side, part in zip(
                sides,
                (
                    read(source, c, w - 1, size),
                    read(source, c, w + 1, size),
                    back(value, 0)[:size],
                    ahead(value, 0)[:size],
                    under,
                    over,
                ),
            ):
                side.append(part)
            center.append(value[:size])
        return center, rate(center, sides, flow_table(w, size))

    store_edges(levels[0][0], levels[-1][0])
    for w in range(1, 13):
        center, change = field_rate(cells, w, sub)
        for c in range(3):
            first[pl.ds(row_of(c, w), sub), :] = center[c] + change[c]
    for c in range(3):
        rows = pl.ds(8 * (12 + c), 8)
        low, high = pl.ds(row_of(c, 1), 8), pl.ds(row_of(c, 12), 8)
        first[low, :] += jnp.where(low_half, signs[c] * behind[rows, :], across[rows, :])
        first[high, :] += jnp.where(low_half, across[rows, :], 0.0)
        before = pl.ds(row_of(c, 3) + 14, 8, stride=sub)
        after = pl.ds(row_of(c, 3) + 9, 8, stride=sub)
        first[before, :] = first[before, :] + below[rows, :]
        first[after, :] = first[after, :] + above[rows, :]

    def close_wall(source):
        for c in range(3):
            source[pl.ds(row_of(c, 11), sub), :] = jnp.where(
                low_half, read(source, c, 11), walls[...] * read(source, c, 10)
            )

    close_wall(first)
    store_edges(levels[0][1], levels[-1][1])
    for w in range(2, 12):
        center, change = field_rate(first, w, sub)
        for c in range(3):
            second[pl.ds(row_of(c, w), sub), :] = 0.75 * read(cells, c, w) + 0.25 * (
                center[c] + change[c]
            )
    close_wall(second)
    store_edges(levels[0][2], levels[-1][2])
    count = basis.shape[0] // 192
    sums = [jnp.zeros((8, 128), jnp.float32) for _ in range(count + 1)]
    for w in range(3, 11):
        center, change = field_rate(second, w, 8)
        for c in range(3):
            rows = pl.ds(64 * c + 8 * (w - 3), 8)
            value = read(cells, c, w, 8) / 3.0 + (2.0 / 3.0) * (center[c] + change[c])
            advanced[rows, :] = value
            for m in range(count):
                sums[m] += basis[pl.ds(192 * m + 64 * c + 8 * (w - 3), 8), :] * value
            sums[count] += value * value
    spot = lanes(1)
    line = gram[...]
    for m in range(count + 1):
        total = jnp.sum(jnp.sum(sums[m], axis=0, keepdims=True), axis=1, keepdims=True)
        line = jnp.where(spot == m, total, line)
    for device in range(message.shape[0]):
        message[device] = line


def gram_place(m, n):
    return 16 + m * (m + 1) // 2 + n


def gram_kernel(basis, out):
    count = basis.shape[0] // 192
    spot = lanes(1)
    line = jnp.zeros((1, 128), jnp.float32)
    for m in range(count):
        sums = [jnp.zeros((8, 128), jnp.float32) for _ in range(m + 1)]
        for tile in range(24):
            value = basis[pl.ds(192 * m + 8 * tile, 8), :]
            for n in range(m + 1):
                sums[n] += value * basis[pl.ds(192 * n + 8 * tile, 8), :]
        for n in range(m + 1):
            total = jnp.sum(jnp.sum(sums[n], axis=0, keepdims=True), axis=1, keepdims=True)
            line = jnp.where(spot == gram_place(m, n), total, line)
    out[...] = line


def finish_kernel(cell_count, messages, advanced, basis, out, hessenberg):
    count = basis.shape[0] // 192
    total = messages[0]
    for device in range(1, messages.shape[0]):
        total = total + messages[device]

    def entry(index):
        return jnp.broadcast_to(total[:, index : index + 1], (8, 128))

    pending = [entry(m) for m in range(count)]
    energy = entry(count)
    weights = []
    for m in range(count):
        diagonal = entry(gram_place(m, m))
        weight = pending[m] / diagonal
        weights.append(weight)
        energy = energy - weight * (2.0 * pending[m] - weight * diagonal)
        for n in range(m + 1, count):
            pending[n] = pending[n] - weight * entry(gram_place(n, m))
    spread = jnp.sqrt(jnp.maximum(energy, 0.0) / cell_count + epsilon)
    scale = 1.0 / spread
    for tile in range(24):
        rows = pl.ds(8 * tile, 8)
        value = advanced[rows, :]
        for m in range(count):
            value = value - weights[m] * basis[pl.ds(192 * m + 8 * tile, 8), :]
        out[rows, :] = value * scale
    for m in range(count):
        hessenberg[m] = weights[m][0, 0]
    hessenberg[count] = spread[0, 0]


def shift(value, axis, step):
    count = lax.axis_size(axis)
    return lax.ppermute(value, axis, [(i, (i + step) % count) for i in range(count)])


def local(field, velocity, basis, wall_region, wall_conductance):
    loop = lax.axis_size("phi")
    ends = lax.axis_size("gz")
    halves = lax.axis_size("row")
    fold = loop == 4
    many = ends > 2
    vectors = basis.shape[0]
    field_rows = field.reshape(192, 128)
    flow_rows = velocity.reshape(192, 128)
    basis_rows = basis.reshape(vectors * 192, 128)
    side = corner_row if not fold else side_rows
    packed = pl.pallas_call(
        functools.partial(pack_kernel, fold),
        in_specs=[pl.BlockSpec(memory_space=pltpu.SMEM)] + vmem(3),
        out_specs=vmem(5 if fold else 7),
        out_shape=[
            shape(side, 128),
            shape(side, 128),
            shape(8 * tiles, 128),
            shape(8 * tiles, 128),
            shape(8, 128),
        ]
        + ([] if fold else [shape(24, 128)] * 2),
    )(wall_conductance, wall_region, field_rows, flow_rows)
    up, down, inner, outer, reflect = packed[:5]
    below = shift(up, "phi", 1)
    above = shift(down, "phi", -1)
    half = loop // 2
    turned = []
    for p in range(loop):
        for r in range(halves):
            turned.append((p * halves + r, ((p + half) % loop if r == 0 else p) * halves + r))
    behind = lax.ppermute(inner, ("phi", "row"), turned)
    corners = []
    if not fold:
        corners = [shift(packed[5], "phi", half + 1), shift(packed[6], "phi", half - 1)]
    gram = pl.pallas_call(
        gram_kernel, in_specs=vmem(1), out_specs=vmem(1)[0], out_shape=shape(1, 128)
    )(basis_rows)
    radial = pl.pallas_call(
        radial_kernel, in_specs=vmem(4), out_specs=vmem(1)[0], out_shape=shape(radial_rows, 128)
    )(below, above, inner, outer)
    across = lax.ppermute(radial, "row", [(0, 1), (1, 0)])
    walls, strip, cells = pl.pallas_call(
        functools.partial(window_kernel, fold),
        in_specs=vmem(7 + len(corners)),
        out_specs=vmem(3),
        out_shape=[shape(sub, 128), shape(6 * sub, 128), shape(6 * window * sub, 128)],
    )(field_rows, flow_rows, below, above, behind, across, reflect, *corners)
    if many:
        up_pairs = [(i, i + 1) for i in range(ends - 1)]
        others = [
            lax.ppermute(strip, "gz", up_pairs),
            lax.ppermute(strip, "gz", [(b, a) for a, b in up_pairs]),
        ]
    else:
        others = [lax.ppermute(strip, "gz", [(0, 1), (1, 0)])]
    axes = ("phi", "gz", "row")
    devices = lax.axis_size(axes)
    message, advanced = pl.pallas_call(
        functools.partial(stage_kernel, many),
        in_specs=vmem(9 + len(others)),
        out_specs=vmem(2),
        out_shape=[shape(devices, 1, 128), shape(192, 128)],
        scratch_shapes=[
            pltpu.VMEM((3 * window * sub, 128), jnp.float32),
            pltpu.VMEM((3 * window * sub, 128), jnp.float32),
            pltpu.VMEM((3 * sub, 128), jnp.float32),
            pltpu.VMEM((3 * sub, 128), jnp.float32),
        ],
    )(below, above, behind, across, walls, strip, *others, cells, basis_rows, gram)
    messages = lax.all_to_all(message, axes, 0, 0, tiled=True)
    out, hessenberg = pl.pallas_call(
        functools.partial(finish_kernel, float(field.size * devices)),
        in_specs=vmem(3),
        out_specs=vmem(1) + [pl.BlockSpec(memory_space=pltpu.SMEM)],
        out_shape=[shape(192, 128), shape(vectors + 1)],
    )(messages, advanced, basis_rows)
    return out.reshape(field.shape), hessenberg


def solution(mesh):
    return jax.shard_map(
        local,
        mesh=mesh,
        in_specs=(
            P("groups", "row", "phi", "gz"),
            P("groups", "row", "phi", "gz"),
            P("groups", None, "row", "phi", "gz"),
            P(("groups", "phi"), "gz"),
            P("groups"),
        ),
        out_specs=(P("groups", "row", "phi", "gz"), P("groups")),
        check_vma=False,
    )
```

time: 376 us -> 45.9 us (0.12)
  blocking collectives: 271 us -> 11.7 us
  waiting for transfers between devices: 40.8 us -> 8.05 us
  starting transfers between devices: 34.5 us -> 9.98 us
  other arithmetic: 13.4 us -> 0 us
  Pallas kernels: 0 us -> 13.3 us
  between operations: 12.3 us -> 0.65 us
    psum x9 -> x0, blocking collectives: 271 us -> none  [the longest x8 241 us: local(): lax.psum(jnp.sum(vector * remaining), ('phi', 'gz', 'row'))]
    ppermute x21 -> x5, waiting for transfers between devices: 40.8 us -> 8.05 us  [the longest x2 3.63 us: shift(): lax.ppermute(value, axis, [(i, (i + step) % count) for i in range(count)])]
    ppermute x21 -> x5, starting transfers between devices: 34.5 us -> 9.98 us  [the longest x2 5.09 us: shift(): lax.ppermute(value, axis, [(i, (i + step) % count) for i in range(count)])]
    pallas_call x0 -> x6, Pallas kernels: none -> 13.3 us  [the longest x1 3.69 us: local(): pl.pallas_call(functools.partial(stage_kernel, many), in_specs=vmem(9 + l...]
    all_to_all x0 -> x1, blocking collectives: none -> 11.7 us  [local(): messages = lax.all_to_all(message, axes, 0, 0, tiled=True)]
    reduce_sum x11 -> x0, other arithmetic: 7.05 us -> none  [the longest x8 5.04 us: local(): jnp.sum(vector * remaining)]
  transfers between devices with their start and end apart: 21 -> 5, of which waited for: 14 -> 4; matrix products, arithmetic and copies ran while one was open for 1% -> 0% of each run, Pallas kernels for 0% -> 4%
where the time goes in v2:
time: 45.9 us; the launch traced here: 45.5 us
  Pallas kernels  13.3 us (29%)
  blocking collectives  11.7 us (25%)
  starting transfers between devices  9.98 us (22%)
  waiting for transfers between devices  8.05 us (18%)
  local copies, waits for them, and re-layouts  1.89 us (4%)
  between operations  0.65 us (1%)
    all_to_all x1, blocking collectives, local(): messages = lax.all_to_all(message, axes, 0, 0, tiled=True)  11.7 us
    ppermute x2, starting transfers between devices, shift(): lax.ppermute(value, axis, [(i, (i + step) % count) for i in range(count)])  5.09 us
    pallas_call x1, Pallas kernels, local(): pl.pallas_call(functools.partial(stage_kernel, many), in_specs=vmem(9 + l...  3.69 us
    ppermute x2, waiting for transfers between devices, shift(): lax.ppermute(value, axis, [(i, (i + step) % count) for i in range(count)])  3.63 us
    ppermute x1, waiting for transfers between devices, local(): behind = lax.ppermute(inner, ('phi', 'row'), turned)  3.61 us
    ppermute x1, starting transfers between devices, local(): behind = lax.ppermute(inner, ('phi', 'row'), turned)  3.4 us
    pallas_call x1, Pallas kernels, local(): pl.pallas_call(functools.partial(window_kernel, fold), in_specs=vmem(7 +...  2.21 us
    pallas_call x1, Pallas kernels, local(): pl.pallas_call(functools.partial(finish_kernel, float(field.size * device...  2.07 us
  transfers between devices with their start and end apart: 5, of which 4 were waited for; matrix products, arithmetic and copies ran while one was open for 0% of the time, Pallas kernels for 4%

profile of v2, /device:TPU:0, one launch (start us, length us, event | category | flops | bytes accessed | tf_op | source)
XLA Modules:
  0.0 45.5 jit_solution(16767654302481553997)
XLA Ops:
  0.6 1.7 %shard_map.68 = (f32[152,128]{1,0:T(8,128)}, f32[152,128]{1,0:T(8,128)}, f32[120,128]{1,0:T(8,128)}, f32[120,128]{1,0:T(8,128)}, f32[8,128]{1,0:T(8,128)}) custom-call(f32[8]{0:T(128)} %conductance.1, s32[8,128]{1,0:T(8,128)} %region.1, f32[192,128]{1,0:T(8,128)} %bitcast.7, f32[192,128]{1,0:T(8,128)} %bitcast.9), custom_call_target="tpu_custom_call" | custom-call | tf_op jit(solution)/shard_map/pallas_call | solution.py:496
  2.3 3.0 %collective-permute-start = (f32[152,128]{1,0:T(8,128)}, f32[152,128]{1,0:T(8,128)S(1)}, u32[]{:S(2)}, u32[]{:S(2)}) collective-permute-start(f32[152,128]{1,0:T(8,128)} %get-tuple-element.14), channel_id=1, source_target_pairs={{0,4},{4,8},{8,12},{12,0},{1,5},{5,9},{9,13},{13,1},{2,6},{6,10},{... | collective-permute-start | bytes 233480 | tf_op jit(solution)/shard_map/ppermute | solution.py:482
  5.4 2.1 %collective-permute-start.1 = (f32[152,128]{1,0:T(8,128)}, f32[152,128]{1,0:T(8,128)S(1)}, u32[]{:S(2)}, u32[]{:S(2)}) collective-permute-start(f32[152,128]{1,0:T(8,128)} %get-tuple-element.15), channel_id=1, source_target_pairs={{0,12},{4,0},{8,4},{12,8},{1,13},{5,1},{9,5},{13,9},{2,14},{6,2},{... | collective-permute-start | bytes 233480 | tf_op jit(solution)/shard_map/ppermute | solution.py:482
  7.4 2.8 %collective-permute-done.below = f32[152,128]{1,0:T(8,128)S(1)} collective-permute-done((f32[152,128]{1,0:T(8,128)}, f32[152,128]{1,0:T(8,128)S(1)}, u32[]{:S(2)}, u32[]{:S(2)}) %collective-permute-start) | collective-permute-done | bytes 77856 | tf_op jit(solution)/shard_map/ppermute | solution.py:482
  10.2 0.0 copy-start
  10.2 0.8 %collective-permute-done.1.above = f32[152,128]{1,0:T(8,128)S(1)} collective-permute-done((f32[152,128]{1,0:T(8,128)}, f32[152,128]{1,0:T(8,128)S(1)}, u32[]{:S(2)}, u32[]{:S(2)}) %collective-permute-start.1) | collective-permute-done | bytes 77856 | tf_op jit(solution)/shard_map/ppermute | solution.py:482
  11.0 0.0 copy-start.1
  11.1 0.0 copy-done
  11.1 0.6 %copy-done.1 = f32[152,128]{1,0:T(8,128)} copy-done((f32[152,128]{1,0:T(8,128)}, f32[152,128]{1,0:T(8,128)S(1)}, u32[]{:S(2)}) %copy-start.1) | copy-done | bytes 77848
  11.7 0.0 copy-start.4
  11.7 1.6 %shard_map.69 = f32[168,128]{1,0:T(8,128)} custom-call(f32[152,128]{1,0:T(8,128)} %copy-done, f32[152,128]{1,0:T(8,128)} %copy-done.1, f32[120,128]{1,0:T(8,128)} %get-tuple-element.16.inner, f32[120,128]{1,0:T(8,128)} %get-tuple-element.17.outer), custom_call_target="tpu_custom_call" | custom-call | tf_op jit(solution)/shard_map/pallas_call | solution.py:524
  13.3 0.0 collective-permute-start.3
  13.3 0.0 copy-done.4
  13.3 3.4 %collective-permute-start.2 = (f32[120,128]{1,0:T(8,128)S(1)}, f32[120,128]{1,0:T(8,128)S(1)}, u32[]{:S(2)}, u32[]{:S(2)}) collective-permute-start(f32[120,128]{1,0:T(8,128)S(1)} %copy-done.4), channel_id=1, source_target_pairs={{0,8},{1,1},{4,12},{5,5},{8,0},{9,9},{12,4},{13,13},{2,10},{3,3},{... | collective-permute-start | bytes 184328 | tf_op jit(solution)/shard_map/ppermute | solution.py:517
  16.7 3.6 %collective-permute-done.2.behind = f32[120,128]{1,0:T(8,128)S(1)} collective-permute-done((f32[120,128]{1,0:T(8,128)S(1)}, f32[120,128]{1,0:T(8,128)S(1)}, u32[]{:S(2)}, u32[]{:S(2)}) %collective-permute-start.2) | collective-permute-done | bytes 61472 | tf_op jit(solution)/shard_map/ppermute | solution.py:517
  20.3 0.0 copy-start.3
  20.3 0.0 collective-permute-done.3.across
  20.3 0.0 copy-start.2
  20.3 0.6 %copy-done.3 = f32[120,128]{1,0:T(8,128)} copy-done((f32[120,128]{1,0:T(8,128)}, f32[120,128]{1,0:T(8,128)S(1)}, u32[]{:S(2)}) %copy-start.3) | copy-done | bytes 61464
  20.9 0.0 copy-done.2
  20.9 2.2 %shard_map.70 = (f32[16,128]{1,0:T(8,128)}, f32[96,128]{1,0:T(8,128)}, f32[1344,128]{1,0:T(8,128)}) custom-call(f32[192,128]{1,0:T(8,128)} %bitcast.8, f32[192,128]{1,0:T(8,128)} %bitcast.10, f32[152,128]{1,0:T(8,128)} %copy-done, f32[152,128]{1,0:T(8,128)} %copy-done.1, f32[120,128]{1,0:T(8,128)} %copy-done.3, f32[168,128]{1,0:T(8,128)} %copy-done.2, ...), custom_call_target="tpu_custom_call" | custom-call | tf_op jit(solution)/shard_map/pallas_call | solution.py:528
  23.2 1.5 %collective-permute-start.4 = (f32[96,128]{1,0:T(8,128)}, f32[96,128]{1,0:T(8,128)S(1)}, u32[]{:S(2)}, u32[]{:S(2)}) collective-permute-start(f32[96,128]{1,0:T(8,128)} %get-tuple-element.20.strip), channel_id=1, source_target_pairs={{0,2},{2,0},{1,3},{3,1},{4,6},{6,4},{5,7},{7,5},{8,10},{10,8},{9,1... | collective-permute-start | bytes 147464 | tf_op jit(solution)/shard_map/ppermute | solution.py:541
  24.7 2.0 %shard_map.71.rest_3_ = f32[1,128]{1,0:T(1,128)} custom-call(f32[1536,128]{1,0:T(8,128)} %bitcast.4), custom_call_target="tpu_custom_call" | custom-call | tf_op jit(solution)/shard_map/pallas_call | solution.py:521
  26.6 0.8 %collective-permute-done.4.rest_0_ = f32[96,128]{1,0:T(8,128)S(1)} collective-permute-done((f32[96,128]{1,0:T(8,128)}, f32[96,128]{1,0:T(8,128)S(1)}, u32[]{:S(2)}, u32[]{:S(2)}) %collective-permute-start.4) | collective-permute-done | bytes 49184 | tf_op jit(solution)/shard_map/ppermute | solution.py:541
  27.5 0.0 copy-start.5
  27.5 0.6 %copy-done.5 = f32[96,128]{1,0:T(8,128)} copy-done((f32[96,128]{1,0:T(8,128)}, f32[96,128]{1,0:T(8,128)S(1)}, u32[]{:S(2)}) %copy-start.5) | copy-done | bytes 49176
  28.1 3.7 %shard_map.72 = (f32[16,1,128]{2,1,0:T(1,128)}, f32[192,128]{1,0:T(8,128)}) custom-call(f32[152,128]{1,0:T(8,128)} %copy-done, f32[152,128]{1,0:T(8,128)} %copy-done.1, f32[120,128]{1,0:T(8,128)} %copy-done.3, f32[168,128]{1,0:T(8,128)} %copy-done.2, f32[16,128]{1,0:T(8,128)} %get-tuple-element.19.walls, f32[96,128]{1,0:T(8,128)} %get-tuple-element.20.strip, ...), custom_call_target="tpu_custom_call" | custom-call | tf_op jit(solution)/shard_map/pallas_call | solution.py:544
  31.8 11.7 %all_to_all.5.messages = f32[16,1,128]{2,1,0:T(1,128)} all-to-all(f32[16,1,128]{2,1,0:T(1,128)} %get-tuple-element.22), channel_id=1, replica_groups=mesh['groups'=2,'phi'=4,'gz'=2,'row'=2] {'phi','gz','row'}, dimensions={0} | all-to-all | bytes 16384 | tf_op jit(solution)/shard_map/all_to_all | solution.py:556
  43.5 2.1 %shard_map.73 = (f32[192,128]{1,0:T(8,128)}, f32[9]{0:T(128)}) custom-call(f32[16,1,128]{2,1,0:T(1,128)} %all_to_all.5.messages, f32[192,128]{1,0:T(8,128)} %get-tuple-element.23.advanced, f32[1536,128]{1,0:T(8,128)} %bitcast.6), custom_call_target="tpu_custom_call" | custom-call | tf_op jit(solution)/shard_map/pallas_call | solution.py:557
Async XLA Ops:
  2.3 7.9 %collective-permute-start = (f32[152,128]{1,0:T(8,128)}, f32[152,128]{1,0:T(8,128)S(1)}, u32[]{:S(2)}, u32[]{:S(2)}) collective-permute-start(f32[152,128]{1,0:T(8,128)} %get-tuple-element.14), channel_id=1, source_target_pairs={{0,4},{4,8},{8,12},{12,0},{1,5},{5,9},{9,13},{13,1},{2,6},{6,10},{... | collective-permute-start | bytes 233480 | tf_op jit(solution)/shard_map/ppermute | solution.py:482
  5.4 5.7 %collective-permute-start.1 = (f32[152,128]{1,0:T(8,128)}, f32[152,128]{1,0:T(8,128)S(1)}, u32[]{:S(2)}, u32[]{:S(2)}) collective-permute-start(f32[152,128]{1,0:T(8,128)} %get-tuple-element.15), channel_id=1, source_target_pairs={{0,12},{4,0},{8,4},{12,8},{1,13},{5,1},{9,5},{13,9},{2,14},{6,2},{... | collective-permute-start | bytes 233480 | tf_op jit(solution)/shard_map/ppermute | solution.py:482
  10.2 0.8 %copy-start = (f32[152,128]{1,0:T(8,128)}, f32[152,128]{1,0:T(8,128)S(1)}, u32[]{:S(2)}) copy-start(f32[152,128]{1,0:T(8,128)S(1)} %collective-permute-done.below) | copy-start | bytes 233476
  11.0 0.6 %copy-start.1 = (f32[152,128]{1,0:T(8,128)}, f32[152,128]{1,0:T(8,128)S(1)}, u32[]{:S(2)}) copy-start(f32[152,128]{1,0:T(8,128)S(1)} %collective-permute-done.1.above) | copy-start | bytes 233476
  11.7 1.6 %copy-start.4 = (f32[120,128]{1,0:T(8,128)S(1)}, f32[120,128]{1,0:T(8,128)}, u32[]{:S(2)}) copy-start(f32[120,128]{1,0:T(8,128)} %get-tuple-element.16.inner) | copy-start | bytes 184324
  13.3 7.0 %collective-permute-start.3 = (f32[168,128]{1,0:T(8,128)}, f32[168,128]{1,0:T(8,128)S(1)}, u32[]{:S(2)}, u32[]{:S(2)}) collective-permute-start(f32[168,128]{1,0:T(8,128)} %shard_map.69), channel_id=1, source_target_pairs={{0,1},{1,0},{2,3},{3,2},{4,5},{5,4},{6,7},{7,6},{8,9},{9,8},{10,11... | collective-permute-start | bytes 258056 | tf_op jit(solution)/shard_map/ppermute | solution.py:527
  13.3 7.0 %collective-permute-start.2 = (f32[120,128]{1,0:T(8,128)S(1)}, f32[120,128]{1,0:T(8,128)S(1)}, u32[]{:S(2)}, u32[]{:S(2)}) collective-permute-start(f32[120,128]{1,0:T(8,128)S(1)} %copy-done.4), channel_id=1, source_target_pairs={{0,8},{1,1},{4,12},{5,5},{8,0},{9,9},{12,4},{13,13},{2,10},{3,3},{... | collective-permute-start | bytes 184328 | tf_op jit(solution)/shard_map/ppermute | solution.py:517
  20.3 0.6 %copy-start.3 = (f32[120,128]{1,0:T(8,128)}, f32[120,128]{1,0:T(8,128)S(1)}, u32[]{:S(2)}) copy-start(f32[120,128]{1,0:T(8,128)S(1)} %collective-permute-done.2.behind) | copy-start | bytes 184324
  20.3 0.7 %copy-start.2 = (f32[168,128]{1,0:T(8,128)}, f32[168,128]{1,0:T(8,128)S(1)}, u32[]{:S(2)}) copy-start(f32[168,128]{1,0:T(8,128)S(1)} %collective-permute-done.3.across) | copy-start | bytes 258052
  23.2 4.3 %collective-permute-start.4 = (f32[96,128]{1,0:T(8,128)}, f32[96,128]{1,0:T(8,128)S(1)}, u32[]{:S(2)}, u32[]{:S(2)}) collective-permute-start(f32[96,128]{1,0:T(8,128)} %get-tuple-element.20.strip), channel_id=1, source_target_pairs={{0,2},{2,0},{1,3},{3,1},{4,6},{6,4},{5,7},{7,5},{8,10},{10,8},{9,1... | collective-permute-start | bytes 147464 | tf_op jit(solution)/shard_map/ppermute | solution.py:541
  27.5 0.6 %copy-start.5 = (f32[96,128]{1,0:T(8,128)}, f32[96,128]{1,0:T(8,128)S(1)}, u32[]{:S(2)}) copy-start(f32[96,128]{1,0:T(8,128)S(1)} %collective-permute-done.4.rest_0_) | copy-start | bytes 147460

commit v3 on v2

--- a/solution.py
+++ b/solution.py
@@ -17,10 +17,8 @@
 tiles = 15
 wall_row = 8 * tiles
 corner_row = wall_row + 8
-side_rows = corner_row + 24
-low_corner = 8 * tiles
-high_corner = low_corner + 24
-radial_rows = high_corner + 24
+axis_row = corner_row + 24
+side_rows = axis_row + 24
 window = 14
 sub = 16
 
@@ -34,15 +32,40 @@
 
 
 def shape(*dims):
-    return jax.ShapeDtypeStruct(dims, jnp.float32)
+    return pltpu.VMEM(dims, jnp.float32)
+
+
+def near(*values):
+    return [pltpu.with_memory_space_constraint(value, pltpu.VMEM) for value in values]
 
 
 def lanes(rows):
     return lax.broadcasted_iota(jnp.int32, (rows, 128), 1)
 
 
-def pack_kernel(fold, conductance, region, field, velocity, up, down, inner, outer, reflect, *corners):
-    top = lax.axis_index("row").astype(jnp.float32)
+def layer(source, c, r):
+    return source[pl.ds(c * 64 + r * 8, 8), :]
+
+
+def inner_kernel(field, velocity, inner):
+    middle = lax.axis_index("row").astype(jnp.float32) * 8.0 + 1.5
+    pull = diffuse * (middle + 0.5) / jnp.full((8, 128), middle)
+    carry = pull - advect * jnp.minimum(layer(velocity, 0, 1), 0.0)
+    stretch = (0.5 * advect) * layer(field, 0, 1)
+    for c in range(3):
+        inner[pl.ds(8 * c, 8), :] = layer(field, c, 0)
+        inner[pl.ds(8 * (3 + c), 8), :] = layer(velocity, c, 0)
+        inner[pl.ds(8 * (6 + c), 8), :] = layer(field, c, 1)
+        inner[pl.ds(8 * (9 + c), 8), :] = layer(velocity, c, 1)
+        inner[pl.ds(8 * (12 + c), 8), :] = carry * layer(field, c, 2) + stretch * layer(
+            velocity, c, 2
+        )
+
+
+def sides_kernel(
+    fold, conductance, region, field, velocity, far_field, far_flow, up, down, reflect, *corners
+):
+    top = lax.axis_index("row")
     kinds = region[...]
     value = jnp.zeros(kinds.shape, jnp.float32)
     for kind in range(conductance.shape[0]):
@@ -52,11 +75,11 @@
     def column(source, c, q):
         return source[pl.ds(c * 64 + q, 8, stride=8), :]
 
-    def layer(source, c, r):
-        return source[pl.ds(c * 64 + r * 8, 8), :]
-
-    radius = lax.broadcasted_iota(jnp.int32, (8, 128), 0).astype(jnp.float32) + (top * 8.0 + 0.5)
-    turn = diffuse / radius
+    def cell(source, r, q):
+        return source[pl.ds(r * 8 + q, 3, stride=64), :]
+
+    radius = lax.broadcasted_iota(jnp.int32, (8, 128), 0).astype(jnp.float32)
+    turn = diffuse / (radius + (top.astype(jnp.float32) * 8.0 + 0.5))
     for out, (one, two, three), direction in ((up, (7, 6, 5), -1.0), (down, (0, 1, 2), 1.0)):
         for c in range(3):
             out[pl.ds(8 * c, 8), :] = column(field, c, one)
@@ -74,72 +97,42 @@
             out[pl.ds(8 * (12 + c), 8), :] = term[c]
         out[pl.ds(wall_row, 1), :] = reflect[pl.ds(one, 1), :]
         out[pl.ds(wall_row + 1, 1), :] = reflect[pl.ds(two, 1), :]
+        for place, (r, q) in enumerate(((0, one), (0, two), (1, one))):
+            for part, source in enumerate((far_field, far_flow)):
+                out[pl.ds(corner_row + 8 * place + 3 * part, 3), :] = jnp.where(
+                    top == 0, cell(source, r, q), cell(source, 7 - r, q)
+                )
     for side, (one, two) in ((0, (7, 6)), (1, (0, 1))):
         if fold:
-            out, base = (down, up)[side], corner_row
+            out, base = (down, up)[side], axis_row
         else:
             out, base = corners[side], 0
         for place, (r, q) in enumerate(((0, one), (0, two), (1, one))):
-            out[pl.ds(base + 8 * place, 3), :] = field[pl.ds(r * 8 + q, 3, stride=64), :]
-            out[pl.ds(base + 8 * place + 3, 3), :] = velocity[pl.ds(r * 8 + q, 3, stride=64), :]
-    for out, (one, two, three), direction in ((inner, (0, 1, 2), 1.0), (outer, (7, 6, 5), -1.0)):
-        middle = top * 8.0 + (two + 0.5)
-        pull = diffuse * (middle + 0.5 * direction) / jnp.full((8, 128), middle)
-        speed = layer(velocity, 0, two)
-        carry = pull + advect * jnp.maximum(-direction * speed, 0.0)
-        stretch = (0.5 * advect * direction) * layer(field, 0, two)
-        for c in range(3):
-            out[pl.ds(8 * c, 8), :] = layer(field, c, one)
-            out[pl.ds(8 * (3 + c), 8), :] = layer(velocity, c, one)
-            out[pl.ds(8 * (6 + c), 8), :] = layer(field, c, two)
-            out[pl.ds(8 * (9 + c), 8), :] = layer(velocity, c, two)
-            out[pl.ds(8 * (12 + c), 8), :] = carry * layer(field, c, three) + stretch * layer(
-                velocity, c, three
-            )
-
-
-def radial_kernel(below, above, inner, outer, out):
-    low_half = lax.axis_index("row") == 0
-    for tile in range(tiles):
-        rows = pl.ds(8 * tile, 8)
-        out[rows, :] = jnp.where(low_half, outer[rows, :], inner[rows, :])
-    for source, base in ((below, low_corner), (above, high_corner)):
-        for place, (one, two, first) in enumerate(((7, 0, 0), (7, 0, 48), (6, 1, 0))):
-            out[pl.ds(base + 8 * place, 6), :] = jnp.where(
-                low_half,
-                source[pl.ds(first + one, 6, stride=8), :],
-                source[pl.ds(first + two, 6, stride=8), :],
-            )
+            out[pl.ds(base + 8 * place, 3), :] = cell(field, r, q)
+            out[pl.ds(base + 8 * place + 3, 3), :] = cell(velocity, r, q)
 
 
 def window_kernel(
-    fold, field, velocity, below, above, behind, across, reflect, *rest
+    fold, field, velocity, far_field, far_flow, below, above, behind, reflect, *rest
 ):
     if fold:
-        corner_low, corner_high, corner_base = above, below, corner_row
-        walls, strip, cells = rest[0], rest[1], rest[2]
+        axis_low, axis_high, axis_base = above, below, axis_row
     else:
-        corner_low, corner_high, corner_base = rest[0], rest[1], 0
-        walls, strip, cells = rest[2], rest[3], rest[4]
+        axis_low, axis_high, axis_base = rest[0], rest[1], 0
+    walls, strip, cells = rest[-3:]
     low_half = lax.axis_index("row") == 0
     nothing = jnp.zeros((8, 128), jnp.float32)
-    empty = jnp.zeros((sub, 128), jnp.float32)
     for c in range(6):
-        source = field if c < 3 else velocity
+        source, far = (field, far_field) if c < 3 else (velocity, far_flow)
         sign = signs[c % 3]
-        base = 64 * (c % 3)
-        cells[pl.ds(row_of(c, 0), sub), :] = empty
-        cells[pl.ds(row_of(c, window - 1), sub), :] = empty
         for r in range(8):
-            cells[pl.ds(row_of(c, r + 3), 8), :] = source[pl.ds(base + 8 * r, 8), :]
-        for w in range(1, window - 1):
+            cells[pl.ds(row_of(c, r + 3), 8), :] = layer(source, c % 3, r)
+        for w in range(window):
             cells[pl.ds(row_of(c, w) + 8, 8), :] = nothing
-        for w, first in ((2, 0), (1, 48)):
-            place = pl.ds(first + 8 * c, 8)
-            cells[pl.ds(row_of(c, w), 8), :] = jnp.where(
-                low_half, sign * behind[place, :], across[place, :]
-            )
-            cells[pl.ds(row_of(c, 13 - w), 8), :] = jnp.where(low_half, across[place, :], 0.0)
+        for w in range(3):
+            ghost = sign * behind[pl.ds(48 * (2 - w) + 8 * c, 8), :] if w > 0 else 0.0
+            cells[pl.ds(row_of(c, w), 8), :] = jnp.where(low_half, ghost, layer(far, c % 3, 5 + w))
+            cells[pl.ds(row_of(c, 11 + w), 8), :] = jnp.where(low_half, layer(far, c % 3, w), 0.0)
         for depth in range(2):
             place = pl.ds(48 * depth + 8 * c, 8)
             cells[pl.ds(row_of(c, 3) + 15 - depth, 8, stride=sub), :] = below[place, :]
@@ -147,12 +140,9 @@
     flip = lax.broadcasted_iota(jnp.int32, (6, 128), 0)
     flip = jnp.where((flip == 2) | (flip == 5), 1.0, -1.0)
     for place, (w, step) in enumerate(((2, 0), (2, 1), (1, 0))):
-        for axis_source, base, q in (
-            (corner_low, low_corner, 15 - step),
-            (corner_high, high_corner, 8 + step),
-        ):
-            ghost = flip * axis_source[pl.ds(corner_base + 8 * place, 6), :]
-            other = across[pl.ds(base + 8 * place, 6), :]
+        for axis_source, source, q in ((axis_low, below, 15 - step), (axis_high, above, 8 + step)):
+            ghost = flip * axis_source[pl.ds(axis_base + 8 * place, 6), :]
+            other = source[pl.ds(corner_row + 8 * place, 6), :]
             low = jnp.where(low_half, ghost, other)
             high = jnp.where(low_half, other, 0.0)
             for c in range(6):
@@ -229,7 +219,7 @@
 
 
 def stage_kernel(
-    many, below, above, behind, across, walls, strip, *rest
+    many, below, above, behind, walls, strip, *rest
 ):
     others = rest[: 2 if many else 1]
     (cells, basis, gram, message, advanced, first, second, edge_low, edge_high) = rest[len(others) :]
@@ -381,9 +371,8 @@
             first[pl.ds(row_of(c, w), sub), :] = center[c] + change[c]
     for c in range(3):
         rows = pl.ds(8 * (12 + c), 8)
-        low, high = pl.ds(row_of(c, 1), 8), pl.ds(row_of(c, 12), 8)
-        first[low, :] += jnp.where(low_half, signs[c] * behind[rows, :], across[rows, :])
-        first[high, :] += jnp.where(low_half, across[rows, :], 0.0)
+        low = pl.ds(row_of(c, 1), 8)
+        first[low, :] = first[low, :] + jnp.where(low_half, signs[c] * behind[rows, :], 0.0)
         before = pl.ds(row_of(c, 3) + 14, 8, stride=sub)
         after = pl.ds(row_of(c, 3) + 9, 8, stride=sub)
         first[before, :] = first[before, :] + below[rows, :]
@@ -491,46 +480,49 @@
     vectors = basis.shape[0]
     field_rows = field.reshape(192, 128)
     flow_rows = velocity.reshape(192, 128)
-    basis_rows = basis.reshape(vectors * 192, 128)
-    side = corner_row if not fold else side_rows
-    packed = pl.pallas_call(
-        functools.partial(pack_kernel, fold),
-        in_specs=[pl.BlockSpec(memory_space=pltpu.SMEM)] + vmem(3),
-        out_specs=vmem(5 if fold else 7),
-        out_shape=[
-            shape(side, 128),
-            shape(side, 128),
-            shape(8 * tiles, 128),
-            shape(8 * tiles, 128),
-            shape(8, 128),
-        ]
-        + ([] if fold else [shape(24, 128)] * 2),
-    )(wall_conductance, wall_region, field_rows, flow_rows)
-    up, down, inner, outer, reflect = packed[:5]
-    below = shift(up, "phi", 1)
-    above = shift(down, "phi", -1)
+    swap = [(0, 1), (1, 0)]
+    far_field = lax.ppermute(field_rows, "row", swap)
+    far_flow = lax.ppermute(flow_rows, "row", swap)
+    field_rows, flow_rows, basis_rows = near(
+        field_rows, flow_rows, basis.reshape(vectors * 192, 128)
+    )
+    inner = pl.pallas_call(
+        inner_kernel, in_specs=vmem(2), out_specs=vmem(1)[0], out_shape=shape(8 * tiles, 128)
+    )(field_rows, flow_rows)
     half = loop // 2
     turned = []
     for p in range(loop):
         for r in range(halves):
             turned.append((p * halves + r, ((p + half) % loop if r == 0 else p) * halves + r))
     behind = lax.ppermute(inner, ("phi", "row"), turned)
+    far_field, far_flow = near(far_field, far_flow)
+    side = side_rows if fold else axis_row
+    packed = pl.pallas_call(
+        functools.partial(sides_kernel, fold),
+        in_specs=[pl.BlockSpec(memory_space=pltpu.SMEM)] + vmem(5),
+        out_specs=vmem(3 if fold else 5),
+        out_shape=[shape(side, 128), shape(side, 128), shape(8, 128)]
+        + ([] if fold else [shape(24, 128)] * 2),
+    )(wall_conductance, wall_region, field_rows, flow_rows, far_field, far_flow)
+    up, down, reflect = packed[:3]
+    below = shift(up, "phi", 1)
+    above = shift(down, "phi", -1)
     corners = []
     if not fold:
-        corners = [shift(packed[5], "phi", half + 1), shift(packed[6], "phi", half - 1)]
+        corners = [shift(packed[3], "phi", half + 1), shift(packed[4], "phi", half - 1)]
     gram = pl.pallas_call(
         gram_kernel, in_specs=vmem(1), out_specs=vmem(1)[0], out_shape=shape(1, 128)
     )(basis_rows)
-    radial = pl.pallas_call(
-        radial_kernel, in_specs=vmem(4), out_specs=vmem(1)[0], out_shape=shape(radial_rows, 128)
-    )(below, above, inner, outer)
-    across = lax.ppermute(radial, "row", [(0, 1), (1, 0)])
+    below, above, behind, gram, *corners = lax.optimization_barrier(
+        (below, above, behind, gram, *corners)
+    )
+    below, above, behind, gram, *corners = near(below, above, behind, gram, *corners)
     walls, strip, cells = pl.pallas_call(
         functools.partial(window_kernel, fold),
-        in_specs=vmem(7 + len(corners)),
+        in_specs=vmem(8 + len(corners)),
         out_specs=vmem(3),
         out_shape=[shape(sub, 128), shape(6 * sub, 128), shape(6 * window * sub, 128)],
-    )(field_rows, flow_rows, below, above, behind, across, reflect, *corners)
+    )(field_rows, flow_rows, far_field, far_flow, below, above, behind, reflect, *corners)
     if many:
         up_pairs = [(i, i + 1) for i in range(ends - 1)]
         others = [
@@ -538,12 +530,13 @@
             lax.ppermute(strip, "gz", [(b, a) for a, b in up_pairs]),
         ]
     else:
-        others = [lax.ppermute(strip, "gz", [(0, 1), (1, 0)])]
+        others = [lax.ppermute(strip, "gz", swap)]
+    walls, strip, cells, *others = near(walls, strip, cells, *others)
     axes = ("phi", "gz", "row")
     devices = lax.axis_size(axes)
     message, advanced = pl.pallas_call(
         functools.partial(stage_kernel, many),
-        in_specs=vmem(9 + len(others)),
+        in_specs=vmem(8 + len(others)),
         out_specs=vmem(2),
         out_shape=[shape(devices, 1, 128), shape(192, 128)],
         scratch_shapes=[
@@ -552,13 +545,17 @@
             pltpu.VMEM((3 * sub, 128), jnp.float32),
             pltpu.VMEM((3 * sub, 128), jnp.float32),
         ],
-    )(below, above, behind, across, walls, strip, *others, cells, basis_rows, gram)
+    )(below, above, behind, walls, strip, *others, cells, basis_rows, gram)
     messages = lax.all_to_all(message, axes, 0, 0, tiled=True)
+    messages, advanced = near(messages, advanced)
     out, hessenberg = pl.pallas_call(
         functools.partial(finish_kernel, float(field.size * devices)),
         in_specs=vmem(3),
         out_specs=vmem(1) + [pl.BlockSpec(memory_space=pltpu.SMEM)],
-        out_shape=[shape(192, 128), shape(vectors + 1)],
+        out_shape=[
+            jax.ShapeDtypeStruct((192, 128), jnp.float32),
+            jax.ShapeDtypeStruct((vectors + 1,), jnp.float32),
+        ],
     )(messages, advanced, basis_rows)
     return out.reshape(field.shape), hessenberg
 

time: 45.9 us -> 36.3 us (0.79)
  Pallas kernels: 13.3 us -> 4.59 us
  waiting for transfers between devices: 8.05 us -> 6.6 us
  local copies, waits for them, and re-layouts: 1.89 us -> 2.93 us
  blocking collectives: 11.7 us -> 11 us
    pallas_call x4, Pallas kernels: 9.2 us -> 3.38 us  [the longest x1 1.64 us: local(): pl.pallas_call(functools.partial(stage_kernel, many), in_specs=vmem(8 + l...]
    ppermute x2, waiting for transfers between devices: 3.63 us -> 0.01 us  [shift(): lax.ppermute(value, axis, [(i, (i + step) % count) for i in range(count)])]
    ppermute x2 -> x3, waiting for transfers between devices: 0.82 us -> 3.9 us  [the longest x1 2.47 us: local(): others = [lax.ppermute(strip, 'gz', swap)]]
    pallas_call x1, Pallas kernels: 1.99 us -> 0.35 us  [local(): pl.pallas_call(gram_kernel, in_specs=vmem(1), out_specs=vmem(1)[0], out_s...]
    pallas_call x1, Pallas kernels: 2.07 us -> 0.86 us  [local(): pl.pallas_call(functools.partial(finish_kernel, float(field.size * device...]
    unnamed x12 -> x14, local copies, waits for them, and re-layouts: 1.89 us -> 2.93 us
    ppermute x1, waiting for transfers between devices: 3.61 us -> 2.69 us  [local(): behind = lax.ppermute(inner, ('phi', 'row'), turned)]
    ppermute x2 -> x3, starting transfers between devices: 1.49 us -> 2.28 us  [the longest x1 1.68 us: local(): others = [lax.ppermute(strip, 'gz', swap)]]
  transfers between devices with their start and end apart: 5 -> 6, of which waited for: 4 -> 4; matrix products, arithmetic and copies ran while one was open for 0% -> 0% of each run, Pallas kernels for 4% -> 1%
where the time goes in v3:
time: 36.3 us; the launch traced here: 36 us
  blocking collectives  11 us (30%)
  starting transfers between devices  10.2 us (28%)
  waiting for transfers between devices  6.6 us (18%)
  Pallas kernels  4.59 us (13%)
  local copies, waits for them, and re-layouts  2.93 us (8%)
  between operations  0.71 us (2%)
    all_to_all x1, blocking collectives, local(): messages = lax.all_to_all(message, axes, 0, 0, tiled=True)  11 us
    ppermute x2, starting transfers between devices, shift(): lax.ppermute(value, axis, [(i, (i + step) % count) for i in range(count)])  4.88 us
    ppermute x1, starting transfers between devices, local(): behind = lax.ppermute(inner, ('phi', 'row'), turned)  2.99 us
    unnamed x14, local copies, waits for them, and re-layouts  2.93 us
    ppermute x1, waiting for transfers between devices, local(): behind = lax.ppermute(inner, ('phi', 'row'), turned)  2.69 us
    ppermute x1, waiting for transfers between devices, local(): others = [lax.ppermute(strip, 'gz', swap)]  2.47 us
    ppermute x1, starting transfers between devices, local(): others = [lax.ppermute(strip, 'gz', swap)]  1.68 us
    pallas_call x1, Pallas kernels, local(): pl.pallas_call(functools.partial(stage_kernel, many), in_specs=vmem(8 + l...  1.64 us
  transfers between devices with their start and end apart: 6, of which 4 were waited for; matrix products, arithmetic and copies ran while one was open for 0% of the time, Pallas kernels for 1%

profile of v3, /device:TPU:0, one launch (start us, length us, event | category | flops | bytes accessed | tf_op | source)
XLA Modules:
  0.0 36.0 jit_solution(9746895159016339118)
XLA Ops:
  0.6 0.5 %collective-permute-start = (f32[192,128]{1,0:T(8,128)}, f32[192,128]{1,0:T(8,128)S(1)}, u32[]{:S(2)}, u32[]{:S(2)}) collective-permute-start(f32[192,128]{1,0:T(8,128)} %bitcast.7), channel_id=1, source_target_pairs={{0,1},{1,0},{2,3},{3,2},{4,5},{5,4},{6,7},{7,6},{8,9},{9,8},{10,11... | collective-permute-start | bytes 294920 | tf_op jit(solution)/shard_map/ppermute | solution.py:484
  1.1 0.1 collective-permute-start.1
  1.2 1.1 %collective-permute-done.far_field = f32[192,128]{1,0:T(8,128)S(1)} collective-permute-done((f32[192,128]{1,0:T(8,128)}, f32[192,128]{1,0:T(8,128)S(1)}, u32[]{:S(2)}, u32[]{:S(2)}) %collective-permute-start) | collective-permute-done | bytes 98336 | tf_op jit(solution)/shard_map/ppermute | solution.py:484
  2.3 0.4 collective-permute-done.1.far_flow
  2.7 0.0 copy-start.2
  2.7 0.9 %copy-done.2 = f32[3,8,8,128]{3,2,1,0:T(8,128)S(1)} copy-done((f32[3,8,8,128]{3,2,1,0:T(8,128)S(1)}, f32[3,8,8,128]{3,2,1,0:T(8,128)}, u32[]{:S(2)}) %copy-start.2) | copy-done | bytes 98328
  3.6 0.0 copy-start.4
  3.6 0.9 %copy-done.4 = f32[3,8,8,128]{3,2,1,0:T(8,128)S(1)} copy-done((f32[3,8,8,128]{3,2,1,0:T(8,128)S(1)}, f32[3,8,8,128]{3,2,1,0:T(8,128)}, u32[]{:S(2)}) %copy-start.4) | copy-done | bytes 98328
  4.4 0.8 %shard_map.68 = (f32[176,128]{1,0:T(8,128)S(1)}, f32[176,128]{1,0:T(8,128)S(1)}, f32[8,128]{1,0:T(8,128)S(1)}) custom-call(f32[8]{0:T(128)} %conductance.1, s32[8,128]{1,0:T(8,128)} %region.1, f32[192,128]{1,0:T(8,128)S(1)} %bitcast.8, f32[192,128]{1,0:T(8,128)S(1)} %bitcast.12, f32[192,128]{1,0:T(8,128)S(1)} %collective-permute-done.far_field, ...), custom_call_target="tpu_custom_call" | custom-call | tf_op jit(solution)/shard_map/pallas_call | solution.py:500
  5.2 0.0 copy-start.6
  5.2 2.8 %collective-permute-start.2 = (f32[176,128]{1,0:T(8,128)S(1)}, f32[176,128]{1,0:T(8,128)S(1)}, u32[]{:S(2)}, u32[]{:S(2)}) collective-permute-start(f32[176,128]{1,0:T(8,128)S(1)} %get-tuple-element.16), channel_id=1, source_target_pairs={{0,4},{4,8},{8,12},{12,0},{1,5},{5,9},{9,13},{13,1},{2,6},{6,10},{... | collective-permute-start | bytes 270344 | tf_op jit(solution)/shard_map/ppermute | solution.py:471
  8.0 2.1 %collective-permute-start.3 = (f32[176,128]{1,0:T(8,128)S(1)}, f32[176,128]{1,0:T(8,128)S(1)}, u32[]{:S(2)}, u32[]{:S(2)}) collective-permute-start(f32[176,128]{1,0:T(8,128)S(1)} %get-tuple-element.17), channel_id=1, source_target_pairs={{0,12},{4,0},{8,4},{12,8},{1,13},{5,1},{9,5},{13,9},{2,14},{6,2},{... | collective-permute-start | bytes 270344 | tf_op jit(solution)/shard_map/ppermute | solution.py:471
  10.1 0.0 copy-start.3
  10.1 0.0 copy-start.5
  10.1 0.0 copy-done.6
  10.1 3.0 %collective-permute-start.4 = (f32[120,128]{1,0:T(8,128)S(1)}, f32[120,128]{1,0:T(8,128)S(1)}, u32[]{:S(2)}, u32[]{:S(2)}) collective-permute-start(f32[120,128]{1,0:T(8,128)S(1)} %shard_map.69), channel_id=1, source_target_pairs={{0,8},{1,1},{4,12},{5,5},{8,0},{9,9},{12,4},{13,13},{2,10},{3,3},{... | collective-permute-start | bytes 184328 | tf_op jit(solution)/shard_map/ppermute | solution.py:497
  13.1 0.0 copy-start
  13.2 1.1 %copy-done = f32[8,3,8,8,128]{4,3,2,1,0:T(8,128)S(1)} copy-done((f32[8,3,8,8,128]{4,3,2,1,0:T(8,128)S(1)}, f32[8,3,8,8,128]{4,3,2,1,0:T(8,128)}, u32[]{:S(2)}) %copy-start) | copy-done | bytes 786456
  14.3 0.0 copy-start.1
  14.3 0.4 shard_map.70.rest_3_
  14.6 2.7 %collective-permute-done.4.behind = f32[120,128]{1,0:T(8,128)S(1)} collective-permute-done((f32[120,128]{1,0:T(8,128)S(1)}, f32[120,128]{1,0:T(8,128)S(1)}, u32[]{:S(2)}, u32[]{:S(2)}) %collective-permute-start.4) | collective-permute-done | bytes 61472 | tf_op jit(solution)/shard_map/ppermute | solution.py:497
  17.3 0.0 collective-permute-done.2.below
  17.3 0.0 collective-permute-done.3.above
  17.3 0.0 copy-done.3
  17.3 0.0 copy-done.5
  17.3 1.0 %shard_map.71 = (f32[16,128]{1,0:T(8,128)S(1)}, f32[96,128]{1,0:T(8,128)S(1)}, f32[1344,128]{1,0:T(8,128)S(1)}) custom-call(f32[192,128]{1,0:T(8,128)S(1)} %bitcast.10, f32[192,128]{1,0:T(8,128)S(1)} %bitcast.14, f32[192,128]{1,0:T(8,128)S(1)} %collective-permute-done.far_field, f32[192,128]{1,0:T(8,128)S(1)} %collective-permute-done.1.far_flow, ...), custom_call_target="tpu_custom_call" | custom-call | tf_op jit(solution)/shard_map/pallas_call | solution.py:520
  18.3 1.7 %collective-permute-start.5 = (f32[96,128]{1,0:T(8,128)S(1)}, f32[96,128]{1,0:T(8,128)S(1)}, u32[]{:S(2)}, u32[]{:S(2)}) collective-permute-start(f32[96,128]{1,0:T(8,128)S(1)} %get-tuple-element.23.strip), channel_id=1, source_target_pairs={{0,2},{2,0},{1,3},{3,1},{4,6},{6,4},{5,7},{7,5},{8,10},{10,8},{9,1... | collective-permute-start | bytes 147464 | tf_op jit(solution)/shard_map/ppermute | solution.py:533
  20.0 2.5 %collective-permute-done.5.rest_0_ = f32[96,128]{1,0:T(8,128)S(1)} collective-permute-done((f32[96,128]{1,0:T(8,128)S(1)}, f32[96,128]{1,0:T(8,128)S(1)}, u32[]{:S(2)}, u32[]{:S(2)}) %collective-permute-start.5) | collective-permute-done | bytes 49184 | tf_op jit(solution)/shard_map/ppermute | solution.py:533
  22.5 0.0 copy-done.1
  22.5 1.6 %shard_map.72 = (f32[16,1,128]{2,1,0:T(1,128)S(1)}, f32[192,128]{1,0:T(8,128)S(1)}) custom-call(f32[176,128]{1,0:T(8,128)S(1)} %collective-permute-done.2.below, f32[176,128]{1,0:T(8,128)S(1)} %collective-permute-done.3.above, f32[120,128]{1,0:T(8,128)S(1)} %collective-permute-done.4.behind, f32[16,128]{1,0:T(8,128)S(1)} %get-tuple-element.22.walls, ...), custom_call_target="tpu_custom_call" | custom-call | tf_op jit(solution)/shard_map/pallas_call | solution.py:537
  24.1 11.0 %all_to_all.5.messages = f32[16,1,128]{2,1,0:T(1,128)S(1)} all-to-all(f32[16,1,128]{2,1,0:T(1,128)S(1)} %get-tuple-element.26), channel_id=1, replica_groups=mesh['groups'=2,'phi'=4,'gz'=2,'row'=2] {'phi','gz','row'}, dimensions={0} | all-to-all | bytes 16384 | tf_op jit(solution)/shard_map/all_to_all | solution.py:549
  35.1 0.9 %shard_map.73 = (f32[192,128]{1,0:T(8,128)}, f32[9]{0:T(128)}) custom-call(f32[16,1,128]{2,1,0:T(1,128)S(1)} %all_to_all.5.messages, f32[192,128]{1,0:T(8,128)S(1)} %get-tuple-element.27.advanced, f32[1536,128]{1,0:T(8,128)S(1)} %bitcast.6), custom_call_target="tpu_custom_call" | custom-call | tf_op jit(solution)/shard_map/pallas_call | solution.py:551
  (1 shorter events, 0.0 us)
Async XLA Ops:
  0.6 1.7 %collective-permute-start = (f32[192,128]{1,0:T(8,128)}, f32[192,128]{1,0:T(8,128)S(1)}, u32[]{:S(2)}, u32[]{:S(2)}) collective-permute-start(f32[192,128]{1,0:T(8,128)} %bitcast.7), channel_id=1, source_target_pairs={{0,1},{1,0},{2,3},{3,2},{4,5},{5,4},{6,7},{7,6},{8,9},{9,8},{10,11... | collective-permute-start | bytes 294920 | tf_op jit(solution)/shard_map/ppermute | solution.py:484
  1.1 1.5 %collective-permute-start.1 = (f32[192,128]{1,0:T(8,128)}, f32[192,128]{1,0:T(8,128)S(1)}, u32[]{:S(2)}, u32[]{:S(2)}) collective-permute-start(f32[192,128]{1,0:T(8,128)} %bitcast.11), channel_id=1, source_target_pairs={{0,1},{1,0},{2,3},{3,2},{4,5},{5,4},{6,7},{7,6},{8,9},{9,8},{10,11... | collective-permute-start | bytes 294920 | tf_op jit(solution)/shard_map/ppermute | solution.py:485
  2.7 0.9 %copy-start.2 = (f32[3,8,8,128]{3,2,1,0:T(8,128)S(1)}, f32[3,8,8,128]{3,2,1,0:T(8,128)}, u32[]{:S(2)}) copy-start(f32[3,8,8,128]{3,2,1,0:T(8,128)} %param.5) | copy-start | bytes 294916
  3.6 0.9 %copy-start.4 = (f32[3,8,8,128]{3,2,1,0:T(8,128)S(1)}, f32[3,8,8,128]{3,2,1,0:T(8,128)}, u32[]{:S(2)}) copy-start(f32[3,8,8,128]{3,2,1,0:T(8,128)} %param.6) | copy-start | bytes 294916
  5.2 4.9 %copy-start.6 = (f32[8,128]{1,0:T(8,128)}, f32[8,128]{1,0:T(8,128)S(1)}, u32[]{:S(2)}) copy-start(f32[8,128]{1,0:T(8,128)S(1)} %get-tuple-element.21.reflect) | copy-start | bytes 12292
  5.2 12.1 %collective-permute-start.2 = (f32[176,128]{1,0:T(8,128)S(1)}, f32[176,128]{1,0:T(8,128)S(1)}, u32[]{:S(2)}, u32[]{:S(2)}) collective-permute-start(f32[176,128]{1,0:T(8,128)S(1)} %get-tuple-element.16), channel_id=1, source_target_pairs={{0,4},{4,8},{8,12},{12,0},{1,5},{5,9},{9,13},{13,1},{2,6},{6,10},{... | collective-permute-start | bytes 270344 | tf_op jit(solution)/shard_map/ppermute | solution.py:471
  8.0 9.3 %collective-permute-start.3 = (f32[176,128]{1,0:T(8,128)S(1)}, f32[176,128]{1,0:T(8,128)S(1)}, u32[]{:S(2)}, u32[]{:S(2)}) collective-permute-start(f32[176,128]{1,0:T(8,128)S(1)} %get-tuple-element.17), channel_id=1, source_target_pairs={{0,12},{4,0},{8,4},{12,8},{1,13},{5,1},{9,5},{13,9},{2,14},{6,2},{... | collective-permute-start | bytes 270344 | tf_op jit(solution)/shard_map/ppermute | solution.py:471
  10.1 7.2 %copy-start.3 = (f32[3,8,8,128]{3,2,1,0:T(8,128)S(1)}, f32[3,8,8,128]{3,2,1,0:T(8,128)}, u32[]{:S(2)}) copy-start(f32[3,8,8,128]{3,2,1,0:T(8,128)} %param.5) | copy-start | bytes 294916
  10.1 7.2 %copy-start.5 = (f32[3,8,8,128]{3,2,1,0:T(8,128)S(1)}, f32[3,8,8,128]{3,2,1,0:T(8,128)}, u32[]{:S(2)}) copy-start(f32[3,8,8,128]{3,2,1,0:T(8,128)} %param.6) | copy-start | bytes 294916
  10.1 7.2 %collective-permute-start.4 = (f32[120,128]{1,0:T(8,128)S(1)}, f32[120,128]{1,0:T(8,128)S(1)}, u32[]{:S(2)}, u32[]{:S(2)}) collective-permute-start(f32[120,128]{1,0:T(8,128)S(1)} %shard_map.69), channel_id=1, source_target_pairs={{0,8},{1,1},{4,12},{5,5},{8,0},{9,9},{12,4},{13,13},{2,10},{3,3},{... | collective-permute-start | bytes 184328 | tf_op jit(solution)/shard_map/ppermute | solution.py:497
  13.1 1.1 %copy-start = (f32[8,3,8,8,128]{4,3,2,1,0:T(8,128)S(1)}, f32[8,3,8,8,128]{4,3,2,1,0:T(8,128)}, u32[]{:S(2)}) copy-start(f32[8,3,8,8,128]{4,3,2,1,0:T(8,128)} %param.7) | copy-start | bytes 2359300
  14.3 8.2 %copy-start.1 = (f32[8,3,8,8,128]{4,3,2,1,0:T(8,128)S(1)}, f32[8,3,8,8,128]{4,3,2,1,0:T(8,128)}, u32[]{:S(2)}) copy-start(f32[8,3,8,8,128]{4,3,2,1,0:T(8,128)} %param.7) | copy-start | bytes 2359300
  18.3 4.2 %collective-permute-start.5 = (f32[96,128]{1,0:T(8,128)S(1)}, f32[96,128]{1,0:T(8,128)S(1)}, u32[]{:S(2)}, u32[]{:S(2)}) collective-permute-start(f32[96,128]{1,0:T(8,128)S(1)} %get-tuple-element.23.strip), channel_id=1, source_target_pairs={{0,2},{2,0},{1,3},{3,1},{4,6},{6,4},{5,7},{7,5},{8,10},{10,8},{9,1... | collective-permute-start | bytes 147464 | tf_op jit(solution)/shard_map/ppermute | solution.py:533

commit v4 on v3

--- a/solution.py
+++ b/solution.py
@@ -47,7 +47,7 @@
     return source[pl.ds(c * 64 + r * 8, 8), :]
 
 
-def inner_kernel(field, velocity, inner):
+def first_kernel(conductance, region, field, velocity, inner, reflect, field_copy, flow_copy):
     middle = lax.axis_index("row").astype(jnp.float32) * 8.0 + 1.5
     pull = diffuse * (middle + 0.5) / jnp.full((8, 128), middle)
     carry = pull - advect * jnp.minimum(layer(velocity, 0, 1), 0.0)
@@ -60,17 +60,19 @@
         inner[pl.ds(8 * (12 + c), 8), :] = carry * layer(field, c, 2) + stretch * layer(
             velocity, c, 2
         )
-
-
-def sides_kernel(
-    fold, conductance, region, field, velocity, far_field, far_flow, up, down, reflect, *corners
-):
-    top = lax.axis_index("row")
     kinds = region[...]
     value = jnp.zeros(kinds.shape, jnp.float32)
     for kind in range(conductance.shape[0]):
         value = jnp.where(kinds == kind, conductance[kind], value)
     reflect[...] = 1.0 - 2.0 * value / (1.0 + value)
+    field_copy[...] = field[...]
+    flow_copy[...] = velocity[...]
+
+
+def sides_kernel(
+    fold, field, velocity, far_field, far_flow, reflect, up, down, *corners
+):
+    top = lax.axis_index("row")
 
     def column(source, c, q):
         return source[pl.ds(c * 64 + q, 8, stride=8), :]
@@ -112,27 +114,40 @@
             out[pl.ds(base + 8 * place + 3, 3), :] = cell(velocity, r, q)
 
 
-def window_kernel(
-    fold, field, velocity, far_field, far_flow, below, above, behind, reflect, *rest
-):
+def packed_row(strip, value, w):
+    slot = lanes(value.shape[0]) // 8
+    return jnp.where(slot == w - 1, pltpu.roll(value, (8 * (w - 1) + 4) % 128, 1), strip)
+
+
+def frame_kernel(field, velocity, far_field, far_flow, strip, cells):
+    low_half = lax.axis_index("row") == 0
+    nothing = jnp.zeros((8, 128), jnp.float32)
+    for c in range(6):
+        source, far = (field, far_field) if c < 3 else (velocity, far_flow)
+        packed = nothing
+        for w in range(window):
+            if w < 3:
+                value = jnp.where(low_half, 0.0, layer(far, c % 3, 5 + w))
+            elif w < 11:
+                value = layer(source, c % 3, w - 3)
+            else:
+                value = jnp.where(low_half, layer(far, c % 3, w - 11), 0.0)
+            cells[pl.ds(row_of(c, w), 8), :] = value
+            cells[pl.ds(row_of(c, w) + 8, 8), :] = nothing
+            if 0 < w < window - 1:
+                packed = packed_row(packed, value, w)
+        strip[pl.ds(sub * c, 8), :] = packed
+        strip[pl.ds(sub * c + 8, 8), :] = nothing
+
+
+def window_kernel(fold, below, above, behind, reflect, frame_strip, frame, *rest):
     if fold:
         axis_low, axis_high, axis_base = above, below, axis_row
     else:
         axis_low, axis_high, axis_base = rest[0], rest[1], 0
     walls, strip, cells = rest[-3:]
     low_half = lax.axis_index("row") == 0
-    nothing = jnp.zeros((8, 128), jnp.float32)
     for c in range(6):
-        source, far = (field, far_field) if c < 3 else (velocity, far_flow)
-        sign = signs[c % 3]
-        for r in range(8):
-            cells[pl.ds(row_of(c, r + 3), 8), :] = layer(source, c % 3, r)
-        for w in range(window):
-            cells[pl.ds(row_of(c, w) + 8, 8), :] = nothing
-        for w in range(3):
-            ghost = sign * behind[pl.ds(48 * (2 - w) + 8 * c, 8), :] if w > 0 else 0.0
-            cells[pl.ds(row_of(c, w), 8), :] = jnp.where(low_half, ghost, layer(far, c % 3, 5 + w))
-            cells[pl.ds(row_of(c, 11 + w), 8), :] = jnp.where(low_half, layer(far, c % 3, w), 0.0)
         for depth in range(2):
             place = pl.ds(48 * depth + 8 * c, 8)
             cells[pl.ds(row_of(c, 3) + 15 - depth, 8, stride=sub), :] = below[place, :]
@@ -143,23 +158,32 @@
         for axis_source, source, q in ((axis_low, below, 15 - step), (axis_high, above, 8 + step)):
             ghost = flip * axis_source[pl.ds(axis_base + 8 * place, 6), :]
             other = source[pl.ds(corner_row + 8 * place, 6), :]
-            low = jnp.where(low_half, ghost, other)
-            high = jnp.where(low_half, other, 0.0)
-            for c in range(6):
-                cells[pl.ds(row_of(c, w) + q, 1), :] = low[c : c + 1]
-                cells[pl.ds(row_of(c, 13 - w) + q, 1), :] = high[c : c + 1]
+            low = pl.ds(row_of(0, w) + q, 6, stride=window * sub)
+            high = pl.ds(row_of(0, 13 - w) + q, 6, stride=window * sub)
+            cells[low, :] = jnp.where(low_half, ghost, other)
+            cells[high, :] = jnp.where(low_half, other, 0.0)
     walls[pl.ds(0, 8), :] = reflect[...]
-    walls[pl.ds(8, 8), :] = nothing
+    walls[pl.ds(8, 8), :] = jnp.zeros((8, 128), jnp.float32)
     walls[pl.ds(8, 2), :] = above[pl.ds(wall_row, 2), :]
     walls[pl.ds(15, 1), :] = below[pl.ds(wall_row, 1), :]
     walls[pl.ds(14, 1), :] = below[pl.ds(wall_row + 1, 1), :]
-    slot = lanes(sub) // 8
+    slot = lanes(8) // 8
     for c in range(6):
-        packed = jnp.where(slot == 12, pltpu.roll(walls[...], 100, 1), 0.0)
+        packed = strip[pl.ds(sub * c, 8), :]
+        for w in range(1, 3):
+            place = pl.ds(row_of(c, w), 8)
+            ghost = signs[c % 3] * behind[pl.ds(48 * (2 - w) + 8 * c, 8), :]
+            ghost = jnp.where(low_half, ghost, cells[place, :])
+            cells[place, :] = ghost
+            packed = packed_row(packed, ghost, w)
+        beyond = jnp.zeros((8, 128), jnp.float32)
         for w in range(1, window - 1):
-            row = cells[pl.ds(row_of(c, w), sub), :]
-            packed = jnp.where(slot == w - 1, pltpu.roll(row, (8 * (w - 1) + 4) % 128, 1), packed)
-        strip[pl.ds(sub * c, sub), :] = packed
+            beyond = packed_row(beyond, cells[pl.ds(row_of(c, w) + 8, 8), :], w)
+        if c == 0:
+            packed = jnp.where(slot == 12, pltpu.roll(walls[pl.ds(0, 8), :], 100, 1), packed)
+            beyond = jnp.where(slot == 12, pltpu.roll(walls[pl.ds(8, 8), :], 100, 1), beyond)
+        strip[pl.ds(sub * c, 8), :] = packed
+        strip[pl.ds(sub * c + 8, 8), :] = beyond
 
 
 def back(value, axis, step=1):
@@ -483,46 +507,52 @@
     swap = [(0, 1), (1, 0)]
     far_field = lax.ppermute(field_rows, "row", swap)
     far_flow = lax.ppermute(flow_rows, "row", swap)
-    field_rows, flow_rows, basis_rows = near(
-        field_rows, flow_rows, basis.reshape(vectors * 192, 128)
-    )
-    inner = pl.pallas_call(
-        inner_kernel, in_specs=vmem(2), out_specs=vmem(1)[0], out_shape=shape(8 * tiles, 128)
-    )(field_rows, flow_rows)
+    (basis_rows,) = near(basis.reshape(vectors * 192, 128))
+    inner, reflect, field_rows, flow_rows = pl.pallas_call(
+        first_kernel,
+        in_specs=[pl.BlockSpec(memory_space=pltpu.SMEM)] + vmem(3),
+        out_specs=vmem(4),
+        out_shape=[shape(8 * tiles, 128), shape(8, 128), shape(192, 128), shape(192, 128)],
+    )(wall_conductance, wall_region, field_rows, flow_rows)
     half = loop // 2
     turned = []
     for p in range(loop):
         for r in range(halves):
             turned.append((p * halves + r, ((p + half) % loop if r == 0 else p) * halves + r))
     behind = lax.ppermute(inner, ("phi", "row"), turned)
-    far_field, far_flow = near(far_field, far_flow)
+    field_rows, flow_rows, far_field, far_flow, reflect = near(
+        field_rows, flow_rows, far_field, far_flow, reflect
+    )
     side = side_rows if fold else axis_row
     packed = pl.pallas_call(
         functools.partial(sides_kernel, fold),
-        in_specs=[pl.BlockSpec(memory_space=pltpu.SMEM)] + vmem(5),
-        out_specs=vmem(3 if fold else 5),
-        out_shape=[shape(side, 128), shape(side, 128), shape(8, 128)]
-        + ([] if fold else [shape(24, 128)] * 2),
-    )(wall_conductance, wall_region, field_rows, flow_rows, far_field, far_flow)
-    up, down, reflect = packed[:3]
-    below = shift(up, "phi", 1)
-    above = shift(down, "phi", -1)
+        in_specs=vmem(5),
+        out_specs=vmem(2 if fold else 4),
+        out_shape=[shape(side, 128)] * 2 + ([] if fold else [shape(24, 128)] * 2),
+    )(field_rows, flow_rows, far_field, far_flow, reflect)
+    below = shift(packed[0], "phi", 1)
+    above = shift(packed[1], "phi", -1)
     corners = []
     if not fold:
-        corners = [shift(packed[3], "phi", half + 1), shift(packed[4], "phi", half - 1)]
+        corners = [shift(packed[2], "phi", half + 1), shift(packed[3], "phi", half - 1)]
     gram = pl.pallas_call(
         gram_kernel, in_specs=vmem(1), out_specs=vmem(1)[0], out_shape=shape(1, 128)
     )(basis_rows)
-    below, above, behind, gram, *corners = lax.optimization_barrier(
-        (below, above, behind, gram, *corners)
+    window_shapes = [shape(6 * sub, 128), shape(6 * window * sub, 128)]
+    strip, cells = pl.pallas_call(
+        frame_kernel, in_specs=vmem(4), out_specs=vmem(2), out_shape=window_shapes
+    )(field_rows, flow_rows, far_field, far_flow)
+    received = near(
+        *lax.optimization_barrier((below, above, behind, gram, strip, cells, *corners))
     )
-    below, above, behind, gram, *corners = near(below, above, behind, gram, *corners)
+    below, above, behind, gram, strip, cells = received[:6]
     walls, strip, cells = pl.pallas_call(
         functools.partial(window_kernel, fold),
-        in_specs=vmem(8 + len(corners)),
+        in_specs=vmem(6 + len(corners)),
         out_specs=vmem(3),
-        out_shape=[shape(sub, 128), shape(6 * sub, 128), shape(6 * window * sub, 128)],
-    )(field_rows, flow_rows, far_field, far_flow, below, above, behind, reflect, *corners)
+        out_shape=[shape(sub, 128)] + window_shapes,
+        input_output_aliases={4: 1, 5: 2},
+    )(below, above, behind, reflect, strip, cells, *received[6:])
     if many:
         up_pairs = [(i, i + 1) for i in range(ends - 1)]
         others = [

time: 36.3 us -> 32.8 us (0.904)
  local copies, waits for them, and re-layouts: 2.93 us -> 1.13 us
  waiting for transfers between devices: 6.6 us -> 5.45 us
    unnamed x14 -> x4, local copies, waits for them, and re-layouts: 2.93 us -> 1.13 us
    ppermute x1, waiting for transfers between devices: 1.07 us -> 0.08 us  [local(): far_field = lax.ppermute(field_rows, 'row', swap)]
    pallas_call x3 -> x4, Pallas kernels: 1.74 us -> 1.41 us  [the longest x1 0.99 us: local(): pl.pallas_call(first_kernel, in_specs=[pl.BlockSpec(memory_space=pltpu.SM...]
  transfers between devices with their start and end apart: 6 -> 6, of which waited for: 4 -> 4; matrix products, arithmetic and copies ran while one was open for 0% -> 0% of each run, Pallas kernels for 1% -> 5%
where the time goes in v4:
time: 32.8 us; the launch traced here: 32.5 us
  blocking collectives  11 us (34%)
  starting transfers between devices  10 us (30%)
  waiting for transfers between devices  5.45 us (17%)
  Pallas kernels  4.25 us (13%)
  local copies, waits for them, and re-layouts  1.13 us (3%)
  between operations  0.69 us (2%)
    all_to_all x1, blocking collectives, local(): messages = lax.all_to_all(message, axes, 0, 0, tiled=True)  11 us
    ppermute x2, starting transfers between devices, shift(): lax.ppermute(value, axis, [(i, (i + step) % count) for i in range(count)])  4.88 us
    ppermute x1, starting transfers between devices, local(): behind = lax.ppermute(inner, ('phi', 'row'), turned)  2.84 us
    ppermute x1, waiting for transfers between devices, local(): behind = lax.ppermute(inner, ('phi', 'row'), turned)  2.53 us
    ppermute x1, waiting for transfers between devices, local(): others = [lax.ppermute(strip, 'gz', swap)]  2.47 us
    ppermute x1, starting transfers between devices, local(): others = [lax.ppermute(strip, 'gz', swap)]  1.68 us
    pallas_call x1, Pallas kernels, local(): pl.pallas_call(functools.partial(stage_kernel, many), in_specs=vmem(8 + l...  1.63 us
    unnamed x4, local copies, waits for them, and re-layouts  1.13 us
  transfers between devices with their start and end apart: 6, of which 4 were waited for; matrix products, arithmetic and copies ran while one was open for 0% of the time, Pallas kernels for 5%

profile of v4, /device:TPU:0, one launch (start us, length us, event | category | flops | bytes accessed | tf_op | source)
XLA Modules:
  0.0 32.5 jit_solution(63446986491703242)
XLA Ops:
  0.6 0.5 %collective-permute-start = (f32[192,128]{1,0:T(8,128)}, f32[192,128]{1,0:T(8,128)S(1)}, u32[]{:S(2)}, u32[]{:S(2)}) collective-permute-start(f32[192,128]{1,0:T(8,128)} %bitcast.7), channel_id=1, source_target_pairs={{0,1},{1,0},{2,3},{3,2},{4,5},{5,4},{6,7},{7,6},{8,9},{9,8},{10,11... | collective-permute-start | bytes 294920 | tf_op jit(solution)/shard_map/ppermute | solution.py:508
  1.1 0.1 collective-permute-start.1
  1.2 1.0 %shard_map.68 = (f32[120,128]{1,0:T(8,128)S(1)}, f32[8,128]{1,0:T(8,128)S(1)}, f32[192,128]{1,0:T(8,128)S(1)}, f32[192,128]{1,0:T(8,128)S(1)}) custom-call(f32[8]{0:T(128)} %conductance.1, s32[8,128]{1,0:T(8,128)} %region.1, f32[192,128]{1,0:T(8,128)} %bitcast.8, f32[192,128]{1,0:T(8,128)} %bitcast.10), custom_call_target="tpu_custom_call" | custom-call | tf_op jit(solution)/shard_map/pallas_call | solution.py:511
  2.2 0.1 collective-permute-done.far_field
  2.3 0.4 %collective-permute-done.1.far_flow = f32[192,128]{1,0:T(8,128)S(1)} collective-permute-done((f32[192,128]{1,0:T(8,128)}, f32[192,128]{1,0:T(8,128)S(1)}, u32[]{:S(2)}, u32[]{:S(2)}) %collective-permute-start.1) | collective-permute-done | bytes 98336 | tf_op jit(solution)/shard_map/ppermute | solution.py:509
  2.7 0.1 shard_map.69
  2.7 2.8 %collective-permute-start.2 = (f32[176,128]{1,0:T(8,128)S(1)}, f32[176,128]{1,0:T(8,128)S(1)}, u32[]{:S(2)}, u32[]{:S(2)}) collective-permute-start(f32[176,128]{1,0:T(8,128)S(1)} %get-tuple-element.26), channel_id=1, source_target_pairs={{0,4},{4,8},{8,12},{12,0},{1,5},{5,9},{9,13},{13,1},{2,6},{6,10},{... | collective-permute-start | bytes 270344 | tf_op jit(solution)/shard_map/ppermute | solution.py:495
  5.5 2.1 %collective-permute-start.3 = (f32[176,128]{1,0:T(8,128)S(1)}, f32[176,128]{1,0:T(8,128)S(1)}, u32[]{:S(2)}, u32[]{:S(2)}) collective-permute-start(f32[176,128]{1,0:T(8,128)S(1)} %get-tuple-element.27), channel_id=1, source_target_pairs={{0,12},{4,0},{8,4},{12,8},{1,13},{5,1},{9,5},{13,9},{2,14},{6,2},{... | collective-permute-start | bytes 270344 | tf_op jit(solution)/shard_map/ppermute | solution.py:495
  7.6 2.8 %collective-permute-start.4 = (f32[120,128]{1,0:T(8,128)S(1)}, f32[120,128]{1,0:T(8,128)S(1)}, u32[]{:S(2)}, u32[]{:S(2)}) collective-permute-start(f32[120,128]{1,0:T(8,128)S(1)} %get-tuple-element.28), channel_id=1, source_target_pairs={{0,8},{1,1},{4,12},{5,5},{8,0},{9,9},{12,4},{13,13},{2,10},{3,3},{... | collective-permute-start | bytes 184328 | tf_op jit(solution)/shard_map/ppermute | solution.py:522
  10.5 0.0 copy-start
  10.5 1.1 %copy-done = f32[8,3,8,8,128]{4,3,2,1,0:T(8,128)S(1)} copy-done((f32[8,3,8,8,128]{4,3,2,1,0:T(8,128)S(1)}, f32[8,3,8,8,128]{4,3,2,1,0:T(8,128)}, u32[]{:S(2)}) %copy-start) | copy-done | bytes 786456
  11.6 0.4 %shard_map.70.rest_3_ = f32[1,128]{1,0:T(1,128)S(1)} custom-call(f32[1536,128]{1,0:T(8,128)S(1)} %bitcast.4), custom_call_target="tpu_custom_call" | custom-call | tf_op jit(solution)/shard_map/pallas_call | solution.py:538
  12.0 0.0 copy-start.1
  12.0 0.2 shard_map.71
  12.1 2.5 %collective-permute-done.4.behind = f32[120,128]{1,0:T(8,128)S(1)} collective-permute-done((f32[120,128]{1,0:T(8,128)S(1)}, f32[120,128]{1,0:T(8,128)S(1)}, u32[]{:S(2)}, u32[]{:S(2)}) %collective-permute-start.4) | collective-permute-done | bytes 61472 | tf_op jit(solution)/shard_map/ppermute | solution.py:522
  14.6 0.0 collective-permute-done.2.below
  14.6 0.0 collective-permute-done.3.above
  14.7 0.2 shard_map.72
  14.9 1.7 %collective-permute-start.5 = (f32[96,128]{1,0:T(8,128)S(1)}, f32[96,128]{1,0:T(8,128)S(1)}, u32[]{:S(2)}, u32[]{:S(2)}) collective-permute-start(f32[96,128]{1,0:T(8,128)S(1)} %get-tuple-element.37.strip), channel_id=1, source_target_pairs={{0,2},{2,0},{1,3},{3,1},{4,6},{6,4},{5,7},{7,5},{8,10},{10,8},{9,1... | collective-permute-start | bytes 147464 | tf_op jit(solution)/shard_map/ppermute | solution.py:563
  16.5 2.5 %collective-permute-done.5.rest_0_ = f32[96,128]{1,0:T(8,128)S(1)} collective-permute-done((f32[96,128]{1,0:T(8,128)S(1)}, f32[96,128]{1,0:T(8,128)S(1)}, u32[]{:S(2)}, u32[]{:S(2)}) %collective-permute-start.5) | collective-permute-done | bytes 49184 | tf_op jit(solution)/shard_map/ppermute | solution.py:563
  19.0 0.0 copy-done.1
  19.0 1.6 %shard_map.73 = (f32[16,1,128]{2,1,0:T(1,128)S(1)}, f32[192,128]{1,0:T(8,128)S(1)}) custom-call(f32[176,128]{1,0:T(8,128)S(1)} %collective-permute-done.2.below, f32[176,128]{1,0:T(8,128)S(1)} %collective-permute-done.3.above, f32[120,128]{1,0:T(8,128)S(1)} %collective-permute-done.4.behind, f32[16,128]{1,0:T(8,128)S(1)} %get-tuple-element.36.walls, ...), custom_call_target="tpu_custom_call" | custom-call | tf_op jit(solution)/shard_map/pallas_call | solution.py:567
  20.7 11.0 %all_to_all.5.messages = f32[16,1,128]{2,1,0:T(1,128)S(1)} all-to-all(f32[16,1,128]{2,1,0:T(1,128)S(1)} %get-tuple-element.40), channel_id=1, replica_groups=mesh['groups'=2,'phi'=4,'gz'=2,'row'=2] {'phi','gz','row'}, dimensions={0} | all-to-all | bytes 16384 | tf_op jit(solution)/shard_map/all_to_all | solution.py:579
  31.7 0.9 %shard_map.74 = (f32[192,128]{1,0:T(8,128)}, f32[9]{0:T(128)}) custom-call(f32[16,1,128]{2,1,0:T(1,128)S(1)} %all_to_all.5.messages, f32[192,128]{1,0:T(8,128)S(1)} %get-tuple-element.41.advanced, f32[1536,128]{1,0:T(8,128)S(1)} %bitcast.6), custom_call_target="tpu_custom_call" | custom-call | tf_op jit(solution)/shard_map/pallas_call | solution.py:581
Async XLA Ops:
  0.6 1.7 %collective-permute-start = (f32[192,128]{1,0:T(8,128)}, f32[192,128]{1,0:T(8,128)S(1)}, u32[]{:S(2)}, u32[]{:S(2)}) collective-permute-start(f32[192,128]{1,0:T(8,128)} %bitcast.7), channel_id=1, source_target_pairs={{0,1},{1,0},{2,3},{3,2},{4,5},{5,4},{6,7},{7,6},{8,9},{9,8},{10,11... | collective-permute-start | bytes 294920 | tf_op jit(solution)/shard_map/ppermute | solution.py:508
  1.1 1.5 %collective-permute-start.1 = (f32[192,128]{1,0:T(8,128)}, f32[192,128]{1,0:T(8,128)S(1)}, u32[]{:S(2)}, u32[]{:S(2)}) collective-permute-start(f32[192,128]{1,0:T(8,128)} %bitcast.9), channel_id=1, source_target_pairs={{0,1},{1,0},{2,3},{3,2},{4,5},{5,4},{6,7},{7,6},{8,9},{9,8},{10,11... | collective-permute-start | bytes 294920 | tf_op jit(solution)/shard_map/ppermute | solution.py:509
  2.7 11.9 %collective-permute-start.2 = (f32[176,128]{1,0:T(8,128)S(1)}, f32[176,128]{1,0:T(8,128)S(1)}, u32[]{:S(2)}, u32[]{:S(2)}) collective-permute-start(f32[176,128]{1,0:T(8,128)S(1)} %get-tuple-element.26), channel_id=1, source_target_pairs={{0,4},{4,8},{8,12},{12,0},{1,5},{5,9},{9,13},{13,1},{2,6},{6,10},{... | collective-permute-start | bytes 270344 | tf_op jit(solution)/shard_map/ppermute | solution.py:495
  5.5 9.1 %collective-permute-start.3 = (f32[176,128]{1,0:T(8,128)S(1)}, f32[176,128]{1,0:T(8,128)S(1)}, u32[]{:S(2)}, u32[]{:S(2)}) collective-permute-start(f32[176,128]{1,0:T(8,128)S(1)} %get-tuple-element.27), channel_id=1, source_target_pairs={{0,12},{4,0},{8,4},{12,8},{1,13},{5,1},{9,5},{13,9},{2,14},{6,2},{... | collective-permute-start | bytes 270344 | tf_op jit(solution)/shard_map/ppermute | solution.py:495
  7.6 7.0 %collective-permute-start.4 = (f32[120,128]{1,0:T(8,128)S(1)}, f32[120,128]{1,0:T(8,128)S(1)}, u32[]{:S(2)}, u32[]{:S(2)}) collective-permute-start(f32[120,128]{1,0:T(8,128)S(1)} %get-tuple-element.28), channel_id=1, source_target_pairs={{0,8},{1,1},{4,12},{5,5},{8,0},{9,9},{12,4},{13,13},{2,10},{3,3},{... | collective-permute-start | bytes 184328 | tf_op jit(solution)/shard_map/ppermute | solution.py:522
  10.5 1.1 %copy-start = (f32[8,3,8,8,128]{4,3,2,1,0:T(8,128)S(1)}, f32[8,3,8,8,128]{4,3,2,1,0:T(8,128)}, u32[]{:S(2)}) copy-start(f32[8,3,8,8,128]{4,3,2,1,0:T(8,128)} %param.7) | copy-start | bytes 2359300
  12.0 7.1 %copy-start.1 = (f32[8,3,8,8,128]{4,3,2,1,0:T(8,128)S(1)}, f32[8,3,8,8,128]{4,3,2,1,0:T(8,128)}, u32[]{:S(2)}) copy-start(f32[8,3,8,8,128]{4,3,2,1,0:T(8,128)} %param.7) | copy-start | bytes 2359300
  14.9 4.2 %collective-permute-start.5 = (f32[96,128]{1,0:T(8,128)S(1)}, f32[96,128]{1,0:T(8,128)S(1)}, u32[]{:S(2)}, u32[]{:S(2)}) collective-permute-start(f32[96,128]{1,0:T(8,128)S(1)} %get-tuple-element.37.strip), channel_id=1, source_target_pairs={{0,2},{2,0},{1,3},{3,1},{4,6},{6,4},{5,7},{7,5},{8,10},{10,8},{9,1... | collective-permute-start | bytes 147464 | tf_op jit(solution)/shard_map/ppermute | solution.py:563

commit v5 on v3

--- a/solution.py
+++ b/solution.py
@@ -218,18 +218,11 @@
     return pulls + (keep, mix, turn)
 
 
-def stage_kernel(
-    many, below, above, behind, walls, strip, *rest
-):
+def stage_kernel(many, below, above, behind, walls, strip, *rest):
     others = rest[: 2 if many else 1]
-    (cells, basis, gram, message, advanced, first, second, edge_low, edge_high) = rest[len(others) :]
-    top = lax.axis_index("row")
-    low_half = top == 0
-    place = lax.axis_index("gz")
-    has_low = place > 0
-    has_high = place < lax.axis_size("gz") - 1
-    lane = lanes(sub)
-    slot, inside = lane // 8, lane % 8
+    cells, basis, gram, message, advanced, first, second, edge_low, edge_high = rest[len(others) :]
+    has_high = lax.axis_index("gz") < lax.axis_size("gz") - 1
+    inside = lanes(sub) % 8
     mine = [strip[pl.ds(sub * c, sub), :] for c in range(6)]
     if many:
         from_low = [others[0][pl.ds(sub * c, sub), :] for c in range(6)]
@@ -241,6 +234,28 @@
     else:
         other = [others[0][pl.ds(sub * c, sub), :] for c in range(6)]
         strips = [[jnp.where((inside < 4) == has_high, a, b) for a, b in zip(mine, other)]]
+    strips = [line + [ahead(line[0], 1, 16)] for line in strips]
+    low_half = lax.axis_index("row") == 0
+    ghosts = [jnp.where(low_half, signs[c] * layer(behind, 0, 12 + c), 0.0) for c in range(3)]
+    lows = [layer(below, 0, 12 + c) for c in range(3)]
+    highs = [layer(above, 0, 12 + c) for c in range(3)]
+    march(
+        strips, ghosts, lows, highs, walls, cells, basis, gram, message, advanced,
+        first, second, edge_low, edge_high,
+    )
+
+
+def march(
+    strips, ghosts, lows, highs, walls, cells, basis, gram, message, advanced,
+    first, second, edge_low, edge_high,
+):
+    top = lax.axis_index("row")
+    low_half = top == 0
+    place = lax.axis_index("gz")
+    has_low = place > 0
+    has_high = place < lax.axis_size("gz") - 1
+    lane = lanes(sub)
+    slot = lane // 8
 
     number = (slot - 2).astype(jnp.float32) + top.astype(jnp.float32) * 8.0 + 0.5
     inverse = 1.0 / number
@@ -270,8 +285,8 @@
     levels = []
     flows = []
     for line in strips:
-        factor = ahead(line[0], 1, 16)
-        flow = walled(line[3:], wall_signs)
+        factor = line[6]
+        flow = walled(line[3:6], wall_signs)
         flows.append(flow)
         table = coefficients_of(flow, strip_sides(flow), *strip_scalars)
         start = walled(line[:3], [factor] * 3)
@@ -370,13 +385,12 @@
         for c in range(3):
             first[pl.ds(row_of(c, w), sub), :] = center[c] + change[c]
     for c in range(3):
-        rows = pl.ds(8 * (12 + c), 8)
         low = pl.ds(row_of(c, 1), 8)
-        first[low, :] = first[low, :] + jnp.where(low_half, signs[c] * behind[rows, :], 0.0)
+        first[low, :] = first[low, :] + ghosts[c]
         before = pl.ds(row_of(c, 3) + 14, 8, stride=sub)
         after = pl.ds(row_of(c, 3) + 9, 8, stride=sub)
-        first[before, :] = first[before, :] + below[rows, :]
-        first[after, :] = first[after, :] + above[rows, :]
+        first[before, :] = first[before, :] + lows[c]
+        first[after, :] = first[after, :] + highs[c]
 
     def close_wall(source):
         for c in range(3):
@@ -414,6 +428,267 @@
         message[device] = line
 
 
+side_wall = 16 * tiles
+side_strip = side_wall + 8
+side_axis = side_strip + 16
+side_length = side_axis + 24
+diagonal_wall = 24
+diagonal_length = 32
+share_corner = 8 * tiles
+share_rest = share_corner + 24
+share_turn = share_rest + side_length - side_wall
+share_diagonal = share_turn + 8 * tiles
+share_length = share_diagonal + diagonal_length
+
+
+def faces_up():
+    return (lax.axis_index("phi") + lax.axis_index("row")) % 2 == 0
+
+
+def load_kernel(conductance, region, field, velocity, reflect, field_copy, flow_copy):
+    kinds = region[...]
+    value = jnp.zeros(kinds.shape, jnp.float32)
+    for kind in range(conductance.shape[0]):
+        value = jnp.where(kinds == kind, conductance[kind], value)
+    reflect[...] = 1.0 - 2.0 * value / (1.0 + value)
+    field_copy[...] = field[...]
+    flow_copy[...] = velocity[...]
+
+
+def send_kernel(field, velocity, far_field, far_flow, reflect, side, turn, diagonal, strip):
+    top = lax.axis_index("row")
+    upper = faces_up()
+    slot = lanes(8) // 8
+
+    def facing(load, depth):
+        return jnp.where(upper, load(8 - depth), load(depth - 1))
+
+    def column(source, c, depth):
+        return facing(lambda q: source[pl.ds(c * 64 + q, 8, stride=8), :], depth)
+
+    direction = jnp.where(upper, -1.0, 1.0)
+    index = lax.broadcasted_iota(jnp.int32, (8, 128), 0).astype(jnp.float32)
+    for source, flow, half in ((field, velocity, top), (far_field, far_flow, 1 - top)):
+        base = half * (8 * tiles)
+
+        def put(tile, value):
+            side[pl.ds(pl.multiple_of(base + 8 * tile, 8), 8), :] = value
+
+        bend = (diffuse * direction) / (index + (half.astype(jnp.float32) * 8.0 + 0.5))
+        near_two = [column(source, c, 2) for c in range(3)]
+        flow_two = [column(flow, c, 2) for c in range(3)]
+        distant = [column(source, c, 3) for c in range(3)]
+        carry = diffuse + advect * jnp.maximum(-direction * flow_two[1], 0.0)
+        stretch = (0.5 * advect * direction) * near_two[1]
+        term = [carry * distant[c] + stretch * column(flow, c, 3) for c in range(3)]
+        term[0] = term[0] - bend * distant[1]
+        term[1] = term[1] + bend * distant[0]
+        for c in range(3):
+            put(c, column(source, c, 1))
+            put(3 + c, column(flow, c, 1))
+            put(6 + c, near_two[c])
+            put(9 + c, flow_two[c])
+            put(12 + c, term[c])
+    for depth in (1, 2):
+        wall = facing(lambda q: reflect[pl.ds(q, 1), :], depth)
+        side[pl.ds(side_wall + depth - 1, 1), :] = wall
+        diagonal[pl.ds(diagonal_wall + depth - 1, 1), :] = wall
+
+    for c in range(6):
+        own, far = (field, far_field) if c < 3 else (velocity, far_flow)
+        parts = []
+        for source in (own, far):
+            part = jnp.zeros((8, 128), jnp.float32)
+            for r in range(8):
+                part = jnp.where(
+                    slot == r, pltpu.roll(layer(source, c % 3, r), (8 * r + 4) % 128, 1), part
+                )
+            parts.append(part)
+        low = jnp.where(top == 0, parts[0], parts[1])
+        high = jnp.where(top == 0, parts[1], parts[0])
+        strip[pl.ds(8 * c, 8), :] = jnp.where(slot < 8, low, pltpu.roll(high, 64, 1))
+    for depth in (1, 2):
+        edge = facing(lambda q: strip[pl.ds(q, 6, stride=8), :], depth)
+        side[pl.ds(side_strip + 8 * (depth - 1), 6), :] = edge
+        diagonal[pl.ds(8 * (depth - 1), 6), :] = edge
+    diagonal[pl.ds(16, 6), :] = jnp.where(
+        upper, strip[pl.ds(0, 6, stride=8), :], strip[pl.ds(7, 6, stride=8), :]
+    )
+
+    def inner_cell(own, far, start, count, step):
+        rows = pl.ds(start, count, stride=step)
+        return jnp.where(top == 0, own[rows, :], far[rows, :])
+
+    for place, (r, depth) in enumerate(((0, 1), (0, 2), (1, 1))):
+        for part, (own, far) in enumerate(((field, far_field), (velocity, far_flow))):
+            side[pl.ds(side_axis + 8 * place + 3 * part, 3), :] = jnp.where(
+                upper,
+                inner_cell(own, far, r * 8 + depth - 1, 3, 64),
+                inner_cell(own, far, r * 8 + 8 - depth, 3, 64),
+            )
+    carry = (diffuse * 2.0 / 1.5) - advect * jnp.minimum(layer(far_flow, 0, 1), 0.0)
+    stretch = (0.5 * advect) * layer(far_field, 0, 1)
+    content = []
+    for r in range(2):
+        content += [layer(far_field, c, r) for c in range(3)]
+        content += [layer(far_flow, c, r) for c in range(3)]
+    content += [
+        carry * layer(far_field, c, 2) + stretch * layer(far_flow, c, 2) for c in range(3)
+    ]
+    for tile in range(tiles):
+        value = content[tile]
+        if tile < 6:
+            value = jnp.where(top == 0, strip[pl.ds(8 * tile, 8), :], value)
+        elif tile == 6:
+            value = jnp.where(top == 0, reflect[...], value)
+        turn[pl.ds(8 * tile, 8), :] = value
+
+
+def other_corner(side, first, step):
+    top = lax.axis_index("row")
+    low = side[pl.ds(8 * tiles + first + step, 6, stride=8), :]
+    high = side[pl.ds(first + 7 - step, 6, stride=8), :]
+    return jnp.where(top == 0, low, high)
+
+
+def share_kernel(side, turn, diagonal, out):
+    top = lax.axis_index("row")
+    half = pl.multiple_of((1 - top) * (8 * tiles), 8)
+    out[pl.ds(0, 8 * tiles), :] = side[pl.ds(half, 8 * tiles), :]
+    for place, (first, step) in enumerate(((0, 0), (48, 0), (0, 1))):
+        low = side[pl.ds(first + 7 - step, 6, stride=8), :]
+        high = side[pl.ds(8 * tiles + first + step, 6, stride=8), :]
+        out[pl.ds(share_corner + 8 * place, 6), :] = jnp.where(top == 0, low, high)
+    out[pl.ds(share_rest, side_length - side_wall), :] = side[
+        pl.ds(side_wall, side_length - side_wall), :
+    ]
+    out[pl.ds(share_turn, 8 * tiles), :] = turn[...]
+    out[pl.ds(share_diagonal, diagonal_length), :] = diagonal[...]
+
+
+def compact_kernel(
+    field, velocity, far_field, far_flow, reflect, strip, side, turn, diagonal, opposite, shared,
+    basis, gram, message, advanced, cells, walls, line, first, second, edge_low, edge_high,
+):
+    top = lax.axis_index("row")
+    low_half = top == 0
+    upper = faces_up()
+    mine_low = lax.axis_index("gz") == 0
+
+    def both(own, other):
+        return jnp.where(upper, other, own), jnp.where(upper, own, other)
+
+    own_half = pl.multiple_of(top * (8 * tiles), 8)
+
+    def tile_pair(tile):
+        return both(
+            side[pl.ds(pl.multiple_of(own_half + 8 * tile, 8), 8), :], shared[pl.ds(8 * tile, 8), :]
+        )
+
+    def rest_pair(start, count):
+        return both(
+            side[pl.ds(start, count), :], shared[pl.ds(share_rest + start - side_wall, count), :]
+        )
+
+    def diagonal_pair(start, count):
+        return both(
+            diagonal[pl.ds(start, count), :], shared[pl.ds(share_diagonal + start, count), :]
+        )
+
+    behind = [shared[pl.ds(share_turn + 8 * tile, 8), :] for tile in range(tiles)]
+    nothing = jnp.zeros((8, 128), jnp.float32)
+    for c in range(6):
+        source, far = (field, far_field) if c < 3 else (velocity, far_flow)
+        sign = signs[c % 3]
+        for r in range(8):
+            cells[pl.ds(row_of(c, r + 3), 8), :] = layer(source, c % 3, r)
+        for w in range(window):
+            cells[pl.ds(row_of(c, w) + 8, 8), :] = nothing
+        for w in range(3):
+            ghost = sign * behind[6 * (2 - w) + c] if w > 0 else 0.0
+            cells[pl.ds(row_of(c, w), 8), :] = jnp.where(low_half, ghost, layer(far, c % 3, 5 + w))
+            cells[pl.ds(row_of(c, 11 + w), 8), :] = jnp.where(low_half, layer(far, c % 3, w), 0.0)
+        for depth in range(2):
+            below, above = tile_pair(6 * depth + c)
+            cells[pl.ds(row_of(c, 3) + 15 - depth, 8, stride=sub), :] = below
+            cells[pl.ds(row_of(c, 3) + 8 + depth, 8, stride=sub), :] = above
+    flip = lax.broadcasted_iota(jnp.int32, (6, 128), 0)
+    flip = jnp.where((flip == 2) | (flip == 5), 1.0, -1.0)
+    for place, (w, first_row, step, depth) in enumerate(((2, 0, 0, 0), (2, 48, 0, 1), (1, 0, 1, 0))):
+        axis_high, axis_low = rest_pair(side_axis + 8 * place, 6)
+        below, above = both(
+            other_corner(side, first_row, step), shared[pl.ds(share_corner + 8 * place, 6), :]
+        )
+        for axis_part, other, q in ((axis_low, below, 15 - depth), (axis_high, above, 8 + depth)):
+            low = pl.ds(row_of(0, w) + q, 6, stride=window * sub)
+            high = pl.ds(row_of(0, 13 - w) + q, 6, stride=window * sub)
+            cells[low, :] = jnp.where(low_half, flip * axis_part, other)
+            cells[high, :] = jnp.where(low_half, other, 0.0)
+
+    slot, inside = lanes(sub) // 8, lanes(sub) % 8
+    axial_turn = [
+        jnp.where(
+            low_half, turn[pl.ds(8 * tile, 8), :], shared[pl.ds(share_turn + 8 * tile, 8), :]
+        )
+        for tile in range(7)
+    ]
+    own_side = (inside < 4) == mine_low
+
+    def merge(own, other):
+        return jnp.where(own_side[: own.shape[0]], own, other)
+
+    for part, (tile, pair) in enumerate(
+        ((reflect[...], rest_pair(side_wall, 2)), (axial_turn[6], diagonal_pair(diagonal_wall, 2)))
+    ):
+        below, above = pair
+        base = sub * part
+        walls[pl.ds(base, 8), :] = tile
+        walls[pl.ds(base + 8, 8), :] = nothing
+        walls[pl.ds(base + 8, 2), :] = above
+        walls[pl.ds(base + 15, 1), :] = below[0:1]
+        walls[pl.ds(base + 14, 1), :] = below[1:2]
+    factor = merge(
+        pltpu.roll(walls[pl.ds(0, sub), :], 84, 1), pltpu.roll(walls[pl.ds(sub, sub), :], 84, 1)
+    )
+
+    for c in range(6):
+        own = strip[pl.ds(8 * c, 8), :]
+        line[pl.ds(sub * c, 8), :] = merge(own, axial_turn[c])
+        line[pl.ds(sub * c + 8, 8), :] = nothing
+    for depth in (1, 2):
+        below, above = rest_pair(side_strip + 8 * (depth - 1), 6)
+        beyond_below, beyond_above = diagonal_pair(8 * (depth - 1), 6)
+        line[pl.ds(16 - depth, 6, stride=sub), :] = merge(below, beyond_below)
+        line[pl.ds(7 + depth, 6, stride=sub), :] = merge(above, beyond_above)
+    axis_high, axis_low = diagonal_pair(16, 6)
+    combined = []
+    for c in range(6):
+        value = line[pl.ds(sub * c, sub), :]
+        combined.append(jnp.where(low_half, pltpu.roll(value, 16, 1), pltpu.roll(value, 80, 1)))
+    for c in range(6):
+        sign = signs[c % 3]
+        across = opposite[pl.ds(8 * c, 8), :]
+        own = jnp.where(
+            slot[:8] == 1,
+            pltpu.roll(behind[c], 12, 1),
+            pltpu.roll(behind[6 + c], 4, 1),
+        )
+        other = jnp.where(slot[:8] == 1, pltpu.roll(across, 8, 1), pltpu.roll(across, 120, 1))
+        line[pl.ds(sub * c, 8), :] = sign * merge(own, other)
+        line[pl.ds(sub * c + 8, 8), :] = nothing
+        line[pl.ds(sub * c + 8, 1), :] = sign * pltpu.roll(axis_high, 8, 1)[c : c + 1]
+        line[pl.ds(sub * c + 15, 1), :] = sign * pltpu.roll(axis_low, 8, 1)[c : c + 1]
+        ghost = line[pl.ds(sub * c, sub), :]
+        combined[c] = jnp.where(jnp.logical_and(slot < 2, low_half), ghost, combined[c])
+    combined.append(factor)
+    ghosts = [jnp.where(low_half, signs[c] * behind[12 + c], 0.0) for c in range(3)]
+    lows, highs = zip(*[tile_pair(12 + c) for c in range(3)])
+    march(
+        [combined], ghosts, lows, highs, walls.at[pl.ds(0, sub), :], cells, basis, gram, message,
+        advanced, first, second, edge_low, edge_high,
+    )
+
+
 def gram_place(m, n):
     return 16 + m * (m + 1) // 2 + n
 
@@ -471,7 +746,16 @@
     return lax.ppermute(value, axis, [(i, (i + step) % count) for i in range(count)])
 
 
-def local(field, velocity, basis, wall_region, wall_conductance):
+def march_scratch():
+    return [
+        shape(3 * window * sub, 128),
+        shape(3 * window * sub, 128),
+        shape(3 * sub, 128),
+        shape(3 * sub, 128),
+    ]
+
+
+def general_plan(field, velocity, basis, wall_region, wall_conductance):
     loop = lax.axis_size("phi")
     ends = lax.axis_size("gz")
     halves = lax.axis_size("row")
@@ -532,20 +816,94 @@
     else:
         others = [lax.ppermute(strip, "gz", swap)]
     walls, strip, cells, *others = near(walls, strip, cells, *others)
-    axes = ("phi", "gz", "row")
-    devices = lax.axis_size(axes)
-    message, advanced = pl.pallas_call(
+    devices = lax.axis_size(("phi", "gz", "row"))
+    return pl.pallas_call(
         functools.partial(stage_kernel, many),
         in_specs=vmem(8 + len(others)),
         out_specs=vmem(2),
         out_shape=[shape(devices, 1, 128), shape(192, 128)],
+        scratch_shapes=march_scratch(),
+    )(below, above, behind, walls, strip, *others, cells, basis_rows, gram)
+
+
+def compact_plan(field, velocity, basis, wall_region, wall_conductance):
+    vectors = basis.shape[0]
+    field_rows = field.reshape(192, 128)
+    flow_rows = velocity.reshape(192, 128)
+    axes = ("phi", "gz", "row")
+    devices = lax.axis_size(axes)
+
+    def exchange(value, partner):
+        pairs = []
+        for p in range(4):
+            for g in range(2):
+                for r in range(2):
+                    q, h = partner(p, g, r)
+                    pairs.append(((p * 2 + g) * 2 + r, (q % 4 * 2 + h) * 2 + r))
+        return lax.ppermute(value, axes, pairs)
+
+    def beside(p, r):
+        return p + 1 if (p + r) % 2 == 0 else p - 1
+
+    swap = [(0, 1), (1, 0)]
+    far_field = lax.ppermute(field_rows, "row", swap)
+    far_flow = lax.ppermute(flow_rows, "row", swap)
+    reflect, field_rows, flow_rows = pl.pallas_call(
+        load_kernel,
+        in_specs=[pl.BlockSpec(memory_space=pltpu.SMEM)] + vmem(3),
+        out_specs=vmem(3),
+        out_shape=[shape(8, 128), shape(192, 128), shape(192, 128)],
+    )(wall_conductance, wall_region, field_rows, flow_rows)
+    blocks = near(field_rows, flow_rows, far_field, far_flow, reflect)
+    side, turn, diagonal, strip = pl.pallas_call(
+        send_kernel,
+        in_specs=vmem(5),
+        out_specs=vmem(4),
+        out_shape=[
+            shape(side_length, 128),
+            shape(8 * tiles, 128),
+            shape(diagonal_length, 128),
+            shape(48, 128),
+        ],
+    )(*blocks)
+    opposite = exchange(strip, lambda p, g, r: (p + 2, 1 - g))
+    turn = exchange(turn, lambda p, g, r: (p, 1 - g) if r == 0 else (p + 2, g))
+    diagonal = exchange(diagonal, lambda p, g, r: (beside(p, r), 1 - g))
+    side = exchange(side, lambda p, g, r: (beside(p, r), g))
+    (basis_rows,) = near(basis.reshape(vectors * 192, 128))
+    gram = pl.pallas_call(
+        gram_kernel, in_specs=vmem(1), out_specs=vmem(1)[0], out_shape=shape(1, 128)
+    )(basis_rows)
+    side, turn, diagonal, opposite, gram = near(
+        *lax.optimization_barrier((side, turn, diagonal, opposite, gram))
+    )
+    share = pl.pallas_call(
+        share_kernel, in_specs=vmem(3), out_specs=vmem(1)[0], out_shape=shape(share_length, 128)
+    )(side, turn, diagonal)
+    shared = lax.ppermute(share, "row", swap)
+    strip, shared = near(strip, shared)
+    return pl.pallas_call(
+        compact_kernel,
+        in_specs=vmem(13),
+        out_specs=vmem(2),
+        out_shape=[shape(devices, 1, 128), shape(192, 128)],
         scratch_shapes=[
-            pltpu.VMEM((3 * window * sub, 128), jnp.float32),
-            pltpu.VMEM((3 * window * sub, 128), jnp.float32),
-            pltpu.VMEM((3 * sub, 128), jnp.float32),
-            pltpu.VMEM((3 * sub, 128), jnp.float32),
-        ],
-    )(below, above, behind, walls, strip, *others, cells, basis_rows, gram)
+            shape(6 * window * sub, 128),
+            shape(2 * sub, 128),
+            shape(6 * sub, 128),
+        ]
+        + march_scratch(),
+    )(*blocks, strip, side, turn, diagonal, opposite, shared, basis_rows, gram)
+
+
+def local(field, velocity, basis, wall_region, wall_conductance):
+    axes = ("phi", "gz", "row")
+    vectors = basis.shape[0]
+    devices = lax.axis_size(axes)
+    compact = tuple(lax.axis_size(axis) for axis in axes) == (4, 2, 2)
+    plan = compact_plan if compact else general_plan
+    message, advanced = plan(field, velocity, basis, wall_region, wall_conductance)
+    (basis_rows,) = near(basis.reshape(vectors * 192, 128))
     messages = lax.all_to_all(message, axes, 0, 0, tiled=True)
     messages, advanced = near(messages, advanced)
     out, hessenberg = pl.pallas_call(

time: 36.3 us -> 29.3 us (0.81)
  waiting for transfers between devices: 6.6 us -> 3.68 us
  blocking collectives: 11 us -> 8.98 us
  local copies, waits for them, and re-layouts: 2.93 us -> 1.14 us
  Pallas kernels: 4.59 us -> 4.18 us
    ppermute x6 -> x7, waiting for transfers between devices: 6.6 us -> 3.68 us  [the longest x4 2.19 us: exchange(): return lax.ppermute(value, axes, pairs)]
    all_to_all x1, blocking collectives: 11 us -> 8.98 us  [local(): messages = lax.all_to_all(message, axes, 0, 0, tiled=True)]
    unnamed x14 -> x4, local copies, waits for them, and re-layouts: 2.93 us -> 1.14 us
    pallas_call x5, Pallas kernels: 3.73 us -> 3.32 us  [the longest x1 1.7 us: compact_plan(): pl.pallas_call(compact_kernel, in_specs=vmem(13), out_specs=vmem(2), out_...]
    ppermute x6 -> x7, starting transfers between devices: 10.2 us -> 10.5 us  [the longest x4 8.22 us: exchange(): return lax.ppermute(value, axes, pairs)]
  transfers between devices with their start and end apart: 6 -> 7, of which waited for: 4 -> 4; matrix products, arithmetic and copies ran while one was open for 0% -> 0% of each run, Pallas kernels for 1% -> 5%
where the time goes in v5:
time: 29.3 us; the launch traced here: 29.1 us
  starting transfers between devices  10.5 us (36%)
  blocking collectives  8.98 us (31%)
  Pallas kernels  4.18 us (14%)
  waiting for transfers between devices  3.68 us (13%)
  local copies, waits for them, and re-layouts  1.14 us (4%)
  between operations  0.67 us (2%)
    all_to_all x1, blocking collectives, local(): messages = lax.all_to_all(message, axes, 0, 0, tiled=True)  8.98 us
    ppermute x4, starting transfers between devices, exchange(): return lax.ppermute(value, axes, pairs)  8.22 us
    ppermute x4, waiting for transfers between devices, exchange(): return lax.ppermute(value, axes, pairs)  2.19 us
    pallas_call x1, Pallas kernels, compact_plan(): pl.pallas_call(compact_kernel, in_specs=vmem(13), out_specs=vmem(2), out_...  1.7 us
    ppermute x1, starting transfers between devices, compact_plan(): shared = lax.ppermute(share, 'row', swap)  1.65 us
    unnamed x4, local copies, waits for them, and re-layouts  1.14 us
    ppermute x1, waiting for transfers between devices, compact_plan(): shared = lax.ppermute(share, 'row', swap)  1.04 us
    pallas_call x1, Pallas kernels, compact_plan(): pl.pallas_call(load_kernel, in_specs=[pl.BlockSpec(memory_space=pltpu.SME...  0.98 us
  transfers between devices with their start and end apart: 7, of which 4 were waited for; matrix products, arithmetic and copies ran while one was open for 0% of the time, Pallas kernels for 5%

profile of v5, /device:TPU:0, one launch (start us, length us, event | category | flops | bytes accessed | tf_op | source)
XLA Modules:
  0.0 29.1 jit_solution(3864042106642751720)
XLA Ops:
  0.6 0.5 %collective-permute-start = (f32[192,128]{1,0:T(8,128)}, f32[192,128]{1,0:T(8,128)S(1)}, u32[]{:S(2)}, u32[]{:S(2)}) collective-permute-start(f32[192,128]{1,0:T(8,128)} %bitcast.7), channel_id=1, source_target_pairs={{0,1},{1,0},{2,3},{3,2},{4,5},{5,4},{6,7},{7,6},{8,9},{9,8},{10,11... | collective-permute-start | bytes 294920 | tf_op jit(solution)/shard_map/ppermute | solution.py:849
  1.1 0.1 collective-permute-start.1
  1.2 1.0 %shard_map.68 = (f32[8,128]{1,0:T(8,128)S(1)}, f32[192,128]{1,0:T(8,128)S(1)}, f32[192,128]{1,0:T(8,128)S(1)}) custom-call(f32[8]{0:T(128)} %conductance.1, s32[8,128]{1,0:T(8,128)} %region.1, f32[192,128]{1,0:T(8,128)} %bitcast.8, f32[192,128]{1,0:T(8,128)} %bitcast.10), custom_call_target="tpu_custom_call" | custom-call | tf_op jit(solution)/shard_map/pallas_call | solution.py:851
  2.2 0.1 collective-permute-done.far_field
  2.3 0.4 %collective-permute-done.1.far_flow = f32[192,128]{1,0:T(8,128)S(1)} collective-permute-done((f32[192,128]{1,0:T(8,128)}, f32[192,128]{1,0:T(8,128)S(1)}, u32[]{:S(2)}, u32[]{:S(2)}) %collective-permute-start.1) | collective-permute-done | bytes 98336 | tf_op jit(solution)/shard_map/ppermute | solution.py:850
  2.7 0.3 shard_map.69
  2.9 2.8 %collective-permute-start.2 = (f32[288,128]{1,0:T(8,128)S(1)}, f32[288,128]{1,0:T(8,128)S(1)}, u32[]{:S(2)}, u32[]{:S(2)}) collective-permute-start(f32[288,128]{1,0:T(8,128)S(1)} %get-tuple-element.22), channel_id=1, source_target_pairs={{0,4},{1,13},{2,6},{3,15},{4,0},{5,9},{6,2},{7,11},{8,12},{9,5},{1... | collective-permute-start | bytes 442376 | tf_op jit(solution)/shard_map/ppermute | solution.py:843
  5.7 1.5 %collective-permute-start.3 = (f32[120,128]{1,0:T(8,128)S(1)}, f32[120,128]{1,0:T(8,128)S(1)}, u32[]{:S(2)}, u32[]{:S(2)}) collective-permute-start(f32[120,128]{1,0:T(8,128)S(1)} %get-tuple-element.23), channel_id=1, source_target_pairs={{0,2},{1,9},{2,0},{3,11},{4,6},{5,13},{6,4},{7,15},{8,10},{9,1},{1... | collective-permute-start | bytes 184328 | tf_op jit(solution)/shard_map/ppermute | solution.py:843
  7.2 2.6 %collective-permute-start.5 = (f32[48,128]{1,0:T(8,128)S(1)}, f32[48,128]{1,0:T(8,128)S(1)}, u32[]{:S(2)}, u32[]{:S(2)}) collective-permute-start(f32[48,128]{1,0:T(8,128)S(1)} %get-tuple-element.21.strip), channel_id=1, source_target_pairs={{0,10},{1,11},{2,8},{3,9},{4,14},{5,15},{6,12},{7,13},{8,2},{9,3},... | collective-permute-start | bytes 73736 | tf_op jit(solution)/shard_map/ppermute | solution.py:843
  9.8 1.4 %collective-permute-start.4 = (f32[32,128]{1,0:T(8,128)S(1)}, f32[32,128]{1,0:T(8,128)S(1)}, u32[]{:S(2)}, u32[]{:S(2)}) collective-permute-start(f32[32,128]{1,0:T(8,128)S(1)} %get-tuple-element.24), channel_id=1, source_target_pairs={{0,6},{1,15},{2,4},{3,13},{4,2},{5,11},{6,0},{7,9},{8,14},{9,7},{1... | collective-permute-start | bytes 49160 | tf_op jit(solution)/shard_map/ppermute | solution.py:843
  11.1 0.0 copy-start
  11.1 1.1 %copy-done = f32[8,3,8,8,128]{4,3,2,1,0:T(8,128)S(1)} copy-done((f32[8,3,8,8,128]{4,3,2,1,0:T(8,128)S(1)}, f32[8,3,8,8,128]{4,3,2,1,0:T(8,128)}, u32[]{:S(2)}) %copy-start) | copy-done | bytes 786456
  12.3 0.0 copy-start.1
  12.3 0.4 %shard_map.70.gram = f32[1,128]{1,0:T(1,128)S(1)} custom-call(f32[1536,128]{1,0:T(8,128)S(1)} %bitcast.4), custom_call_target="tpu_custom_call" | custom-call | tf_op jit(solution)/shard_map/pallas_call | solution.py:874
  12.6 2.2 %collective-permute-done.4.diagonal = f32[32,128]{1,0:T(8,128)S(1)} collective-permute-done((f32[32,128]{1,0:T(8,128)S(1)}, f32[32,128]{1,0:T(8,128)S(1)}, u32[]{:S(2)}, u32[]{:S(2)}) %collective-permute-start.4) | collective-permute-done | bytes 16416 | tf_op jit(solution)/shard_map/ppermute | solution.py:843
  14.8 0.0 collective-permute-done.5.opposite
  14.8 0.0 collective-permute-done.3.turn
  14.8 0.0 collective-permute-done.2.side
  14.8 1.7 %collective-permute-start.6 = (f32[344,128]{1,0:T(8,128)S(1)}, f32[344,128]{1,0:T(8,128)S(1)}, u32[]{:S(2)}, u32[]{:S(2)}) collective-permute-start(f32[344,128]{1,0:T(8,128)S(1)} %shard_map.71), channel_id=1, source_target_pairs={{0,1},{1,0},{2,3},{3,2},{4,5},{5,4},{6,7},{7,6},{8,9},{9,8},{10,11... | collective-permute-start | bytes 528392 | tf_op jit(solution)/shard_map/ppermute | solution.py:883
  16.5 1.0 %collective-permute-done.6.shared = f32[344,128]{1,0:T(8,128)S(1)} collective-permute-done((f32[344,128]{1,0:T(8,128)S(1)}, f32[344,128]{1,0:T(8,128)S(1)}, u32[]{:S(2)}, u32[]{:S(2)}) %collective-permute-start.6) | collective-permute-done | bytes 176160 | tf_op jit(solution)/shard_map/ppermute | solution.py:883
  17.5 0.0 copy-done.1
  17.5 1.7 %shard_map.72 = (f32[16,1,128]{2,1,0:T(1,128)S(1)}, f32[192,128]{1,0:T(8,128)S(1)}) custom-call(f32[192,128]{1,0:T(8,128)S(1)} %get-tuple-element.18.field, f32[192,128]{1,0:T(8,128)S(1)} %get-tuple-element.19.velocity, f32[192,128]{1,0:T(8,128)S(1)} %collective-permute-done.far_field, f32[192,128]{1,0:T(8,128)S(1)} %collective-permute-done.1.far_flow, ...), custom_call_target="tpu_custom_call" | custom-call | tf_op jit(solution)/shard_map/pallas_call | solution.py:885
  19.3 9.0 %all_to_all.5.messages = f32[16,1,128]{2,1,0:T(1,128)S(1)} all-to-all(f32[16,1,128]{2,1,0:T(1,128)S(1)} %get-tuple-element.30), channel_id=1, replica_groups=mesh['groups'=2,'phi'=4,'gz'=2,'row'=2] {'phi','gz','row'}, dimensions={0} | all-to-all | bytes 16384 | tf_op jit(solution)/shard_map/all_to_all | solution.py:907
  28.2 0.9 %shard_map.73 = (f32[192,128]{1,0:T(8,128)}, f32[9]{0:T(128)}) custom-call(f32[16,1,128]{2,1,0:T(1,128)S(1)} %all_to_all.5.messages, f32[192,128]{1,0:T(8,128)S(1)} %get-tuple-element.31.advanced, f32[1536,128]{1,0:T(8,128)S(1)} %bitcast.6), custom_call_target="tpu_custom_call" | custom-call | tf_op jit(solution)/shard_map/pallas_call | solution.py:909
  (1 shorter events, 0.0 us)
Async XLA Ops:
  0.6 1.7 %collective-permute-start = (f32[192,128]{1,0:T(8,128)}, f32[192,128]{1,0:T(8,128)S(1)}, u32[]{:S(2)}, u32[]{:S(2)}) collective-permute-start(f32[192,128]{1,0:T(8,128)} %bitcast.7), channel_id=1, source_target_pairs={{0,1},{1,0},{2,3},{3,2},{4,5},{5,4},{6,7},{7,6},{8,9},{9,8},{10,11... | collective-permute-start | bytes 294920 | tf_op jit(solution)/shard_map/ppermute | solution.py:849
  1.1 1.5 %collective-permute-start.1 = (f32[192,128]{1,0:T(8,128)}, f32[192,128]{1,0:T(8,128)S(1)}, u32[]{:S(2)}, u32[]{:S(2)}) collective-permute-start(f32[192,128]{1,0:T(8,128)} %bitcast.9), channel_id=1, source_target_pairs={{0,1},{1,0},{2,3},{3,2},{4,5},{5,4},{6,7},{7,6},{8,9},{9,8},{10,11... | collective-permute-start | bytes 294920 | tf_op jit(solution)/shard_map/ppermute | solution.py:850
  2.9 11.9 %collective-permute-start.2 = (f32[288,128]{1,0:T(8,128)S(1)}, f32[288,128]{1,0:T(8,128)S(1)}, u32[]{:S(2)}, u32[]{:S(2)}) collective-permute-start(f32[288,128]{1,0:T(8,128)S(1)} %get-tuple-element.22), channel_id=1, source_target_pairs={{0,4},{1,13},{2,6},{3,15},{4,0},{5,9},{6,2},{7,11},{8,12},{9,5},{1... | collective-permute-start | bytes 442376 | tf_op jit(solution)/shard_map/ppermute | solution.py:843
  5.7 9.1 %collective-permute-start.3 = (f32[120,128]{1,0:T(8,128)S(1)}, f32[120,128]{1,0:T(8,128)S(1)}, u32[]{:S(2)}, u32[]{:S(2)}) collective-permute-start(f32[120,128]{1,0:T(8,128)S(1)} %get-tuple-element.23), channel_id=1, source_target_pairs={{0,2},{1,9},{2,0},{3,11},{4,6},{5,13},{6,4},{7,15},{8,10},{9,1},{1... | collective-permute-start | bytes 184328 | tf_op jit(solution)/shard_map/ppermute | solution.py:843
  7.2 7.6 %collective-permute-start.5 = (f32[48,128]{1,0:T(8,128)S(1)}, f32[48,128]{1,0:T(8,128)S(1)}, u32[]{:S(2)}, u32[]{:S(2)}) collective-permute-start(f32[48,128]{1,0:T(8,128)S(1)} %get-tuple-element.21.strip), channel_id=1, source_target_pairs={{0,10},{1,11},{2,8},{3,9},{4,14},{5,15},{6,12},{7,13},{8,2},{9,3},... | collective-permute-start | bytes 73736 | tf_op jit(solution)/shard_map/ppermute | solution.py:843
  9.8 5.0 %collective-permute-start.4 = (f32[32,128]{1,0:T(8,128)S(1)}, f32[32,128]{1,0:T(8,128)S(1)}, u32[]{:S(2)}, u32[]{:S(2)}) collective-permute-start(f32[32,128]{1,0:T(8,128)S(1)} %get-tuple-element.24), channel_id=1, source_target_pairs={{0,6},{1,15},{2,4},{3,13},{4,2},{5,11},{6,0},{7,9},{8,14},{9,7},{1... | collective-permute-start | bytes 49160 | tf_op jit(solution)/shard_map/ppermute | solution.py:843
  11.1 1.1 %copy-start = (f32[8,3,8,8,128]{4,3,2,1,0:T(8,128)S(1)}, f32[8,3,8,8,128]{4,3,2,1,0:T(8,128)}, u32[]{:S(2)}) copy-start(f32[8,3,8,8,128]{4,3,2,1,0:T(8,128)} %param.7) | copy-start | bytes 2359300
  12.3 5.3 %copy-start.1 = (f32[8,3,8,8,128]{4,3,2,1,0:T(8,128)S(1)}, f32[8,3,8,8,128]{4,3,2,1,0:T(8,128)}, u32[]{:S(2)}) copy-start(f32[8,3,8,8,128]{4,3,2,1,0:T(8,128)} %param.7) | copy-start | bytes 2359300
  14.8 2.7 %collective-permute-start.6 = (f32[344,128]{1,0:T(8,128)S(1)}, f32[344,128]{1,0:T(8,128)S(1)}, u32[]{:S(2)}, u32[]{:S(2)}) collective-permute-start(f32[344,128]{1,0:T(8,128)S(1)} %shard_map.71), channel_id=1, source_target_pairs={{0,1},{1,0},{2,3},{3,2},{4,5},{5,4},{6,7},{7,6},{8,9},{9,8},{10,11... | collective-permute-start | bytes 528392 | tf_op jit(solution)/shard_map/ppermute | solution.py:883

commit v6 on v5

--- a/solution.py
+++ b/solution.py
@@ -21,6 +21,7 @@
 side_rows = axis_row + 24
 window = 14
 sub = 16
+kinds_of_coefficient = 15
 
 
 def row_of(component, w):
@@ -172,14 +173,13 @@
 
 def rate(center, sides, coefficients):
     inward, outward, before, after, under, over = sides
-    pull_in, pull_out, pull_before, pull_after, pull_under, pull_over, keep, mix, turn = coefficients
+    pull_in, pull_out, pull_before, pull_after, pull_under, pull_over, mix, turn = coefficients
     result = []
     for c in range(3):
         value = (
             (pull_in * inward[c] + pull_out * outward[c])
             + (pull_before * before[c] + pull_after * after[c])
             + (pull_under * under[c] + pull_over * over[c])
-            + keep * center[c]
         )
         for d in range(3):
             value = value + mix[c][d] * center[d]
@@ -212,15 +212,16 @@
                 half * (over[c] - under[c]),
             ]
         )
-    mix[0][0] = mix[0][0] - diffuse * inverse_square
-    mix[1][1] = mix[1][1] - diffuse * inverse_square + bend * radial
+    mix[0][0] = mix[0][0] + (keep - diffuse * inverse_square)
+    mix[1][1] = mix[1][1] + (keep - diffuse * inverse_square) + bend * radial
     mix[1][0] = mix[1][0] - bend * around
-    return pulls + (keep, mix, turn)
+    mix[2][2] = mix[2][2] + keep
+    return pulls + (mix, turn)
 
 
 def stage_kernel(many, below, above, behind, walls, strip, *rest):
     others = rest[: 2 if many else 1]
-    cells, basis, gram, message, advanced, first, second, edge_low, edge_high = rest[len(others) :]
+    cells, basis, gram, message, advanced, first, second, edge, edge_flow, table = rest[len(others) :]
     has_high = lax.axis_index("gz") < lax.axis_size("gz") - 1
     inside = lanes(sub) % 8
     mine = [strip[pl.ds(sub * c, sub), :] for c in range(6)]
@@ -241,13 +242,13 @@
     highs = [layer(above, 0, 12 + c) for c in range(3)]
     march(
         strips, ghosts, lows, highs, walls, cells, basis, gram, message, advanced,
-        first, second, edge_low, edge_high,
+        first, second, edge, edge_flow, table,
     )
 
 
 def march(
     strips, ghosts, lows, highs, walls, cells, basis, gram, message, advanced,
-    first, second, edge_low, edge_high,
+    first, second, edge, edge_flow, table,
 ):
     top = lax.axis_index("row")
     low_half = top == 0
@@ -288,24 +289,30 @@
         factor = line[6]
         flow = walled(line[3:6], wall_signs)
         flows.append(flow)
-        table = coefficients_of(flow, strip_sides(flow), *strip_scalars)
+        weights = coefficients_of(flow, strip_sides(flow), *strip_scalars)
         start = walled(line[:3], [factor] * 3)
-        one = rate(start, strip_sides(start), table)
+        one = rate(start, strip_sides(start), weights)
         one = walled([a + b for a, b in zip(start, one)], [factor] * 3)
-        two = rate(one, strip_sides(one), table)
+        two = rate(one, strip_sides(one), weights)
         two = [0.75 * s + 0.25 * (a + b) for s, a, b in zip(start, one, two)]
         levels.append((start, one, two))
 
-    def store_edges(low_values, high_values):
+    inner_side = lane % 8 < 4
+
+    def store_edges(target, low_values, high_values):
         for c in range(3):
-            edge_low[pl.ds(sub * c, sub), :] = jnp.where(has_low, low_values[c], 0.0)
-            edge_high[pl.ds(sub * c, sub), :] = jnp.where(has_high, high_values[c], 0.0)
-
-    def axial(value, c, w, size):
-        low = pltpu.roll(edge_low[pl.ds(sub * c, size), :], (128 - (8 * (w - 1) + 3)) % 128, 1)
-        high = pltpu.roll(edge_high[pl.ds(sub * c, size), :], (127 - (8 * (w - 1) + 4)) % 128, 1)
+            low = jnp.where(has_low, back(low_values[c], 1), 0.0)
+            high = jnp.where(has_high, ahead(high_values[c], 1), 0.0)
+            target[pl.ds(sub * c, sub), :] = jnp.where(inner_side, high, low)
+
+    def axial(value, source, c, w, start, size):
+        ghost = source[pl.ds(sub * c + start, size), :]
+        ghost = pltpu.roll(ghost, 128 - (8 * (w - 1) + 4), 1)
         at = lane[:size]
-        return jnp.where(at == 0, low, back(value, 1)), jnp.where(at == 127, high, ahead(value, 1))
+        return (
+            jnp.where(at == 0, ghost, back(value, 1)),
+            jnp.where(at == 127, ghost, ahead(value, 1)),
+        )
 
     def pick(low, high):
         return jnp.where(low_half, np.float32(low), np.float32(high))
@@ -326,62 +333,60 @@
             )
         return [pick(a, b) for a, b in zip(*options)]
 
-    def read(source, c, w, size=sub):
-        return source[pl.ds(row_of(c, w), size), :]
+    def read(source, c, w, start=0, size=sub):
+        return source[pl.ds(row_of(c, w) + start, size), :]
 
     for c in range(6):
         last = read(cells, c, 10)
         factor = walls[...] if c < 3 else wall_signs[c - 3]
         cells[pl.ds(row_of(c, 11), sub), :] = jnp.where(low_half, read(cells, c, 11), factor * last)
 
-    flow_low, flow_high = flows[0], flows[-1]
-
-    def flow_table(w, size):
-        speed, sides = [], [[], [], [], [], [], []]
+    def surroundings(source, first_component, ends, w, start, size):
+        center, sides = [], [[], [], [], [], [], []]
         for c in range(3):
-            value = read(cells, 3 + c, w)
-            low = pltpu.roll(jnp.where(has_low, flow_low[c], 0.0), (128 - (8 * (w - 1) + 3)) % 128, 1)
-            high = pltpu.roll(jnp.where(has_high, flow_high[c], 0.0), (127 - (8 * (w - 1) + 4)) % 128, 1)
-            under = jnp.where(lane == 0, low, back(value, 1))
-            over = jnp.where(lane == 127, high, ahead(value, 1))
+            at = first_component + c
+            whole = read(source, at, w)
+            value = whole[:size]
+            under, over = axial(value, ends, c, w, start, size)
             for side, part in zip(
                 sides,
                 (
-                    read(cells, 3 + c, w - 1),
-                    read(cells, 3 + c, w + 1),
-                    back(value, 0),
-                    ahead(value, 0),
-                    under,
-                    over,
-                ),
-            ):
-                side.append(part[:size])
-            speed.append(value[:size])
-        return coefficients_of(speed, sides, *scalars(w))
-
-    def field_rate(source, w, size):
-        center, sides = [], [[], [], [], [], [], []]
-        for c in range(3):
-            value = read(source, c, w)
-            under, over = axial(value[:size], c, w, size)
-            for side, part in zip(
-                sides,
-                (
-                    read(source, c, w - 1, size),
-                    read(source, c, w + 1, size),
-                    back(value, 0)[:size],
-                    ahead(value, 0)[:size],
+                    read(source, at, w - 1, start, size),
+                    read(source, at, w + 1, start, size),
+                    back(whole, 0)[:size],
+                    ahead(whole, 0)[:size],
                     under,
                     over,
                 ),
             ):
                 side.append(part)
-            center.append(value[:size])
-        return center, rate(center, sides, flow_table(w, size))
-
-    store_edges(levels[0][0], levels[-1][0])
+            center.append(value)
+        return center, sides
+
+    def table_rows(kind, w, start, size):
+        return pl.ds((kind * 12 + w - 1) * sub + start, size)
+
+    def make_table(w):
+        weights = coefficients_of(*surroundings(cells, 3, edge_flow, w, 0, sub), *scalars(w))
+        flat = list(weights[:6]) + [value for row in weights[6] for value in row]
+        if w not in (1, 12):
+            for kind, value in enumerate(flat):
+                table[table_rows(kind, w, 0, sub), :] = value
+        return weights
+
+    def stored_table(w, start, size):
+        flat = [table[table_rows(kind, w, start, size), :] for kind in range(kinds_of_coefficient)]
+        mix = [flat[6:9], flat[9:12], flat[12:15]]
+        return tuple(flat[:6]) + (mix, scalars(w)[-1])
+
+    def field_rate(source, w, start=0, size=sub, weights=None):
+        center, sides = surroundings(source, 0, edge, w, start, size)
+        return center, rate(center, sides, weights or stored_table(w, start, size))
+
+    store_edges(edge_flow, flows[0], flows[-1])
+    store_edges(edge, levels[0][0], levels[-1][0])
     for w in range(1, 13):
-        center, change = field_rate(cells, w, sub)
+        center, change = field_rate(cells, w, weights=make_table(w))
         for c in range(3):
             first[pl.ds(row_of(c, w), sub), :] = center[c] + change[c]
     for c in range(3):
@@ -399,22 +404,22 @@
             )
 
     close_wall(first)
-    store_edges(levels[0][1], levels[-1][1])
+    store_edges(edge, levels[0][1], levels[-1][1])
     for w in range(2, 12):
-        center, change = field_rate(first, w, sub)
+        center, change = field_rate(first, w)
         for c in range(3):
             second[pl.ds(row_of(c, w), sub), :] = 0.75 * read(cells, c, w) + 0.25 * (
                 center[c] + change[c]
             )
     close_wall(second)
-    store_edges(levels[0][2], levels[-1][2])
+    store_edges(edge, levels[0][2], levels[-1][2])
     count = basis.shape[0] // 192
     sums = [jnp.zeros((8, 128), jnp.float32) for _ in range(count + 1)]
     for w in range(3, 11):
-        center, change = field_rate(second, w, 8)
+        center, change = field_rate(second, w, 0, 8)
         for c in range(3):
             rows = pl.ds(64 * c + 8 * (w - 3), 8)
-            value = read(cells, c, w, 8) / 3.0 + (2.0 / 3.0) * (center[c] + change[c])
+            value = read(cells, c, w, 0, 8) / 3.0 + (2.0 / 3.0) * (center[c] + change[c])
             advanced[rows, :] = value
             for m in range(count):
                 sums[m] += basis[pl.ds(192 * m + 64 * c + 8 * (w - 3), 8), :] * value
@@ -568,7 +573,7 @@
 
 def compact_kernel(
     field, velocity, far_field, far_flow, reflect, strip, side, turn, diagonal, opposite, shared,
-    basis, gram, message, advanced, cells, walls, line, first, second, edge_low, edge_high,
+    basis, gram, message, advanced, cells, walls, line, first, second, edge, edge_flow, table,
 ):
     top = lax.axis_index("row")
     low_half = top == 0
@@ -685,7 +690,7 @@
     lows, highs = zip(*[tile_pair(12 + c) for c in range(3)])
     march(
         [combined], ghosts, lows, highs, walls.at[pl.ds(0, sub), :], cells, basis, gram, message,
-        advanced, first, second, edge_low, edge_high,
+        advanced, first, second, edge, edge_flow, table,
     )
 
 
@@ -752,6 +757,7 @@
         shape(3 * window * sub, 128),
         shape(3 * sub, 128),
         shape(3 * sub, 128),
+        shape(kinds_of_coefficient * 12 * sub, 128),
     ]
 
 

time: 29.3 us -> 29 us (0.990)
  Pallas kernels: 4.18 us -> 3.83 us
    pallas_call x1, Pallas kernels: 1.7 us -> 1.35 us  [compact_plan(): pl.pallas_call(compact_kernel, in_specs=vmem(13), out_specs=vmem(2), out_...]
where the time goes in v6:
time: 29 us; the launch traced here: 28.8 us
  starting transfers between devices  10.5 us (36%)
  blocking collectives  8.99 us (31%)
  Pallas kernels  3.83 us (13%)
  waiting for transfers between devices  3.68 us (13%)
  local copies, waits for them, and re-layouts  1.14 us (4%)
  between operations  0.67 us (2%)
    all_to_all x1, blocking collectives, local(): messages = lax.all_to_all(message, axes, 0, 0, tiled=True)  8.99 us
    ppermute x4, starting transfers between devices, exchange(): return lax.ppermute(value, axes, pairs)  8.22 us
    ppermute x4, waiting for transfers between devices, exchange(): return lax.ppermute(value, axes, pairs)  2.19 us
    ppermute x1, starting transfers between devices, compact_plan(): shared = lax.ppermute(share, 'row', swap)  1.65 us
    pallas_call x1, Pallas kernels, compact_plan(): pl.pallas_call(compact_kernel, in_specs=vmem(13), out_specs=vmem(2), out_...  1.35 us
    unnamed x4, local copies, waits for them, and re-layouts  1.14 us
    ppermute x1, waiting for transfers between devices, compact_plan(): shared = lax.ppermute(share, 'row', swap)  1.04 us
    pallas_call x1, Pallas kernels, compact_plan(): pl.pallas_call(load_kernel, in_specs=[pl.BlockSpec(memory_space=pltpu.SME...  0.98 us
  transfers between devices with their start and end apart: 7, of which 4 were waited for; matrix products, arithmetic and copies ran while one was open for 0% of the time, Pallas kernels for 5%

profile of v6, /device:TPU:0, one launch (start us, length us, event | category | flops | bytes accessed | tf_op | source)
XLA Modules:
  0.0 28.8 jit_solution(7449978225546813870)
XLA Ops:
  0.6 0.5 %collective-permute-start = (f32[192,128]{1,0:T(8,128)}, f32[192,128]{1,0:T(8,128)S(1)}, u32[]{:S(2)}, u32[]{:S(2)}) collective-permute-start(f32[192,128]{1,0:T(8,128)} %bitcast.7), channel_id=1, source_target_pairs={{0,1},{1,0},{2,3},{3,2},{4,5},{5,4},{6,7},{7,6},{8,9},{9,8},{10,11... | collective-permute-start | bytes 294920 | tf_op jit(solution)/shard_map/ppermute | solution.py:855
  1.1 0.1 collective-permute-start.1
  1.2 1.0 %shard_map.68 = (f32[8,128]{1,0:T(8,128)S(1)}, f32[192,128]{1,0:T(8,128)S(1)}, f32[192,128]{1,0:T(8,128)S(1)}) custom-call(f32[8]{0:T(128)} %conductance.1, s32[8,128]{1,0:T(8,128)} %region.1, f32[192,128]{1,0:T(8,128)} %bitcast.8, f32[192,128]{1,0:T(8,128)} %bitcast.10), custom_call_target="tpu_custom_call" | custom-call | tf_op jit(solution)/shard_map/pallas_call | solution.py:857
  2.2 0.1 collective-permute-done.far_field
  2.3 0.4 %collective-permute-done.1.far_flow = f32[192,128]{1,0:T(8,128)S(1)} collective-permute-done((f32[192,128]{1,0:T(8,128)}, f32[192,128]{1,0:T(8,128)S(1)}, u32[]{:S(2)}, u32[]{:S(2)}) %collective-permute-start.1) | collective-permute-done | bytes 98336 | tf_op jit(solution)/shard_map/ppermute | solution.py:856
  2.7 0.3 shard_map.69
  2.9 2.8 %collective-permute-start.2 = (f32[288,128]{1,0:T(8,128)S(1)}, f32[288,128]{1,0:T(8,128)S(1)}, u32[]{:S(2)}, u32[]{:S(2)}) collective-permute-start(f32[288,128]{1,0:T(8,128)S(1)} %get-tuple-element.22), channel_id=1, source_target_pairs={{0,4},{1,13},{2,6},{3,15},{4,0},{5,9},{6,2},{7,11},{8,12},{9,5},{1... | collective-permute-start | bytes 442376 | tf_op jit(solution)/shard_map/ppermute | solution.py:849
  5.7 1.5 %collective-permute-start.3 = (f32[120,128]{1,0:T(8,128)S(1)}, f32[120,128]{1,0:T(8,128)S(1)}, u32[]{:S(2)}, u32[]{:S(2)}) collective-permute-start(f32[120,128]{1,0:T(8,128)S(1)} %get-tuple-element.23), channel_id=1, source_target_pairs={{0,2},{1,9},{2,0},{3,11},{4,6},{5,13},{6,4},{7,15},{8,10},{9,1},{1... | collective-permute-start | bytes 184328 | tf_op jit(solution)/shard_map/ppermute | solution.py:849
  7.2 2.6 %collective-permute-start.5 = (f32[48,128]{1,0:T(8,128)S(1)}, f32[48,128]{1,0:T(8,128)S(1)}, u32[]{:S(2)}, u32[]{:S(2)}) collective-permute-start(f32[48,128]{1,0:T(8,128)S(1)} %get-tuple-element.21.strip), channel_id=1, source_target_pairs={{0,10},{1,11},{2,8},{3,9},{4,14},{5,15},{6,12},{7,13},{8,2},{9,3},... | collective-permute-start | bytes 73736 | tf_op jit(solution)/shard_map/ppermute | solution.py:849
  9.8 1.4 %collective-permute-start.4 = (f32[32,128]{1,0:T(8,128)S(1)}, f32[32,128]{1,0:T(8,128)S(1)}, u32[]{:S(2)}, u32[]{:S(2)}) collective-permute-start(f32[32,128]{1,0:T(8,128)S(1)} %get-tuple-element.24), channel_id=1, source_target_pairs={{0,6},{1,15},{2,4},{3,13},{4,2},{5,11},{6,0},{7,9},{8,14},{9,7},{1... | collective-permute-start | bytes 49160 | tf_op jit(solution)/shard_map/ppermute | solution.py:849
  11.1 0.0 copy-start
  11.1 1.1 %copy-done = f32[8,3,8,8,128]{4,3,2,1,0:T(8,128)S(1)} copy-done((f32[8,3,8,8,128]{4,3,2,1,0:T(8,128)S(1)}, f32[8,3,8,8,128]{4,3,2,1,0:T(8,128)}, u32[]{:S(2)}) %copy-start) | copy-done | bytes 786456
  12.3 0.0 copy-start.1
  12.3 0.4 %shard_map.70.gram = f32[1,128]{1,0:T(1,128)S(1)} custom-call(f32[1536,128]{1,0:T(8,128)S(1)} %bitcast.4), custom_call_target="tpu_custom_call" | custom-call | tf_op jit(solution)/shard_map/pallas_call | solution.py:880
  12.6 2.2 %collective-permute-done.4.diagonal = f32[32,128]{1,0:T(8,128)S(1)} collective-permute-done((f32[32,128]{1,0:T(8,128)S(1)}, f32[32,128]{1,0:T(8,128)S(1)}, u32[]{:S(2)}, u32[]{:S(2)}) %collective-permute-start.4) | collective-permute-done | bytes 16416 | tf_op jit(solution)/shard_map/ppermute | solution.py:849
  14.8 0.0 collective-permute-done.5.opposite
  14.8 0.0 collective-permute-done.3.turn
  14.8 0.0 collective-permute-done.2.side
  14.8 1.7 %collective-permute-start.6 = (f32[344,128]{1,0:T(8,128)S(1)}, f32[344,128]{1,0:T(8,128)S(1)}, u32[]{:S(2)}, u32[]{:S(2)}) collective-permute-start(f32[344,128]{1,0:T(8,128)S(1)} %shard_map.71), channel_id=1, source_target_pairs={{0,1},{1,0},{2,3},{3,2},{4,5},{5,4},{6,7},{7,6},{8,9},{9,8},{10,11... | collective-permute-start | bytes 528392 | tf_op jit(solution)/shard_map/ppermute | solution.py:889
  16.5 1.0 %collective-permute-done.6.shared = f32[344,128]{1,0:T(8,128)S(1)} collective-permute-done((f32[344,128]{1,0:T(8,128)S(1)}, f32[344,128]{1,0:T(8,128)S(1)}, u32[]{:S(2)}, u32[]{:S(2)}) %collective-permute-start.6) | collective-permute-done | bytes 176160 | tf_op jit(solution)/shard_map/ppermute | solution.py:889
  17.5 0.0 copy-done.1
  17.5 1.3 %shard_map.72 = (f32[16,1,128]{2,1,0:T(1,128)S(1)}, f32[192,128]{1,0:T(8,128)S(1)}) custom-call(f32[192,128]{1,0:T(8,128)S(1)} %get-tuple-element.18.field, f32[192,128]{1,0:T(8,128)S(1)} %get-tuple-element.19.velocity, f32[192,128]{1,0:T(8,128)S(1)} %collective-permute-done.far_field, f32[192,128]{1,0:T(8,128)S(1)} %collective-permute-done.1.far_flow, ...), custom_call_target="tpu_custom_call" | custom-call | tf_op jit(solution)/shard_map/pallas_call | solution.py:891
  18.9 9.0 %all_to_all.5.messages = f32[16,1,128]{2,1,0:T(1,128)S(1)} all-to-all(f32[16,1,128]{2,1,0:T(1,128)S(1)} %get-tuple-element.30), channel_id=1, replica_groups=mesh['groups'=2,'phi'=4,'gz'=2,'row'=2] {'phi','gz','row'}, dimensions={0} | all-to-all | bytes 16384 | tf_op jit(solution)/shard_map/all_to_all | solution.py:913
  27.9 0.9 %shard_map.73 = (f32[192,128]{1,0:T(8,128)}, f32[9]{0:T(128)}) custom-call(f32[16,1,128]{2,1,0:T(1,128)S(1)} %all_to_all.5.messages, f32[192,128]{1,0:T(8,128)S(1)} %get-tuple-element.31.advanced, f32[1536,128]{1,0:T(8,128)S(1)} %bitcast.6), custom_call_target="tpu_custom_call" | custom-call | tf_op jit(solution)/shard_map/pallas_call | solution.py:915
  (1 shorter events, 0.0 us)
Async XLA Ops:
  0.6 1.7 %collective-permute-start = (f32[192,128]{1,0:T(8,128)}, f32[192,128]{1,0:T(8,128)S(1)}, u32[]{:S(2)}, u32[]{:S(2)}) collective-permute-start(f32[192,128]{1,0:T(8,128)} %bitcast.7), channel_id=1, source_target_pairs={{0,1},{1,0},{2,3},{3,2},{4,5},{5,4},{6,7},{7,6},{8,9},{9,8},{10,11... | collective-permute-start | bytes 294920 | tf_op jit(solution)/shard_map/ppermute | solution.py:855
  1.1 1.5 %collective-permute-start.1 = (f32[192,128]{1,0:T(8,128)}, f32[192,128]{1,0:T(8,128)S(1)}, u32[]{:S(2)}, u32[]{:S(2)}) collective-permute-start(f32[192,128]{1,0:T(8,128)} %bitcast.9), channel_id=1, source_target_pairs={{0,1},{1,0},{2,3},{3,2},{4,5},{5,4},{6,7},{7,6},{8,9},{9,8},{10,11... | collective-permute-start | bytes 294920 | tf_op jit(solution)/shard_map/ppermute | solution.py:856
  2.9 11.9 %collective-permute-start.2 = (f32[288,128]{1,0:T(8,128)S(1)}, f32[288,128]{1,0:T(8,128)S(1)}, u32[]{:S(2)}, u32[]{:S(2)}) collective-permute-start(f32[288,128]{1,0:T(8,128)S(1)} %get-tuple-element.22), channel_id=1, source_target_pairs={{0,4},{1,13},{2,6},{3,15},{4,0},{5,9},{6,2},{7,11},{8,12},{9,5},{1... | collective-permute-start | bytes 442376 | tf_op jit(solution)/shard_map/ppermute | solution.py:849
  5.7 9.1 %collective-permute-start.3 = (f32[120,128]{1,0:T(8,128)S(1)}, f32[120,128]{1,0:T(8,128)S(1)}, u32[]{:S(2)}, u32[]{:S(2)}) collective-permute-start(f32[120,128]{1,0:T(8,128)S(1)} %get-tuple-element.23), channel_id=1, source_target_pairs={{0,2},{1,9},{2,0},{3,11},{4,6},{5,13},{6,4},{7,15},{8,10},{9,1},{1... | collective-permute-start | bytes 184328 | tf_op jit(solution)/shard_map/ppermute | solution.py:849
  7.2 7.6 %collective-permute-start.5 = (f32[48,128]{1,0:T(8,128)S(1)}, f32[48,128]{1,0:T(8,128)S(1)}, u32[]{:S(2)}, u32[]{:S(2)}) collective-permute-start(f32[48,128]{1,0:T(8,128)S(1)} %get-tuple-element.21.strip), channel_id=1, source_target_pairs={{0,10},{1,11},{2,8},{3,9},{4,14},{5,15},{6,12},{7,13},{8,2},{9,3},... | collective-permute-start | bytes 73736 | tf_op jit(solution)/shard_map/ppermute | solution.py:849
  9.8 5.0 %collective-permute-start.4 = (f32[32,128]{1,0:T(8,128)S(1)}, f32[32,128]{1,0:T(8,128)S(1)}, u32[]{:S(2)}, u32[]{:S(2)}) collective-permute-start(f32[32,128]{1,0:T(8,128)S(1)} %get-tuple-element.24), channel_id=1, source_target_pairs={{0,6},{1,15},{2,4},{3,13},{4,2},{5,11},{6,0},{7,9},{8,14},{9,7},{1... | collective-permute-start | bytes 49160 | tf_op jit(solution)/shard_map/ppermute | solution.py:849
  11.1 1.1 %copy-start = (f32[8,3,8,8,128]{4,3,2,1,0:T(8,128)S(1)}, f32[8,3,8,8,128]{4,3,2,1,0:T(8,128)}, u32[]{:S(2)}) copy-start(f32[8,3,8,8,128]{4,3,2,1,0:T(8,128)} %param.7) | copy-start | bytes 2359300
  12.3 5.3 %copy-start.1 = (f32[8,3,8,8,128]{4,3,2,1,0:T(8,128)S(1)}, f32[8,3,8,8,128]{4,3,2,1,0:T(8,128)}, u32[]{:S(2)}) copy-start(f32[8,3,8,8,128]{4,3,2,1,0:T(8,128)} %param.7) | copy-start | bytes 2359300
  14.8 2.7 %collective-permute-start.6 = (f32[344,128]{1,0:T(8,128)S(1)}, f32[344,128]{1,0:T(8,128)S(1)}, u32[]{:S(2)}, u32[]{:S(2)}) collective-permute-start(f32[344,128]{1,0:T(8,128)S(1)} %shard_map.71), channel_id=1, source_target_pairs={{0,1},{1,0},{2,3},{3,2},{4,5},{5,4},{6,7},{7,6},{8,9},{9,8},{10,11... | collective-permute-start | bytes 528392 | tf_op jit(solution)/shard_map/ppermute | solution.py:889

commit v7 on v6

--- a/solution.py
+++ b/solution.py
@@ -439,10 +439,12 @@
 side_length = side_axis + 24
 diagonal_wall = 24
 diagonal_length = 32
+strip_length = 56
 share_corner = 8 * tiles
 share_rest = share_corner + 24
 share_turn = share_rest + side_length - side_wall
-share_diagonal = share_turn + 8 * tiles
+share_strip = share_turn + 8 * tiles
+share_diagonal = share_strip + strip_length
 share_length = share_diagonal + diagonal_length
 
 
@@ -531,22 +533,16 @@
                 inner_cell(own, far, r * 8 + depth - 1, 3, 64),
                 inner_cell(own, far, r * 8 + 8 - depth, 3, 64),
             )
-    carry = (diffuse * 2.0 / 1.5) - advect * jnp.minimum(layer(far_flow, 0, 1), 0.0)
-    stretch = (0.5 * advect) * layer(far_field, 0, 1)
-    content = []
-    for r in range(2):
-        content += [layer(far_field, c, r) for c in range(3)]
-        content += [layer(far_flow, c, r) for c in range(3)]
-    content += [
-        carry * layer(far_field, c, 2) + stretch * layer(far_flow, c, 2) for c in range(3)
-    ]
-    for tile in range(tiles):
-        value = content[tile]
-        if tile < 6:
-            value = jnp.where(top == 0, strip[pl.ds(8 * tile, 8), :], value)
-        elif tile == 6:
-            value = jnp.where(top == 0, reflect[...], value)
-        turn[pl.ds(8 * tile, 8), :] = value
+    carry = (diffuse * 2.0 / 1.5) - advect * jnp.minimum(layer(velocity, 0, 1), 0.0)
+    stretch = (0.5 * advect) * layer(field, 0, 1)
+    for c in range(3):
+        for r in range(2):
+            turn[pl.ds(8 * (6 * r + c), 8), :] = layer(field, c, r)
+            turn[pl.ds(8 * (6 * r + 3 + c), 8), :] = layer(velocity, c, r)
+        turn[pl.ds(8 * (12 + c), 8), :] = carry * layer(field, c, 2) + stretch * layer(
+            velocity, c, 2
+        )
+    strip[pl.ds(48, 8), :] = reflect[...]
 
 
 def other_corner(side, first, step):
@@ -556,7 +552,7 @@
     return jnp.where(top == 0, low, high)
 
 
-def share_kernel(side, turn, diagonal, out):
+def share_kernel(side, turn, opposite, diagonal, out):
     top = lax.axis_index("row")
     half = pl.multiple_of((1 - top) * (8 * tiles), 8)
     out[pl.ds(0, 8 * tiles), :] = side[pl.ds(half, 8 * tiles), :]
@@ -568,11 +564,12 @@
         pl.ds(side_wall, side_length - side_wall), :
     ]
     out[pl.ds(share_turn, 8 * tiles), :] = turn[...]
+    out[pl.ds(share_strip, strip_length), :] = opposite[...]
     out[pl.ds(share_diagonal, diagonal_length), :] = diagonal[...]
 
 
 def compact_kernel(
-    field, velocity, far_field, far_flow, reflect, strip, side, turn, diagonal, opposite, shared,
+    field, velocity, far_field, far_flow, reflect, strip, side, diagonal, opposite, shared,
     basis, gram, message, advanced, cells, walls, line, first, second, edge, edge_flow, table,
 ):
     top = lax.axis_index("row")
@@ -631,9 +628,9 @@
             cells[high, :] = jnp.where(low_half, other, 0.0)
 
     slot, inside = lanes(sub) // 8, lanes(sub) % 8
-    axial_turn = [
+    axial_strip = [
         jnp.where(
-            low_half, turn[pl.ds(8 * tile, 8), :], shared[pl.ds(share_turn + 8 * tile, 8), :]
+            low_half, opposite[pl.ds(8 * tile, 8), :], shared[pl.ds(share_strip + 8 * tile, 8), :]
         )
         for tile in range(7)
     ]
@@ -643,7 +640,7 @@
         return jnp.where(own_side[: own.shape[0]], own, other)
 
     for part, (tile, pair) in enumerate(
-        ((reflect[...], rest_pair(side_wall, 2)), (axial_turn[6], diagonal_pair(diagonal_wall, 2)))
+        ((reflect[...], rest_pair(side_wall, 2)), (axial_strip[6], diagonal_pair(diagonal_wall, 2)))
     ):
         below, above = pair
         base = sub * part
@@ -658,7 +655,7 @@
 
     for c in range(6):
         own = strip[pl.ds(8 * c, 8), :]
-        line[pl.ds(sub * c, 8), :] = merge(own, axial_turn[c])
+        line[pl.ds(sub * c, 8), :] = merge(own, axial_strip[c])
         line[pl.ds(sub * c + 8, 8), :] = nothing
     for depth in (1, 2):
         below, above = rest_pair(side_strip + 8 * (depth - 1), 6)
@@ -672,7 +669,7 @@
         combined.append(jnp.where(low_half, pltpu.roll(value, 16, 1), pltpu.roll(value, 80, 1)))
     for c in range(6):
         sign = signs[c % 3]
-        across = opposite[pl.ds(8 * c, 8), :]
+        across = shared[pl.ds(share_strip + 8 * c, 8), :]
         own = jnp.where(
             slot[:8] == 1,
             pltpu.roll(behind[c], 12, 1),
@@ -844,8 +841,8 @@
         for p in range(4):
             for g in range(2):
                 for r in range(2):
-                    q, h = partner(p, g, r)
-                    pairs.append(((p * 2 + g) * 2 + r, (q % 4 * 2 + h) * 2 + r))
+                    q, h, t = partner(p, g, r)
+                    pairs.append(((p * 2 + g) * 2 + r, (q % 4 * 2 + h) * 2 + t))
         return lax.ppermute(value, axes, pairs)
 
     def beside(p, r):
@@ -869,13 +866,13 @@
             shape(side_length, 128),
             shape(8 * tiles, 128),
             shape(diagonal_length, 128),
-            shape(48, 128),
+            shape(strip_length, 128),
         ],
     )(*blocks)
-    opposite = exchange(strip, lambda p, g, r: (p + 2, 1 - g))
-    turn = exchange(turn, lambda p, g, r: (p, 1 - g) if r == 0 else (p + 2, g))
-    diagonal = exchange(diagonal, lambda p, g, r: (beside(p, r), 1 - g))
-    side = exchange(side, lambda p, g, r: (beside(p, r), g))
+    opposite = exchange(strip, lambda p, g, r: (p + 2, 1 - g, 1) if r == 0 else (p, 1 - g, 0))
+    turn = exchange(turn, lambda p, g, r: (p + 2, g, 1) if r == 0 else (p, g, 0))
+    diagonal = exchange(diagonal, lambda p, g, r: (beside(p, r), 1 - g, r))
+    side = exchange(side, lambda p, g, r: (beside(p, r), g, r))
     (basis_rows,) = near(basis.reshape(vectors * 192, 128))
     gram = pl.pallas_call(
         gram_kernel, in_specs=vmem(1), out_specs=vmem(1)[0], out_shape=shape(1, 128)
@@ -884,13 +881,13 @@
         *lax.optimization_barrier((side, turn, diagonal, opposite, gram))
     )
     share = pl.pallas_call(
-        share_kernel, in_specs=vmem(3), out_specs=vmem(1)[0], out_shape=shape(share_length, 128)
-    )(side, turn, diagonal)
+        share_kernel, in_specs=vmem(4), out_specs=vmem(1)[0], out_shape=shape(share_length, 128)
+    )(side, turn, opposite, diagonal)
     shared = lax.ppermute(share, "row", swap)
     strip, shared = near(strip, shared)
     return pl.pallas_call(
         compact_kernel,
-        in_specs=vmem(13),
+        in_specs=vmem(12),
         out_specs=vmem(2),
         out_shape=[shape(devices, 1, 128), shape(192, 128)],
         scratch_shapes=[
@@ -899,7 +896,7 @@
             shape(6 * sub, 128),
         ]
         + march_scratch(),
-    )(*blocks, strip, side, turn, diagonal, opposite, shared, basis_rows, gram)
+    )(*blocks, strip, side, diagonal, opposite, shared, basis_rows, gram)
 
 
 def local(field, velocity, basis, wall_region, wall_conductance):

time: 29 us -> 28.1 us (0.969)
  starting transfers between devices: 10.5 us -> 8.37 us
  waiting for transfers between devices: 3.68 us -> 4.31 us
  blocking collectives: 8.99 us -> 9.54 us
    ppermute x4, starting transfers between devices: 8.22 us -> 6.84 us  [exchange(): return lax.ppermute(value, axes, pairs)]
    ppermute x1, starting transfers between devices: 1.65 us -> 0.94 us  [compact_plan(): shared = lax.ppermute(share, 'row', swap)]
    ppermute x4, waiting for transfers between devices: 2.19 us -> 2.79 us  [exchange(): return lax.ppermute(value, axes, pairs)]
    all_to_all x1, blocking collectives: 8.99 us -> 9.54 us  [local(): messages = lax.all_to_all(message, axes, 0, 0, tiled=True)]
where the time goes in v7:
time: 28.1 us; the launch traced here: 27.8 us
  blocking collectives  9.54 us (34%)
  starting transfers between devices  8.37 us (30%)
  waiting for transfers between devices  4.31 us (15%)
  Pallas kernels  3.82 us (14%)
  local copies, waits for them, and re-layouts  1.14 us (4%)
  between operations  0.66 us (2%)
    all_to_all x1, blocking collectives, local(): messages = lax.all_to_all(message, axes, 0, 0, tiled=True)  9.54 us
    ppermute x4, starting transfers between devices, exchange(): return lax.ppermute(value, axes, pairs)  6.84 us
    ppermute x4, waiting for transfers between devices, exchange(): return lax.ppermute(value, axes, pairs)  2.79 us
    pallas_call x1, Pallas kernels, compact_plan(): pl.pallas_call(compact_kernel, in_specs=vmem(12), out_specs=vmem(2), out_...  1.34 us
    unnamed x4, local copies, waits for them, and re-layouts  1.14 us
    ppermute x1, waiting for transfers between devices, compact_plan(): shared = lax.ppermute(share, 'row', swap)  1.08 us
    pallas_call x1, Pallas kernels, compact_plan(): pl.pallas_call(load_kernel, in_specs=[pl.BlockSpec(memory_space=pltpu.SME...  0.98 us
    ppermute x1, starting transfers between devices, compact_plan(): shared = lax.ppermute(share, 'row', swap)  0.94 us
  transfers between devices with their start and end apart: 7, of which 4 were waited for; matrix products, arithmetic and copies ran while one was open for 0% of the time, Pallas kernels for 5%

profile of v7, /device:TPU:0, one launch (start us, length us, event | category | flops | bytes accessed | tf_op | source)
XLA Modules:
  0.0 27.8 jit_solution(3585804199362335038)
XLA Ops:
  0.6 0.5 %collective-permute-start = (f32[192,128]{1,0:T(8,128)}, f32[192,128]{1,0:T(8,128)S(1)}, u32[]{:S(2)}, u32[]{:S(2)}) collective-permute-start(f32[192,128]{1,0:T(8,128)} %bitcast.7), channel_id=1, source_target_pairs={{0,1},{1,0},{2,3},{3,2},{4,5},{5,4},{6,7},{7,6},{8,9},{9,8},{10,11... | collective-permute-start | bytes 294920 | tf_op jit(solution)/shard_map/ppermute | solution.py:852
  1.1 0.1 collective-permute-start.1
  1.2 1.0 %shard_map.68 = (f32[8,128]{1,0:T(8,128)S(1)}, f32[192,128]{1,0:T(8,128)S(1)}, f32[192,128]{1,0:T(8,128)S(1)}) custom-call(f32[8]{0:T(128)} %conductance.1, s32[8,128]{1,0:T(8,128)} %region.1, f32[192,128]{1,0:T(8,128)} %bitcast.8, f32[192,128]{1,0:T(8,128)} %bitcast.10), custom_call_target="tpu_custom_call" | custom-call | tf_op jit(solution)/shard_map/pallas_call | solution.py:854
  2.2 0.1 collective-permute-done.far_field
  2.3 0.4 %collective-permute-done.1.far_flow = f32[192,128]{1,0:T(8,128)S(1)} collective-permute-done((f32[192,128]{1,0:T(8,128)}, f32[192,128]{1,0:T(8,128)S(1)}, u32[]{:S(2)}, u32[]{:S(2)}) %collective-permute-start.1) | collective-permute-done | bytes 98336 | tf_op jit(solution)/shard_map/ppermute | solution.py:853
  2.7 0.3 shard_map.69
  2.9 2.8 %collective-permute-start.2 = (f32[288,128]{1,0:T(8,128)S(1)}, f32[288,128]{1,0:T(8,128)S(1)}, u32[]{:S(2)}, u32[]{:S(2)}) collective-permute-start(f32[288,128]{1,0:T(8,128)S(1)} %get-tuple-element.22), channel_id=1, source_target_pairs={{0,4},{1,13},{2,6},{3,15},{4,0},{5,9},{6,2},{7,11},{8,12},{9,5},{1... | collective-permute-start | bytes 442376 | tf_op jit(solution)/shard_map/ppermute | solution.py:846
  5.7 1.1 %collective-permute-start.3 = (f32[120,128]{1,0:T(8,128)S(1)}, f32[120,128]{1,0:T(8,128)S(1)}, u32[]{:S(2)}, u32[]{:S(2)}) collective-permute-start(f32[120,128]{1,0:T(8,128)S(1)} %get-tuple-element.23), channel_id=1, source_target_pairs={{0,9},{1,0},{2,11},{3,2},{4,13},{5,4},{6,15},{7,6},{8,1},{9,8},{10... | collective-permute-start | bytes 184328 | tf_op jit(solution)/shard_map/ppermute | solution.py:846
  6.9 2.5 %collective-permute-start.5 = (f32[56,128]{1,0:T(8,128)S(1)}, f32[56,128]{1,0:T(8,128)S(1)}, u32[]{:S(2)}, u32[]{:S(2)}) collective-permute-start(f32[56,128]{1,0:T(8,128)S(1)} %get-tuple-element.21.strip), channel_id=1, source_target_pairs={{0,11},{1,2},{2,9},{3,0},{4,15},{5,6},{6,13},{7,4},{8,3},{9,10},{1... | collective-permute-start | bytes 86024 | tf_op jit(solution)/shard_map/ppermute | solution.py:846
  9.3 0.4 %collective-permute-start.4 = (f32[32,128]{1,0:T(8,128)S(1)}, f32[32,128]{1,0:T(8,128)S(1)}, u32[]{:S(2)}, u32[]{:S(2)}) collective-permute-start(f32[32,128]{1,0:T(8,128)S(1)} %get-tuple-element.24), channel_id=1, source_target_pairs={{0,6},{1,15},{2,4},{3,13},{4,2},{5,11},{6,0},{7,9},{8,14},{9,7},{1... | collective-permute-start | bytes 49160 | tf_op jit(solution)/shard_map/ppermute | solution.py:846
  9.8 0.0 copy-start
  9.8 1.1 %copy-done = f32[8,3,8,8,128]{4,3,2,1,0:T(8,128)S(1)} copy-done((f32[8,3,8,8,128]{4,3,2,1,0:T(8,128)S(1)}, f32[8,3,8,8,128]{4,3,2,1,0:T(8,128)}, u32[]{:S(2)}) %copy-start) | copy-done | bytes 786456
  10.9 0.0 copy-start.1
  10.9 0.4 %shard_map.70.gram = f32[1,128]{1,0:T(1,128)S(1)} custom-call(f32[1536,128]{1,0:T(8,128)S(1)} %bitcast.4), custom_call_target="tpu_custom_call" | custom-call | tf_op jit(solution)/shard_map/pallas_call | solution.py:877
  11.3 2.8 %collective-permute-done.4.diagonal = f32[32,128]{1,0:T(8,128)S(1)} collective-permute-done((f32[32,128]{1,0:T(8,128)S(1)}, f32[32,128]{1,0:T(8,128)S(1)}, u32[]{:S(2)}, u32[]{:S(2)}) %collective-permute-start.4) | collective-permute-done | bytes 16416 | tf_op jit(solution)/shard_map/ppermute | solution.py:846
  14.0 0.0 collective-permute-done.5.opposite
  14.0 0.0 collective-permute-done.3.turn
  14.0 0.0 collective-permute-done.2.side
  14.1 0.9 %collective-permute-start.6 = (f32[400,128]{1,0:T(8,128)S(1)}, f32[400,128]{1,0:T(8,128)S(1)}, u32[]{:S(2)}, u32[]{:S(2)}) collective-permute-start(f32[400,128]{1,0:T(8,128)S(1)} %shard_map.71), channel_id=1, source_target_pairs={{0,1},{1,0},{2,3},{3,2},{4,5},{5,4},{6,7},{7,6},{8,9},{9,8},{10,11... | collective-permute-start | bytes 614408 | tf_op jit(solution)/shard_map/ppermute | solution.py:886
  15.0 1.1 %collective-permute-done.6.shared = f32[400,128]{1,0:T(8,128)S(1)} collective-permute-done((f32[400,128]{1,0:T(8,128)S(1)}, f32[400,128]{1,0:T(8,128)S(1)}, u32[]{:S(2)}, u32[]{:S(2)}) %collective-permute-start.6) | collective-permute-done | bytes 204832 | tf_op jit(solution)/shard_map/ppermute | solution.py:886
  16.1 0.0 copy-done.1
  16.1 1.3 %shard_map.72 = (f32[16,1,128]{2,1,0:T(1,128)S(1)}, f32[192,128]{1,0:T(8,128)S(1)}) custom-call(f32[192,128]{1,0:T(8,128)S(1)} %get-tuple-element.18.field, f32[192,128]{1,0:T(8,128)S(1)} %get-tuple-element.19.velocity, f32[192,128]{1,0:T(8,128)S(1)} %collective-permute-done.far_field, f32[192,128]{1,0:T(8,128)S(1)} %collective-permute-done.1.far_flow, ...), custom_call_target="tpu_custom_call" | custom-call | tf_op jit(solution)/shard_map/pallas_call | solution.py:888
  17.4 9.5 %all_to_all.5.messages = f32[16,1,128]{2,1,0:T(1,128)S(1)} all-to-all(f32[16,1,128]{2,1,0:T(1,128)S(1)} %get-tuple-element.30), channel_id=1, replica_groups=mesh['groups'=2,'phi'=4,'gz'=2,'row'=2] {'phi','gz','row'}, dimensions={0} | all-to-all | bytes 16384 | tf_op jit(solution)/shard_map/all_to_all | solution.py:910
  27.0 0.9 %shard_map.73 = (f32[192,128]{1,0:T(8,128)}, f32[9]{0:T(128)}) custom-call(f32[16,1,128]{2,1,0:T(1,128)S(1)} %all_to_all.5.messages, f32[192,128]{1,0:T(8,128)S(1)} %get-tuple-element.31.advanced, f32[1536,128]{1,0:T(8,128)S(1)} %bitcast.6), custom_call_target="tpu_custom_call" | custom-call | tf_op jit(solution)/shard_map/pallas_call | solution.py:912
  (1 shorter events, 0.0 us)
Async XLA Ops:
  0.6 1.7 %collective-permute-start = (f32[192,128]{1,0:T(8,128)}, f32[192,128]{1,0:T(8,128)S(1)}, u32[]{:S(2)}, u32[]{:S(2)}) collective-permute-start(f32[192,128]{1,0:T(8,128)} %bitcast.7), channel_id=1, source_target_pairs={{0,1},{1,0},{2,3},{3,2},{4,5},{5,4},{6,7},{7,6},{8,9},{9,8},{10,11... | collective-permute-start | bytes 294920 | tf_op jit(solution)/shard_map/ppermute | solution.py:852
  1.1 1.5 %collective-permute-start.1 = (f32[192,128]{1,0:T(8,128)}, f32[192,128]{1,0:T(8,128)S(1)}, u32[]{:S(2)}, u32[]{:S(2)}) collective-permute-start(f32[192,128]{1,0:T(8,128)} %bitcast.9), channel_id=1, source_target_pairs={{0,1},{1,0},{2,3},{3,2},{4,5},{5,4},{6,7},{7,6},{8,9},{9,8},{10,11... | collective-permute-start | bytes 294920 | tf_op jit(solution)/shard_map/ppermute | solution.py:853
  2.9 11.1 %collective-permute-start.2 = (f32[288,128]{1,0:T(8,128)S(1)}, f32[288,128]{1,0:T(8,128)S(1)}, u32[]{:S(2)}, u32[]{:S(2)}) collective-permute-start(f32[288,128]{1,0:T(8,128)S(1)} %get-tuple-element.22), channel_id=1, source_target_pairs={{0,4},{1,13},{2,6},{3,15},{4,0},{5,9},{6,2},{7,11},{8,12},{9,5},{1... | collective-permute-start | bytes 442376 | tf_op jit(solution)/shard_map/ppermute | solution.py:846
  5.7 8.3 %collective-permute-start.3 = (f32[120,128]{1,0:T(8,128)S(1)}, f32[120,128]{1,0:T(8,128)S(1)}, u32[]{:S(2)}, u32[]{:S(2)}) collective-permute-start(f32[120,128]{1,0:T(8,128)S(1)} %get-tuple-element.23), channel_id=1, source_target_pairs={{0,9},{1,0},{2,11},{3,2},{4,13},{5,4},{6,15},{7,6},{8,1},{9,8},{10... | collective-permute-start | bytes 184328 | tf_op jit(solution)/shard_map/ppermute | solution.py:846
  6.9 7.2 %collective-permute-start.5 = (f32[56,128]{1,0:T(8,128)S(1)}, f32[56,128]{1,0:T(8,128)S(1)}, u32[]{:S(2)}, u32[]{:S(2)}) collective-permute-start(f32[56,128]{1,0:T(8,128)S(1)} %get-tuple-element.21.strip), channel_id=1, source_target_pairs={{0,11},{1,2},{2,9},{3,0},{4,15},{5,6},{6,13},{7,4},{8,3},{9,10},{1... | collective-permute-start | bytes 86024 | tf_op jit(solution)/shard_map/ppermute | solution.py:846
  9.3 4.7 %collective-permute-start.4 = (f32[32,128]{1,0:T(8,128)S(1)}, f32[32,128]{1,0:T(8,128)S(1)}, u32[]{:S(2)}, u32[]{:S(2)}) collective-permute-start(f32[32,128]{1,0:T(8,128)S(1)} %get-tuple-element.24), channel_id=1, source_target_pairs={{0,6},{1,15},{2,4},{3,13},{4,2},{5,11},{6,0},{7,9},{8,14},{9,7},{1... | collective-permute-start | bytes 49160 | tf_op jit(solution)/shard_map/ppermute | solution.py:846
  9.8 1.1 %copy-start = (f32[8,3,8,8,128]{4,3,2,1,0:T(8,128)S(1)}, f32[8,3,8,8,128]{4,3,2,1,0:T(8,128)}, u32[]{:S(2)}) copy-start(f32[8,3,8,8,128]{4,3,2,1,0:T(8,128)} %param.7) | copy-start | bytes 2359300
  10.9 5.2 %copy-start.1 = (f32[8,3,8,8,128]{4,3,2,1,0:T(8,128)S(1)}, f32[8,3,8,8,128]{4,3,2,1,0:T(8,128)}, u32[]{:S(2)}) copy-start(f32[8,3,8,8,128]{4,3,2,1,0:T(8,128)} %param.7) | copy-start | bytes 2359300
  14.1 2.0 %collective-permute-start.6 = (f32[400,128]{1,0:T(8,128)S(1)}, f32[400,128]{1,0:T(8,128)S(1)}, u32[]{:S(2)}, u32[]{:S(2)}) collective-permute-start(f32[400,128]{1,0:T(8,128)S(1)} %shard_map.71), channel_id=1, source_target_pairs={{0,1},{1,0},{2,3},{3,2},{4,5},{5,4},{6,7},{7,6},{8,9},{9,8},{10,11... | collective-permute-start | bytes 614408 | tf_op jit(solution)/shard_map/ppermute | solution.py:886

commit v8 on v7

--- a/solution.py
+++ b/solution.py
@@ -424,11 +424,7 @@
             for m in range(count):
                 sums[m] += basis[pl.ds(192 * m + 64 * c + 8 * (w - 3), 8), :] * value
             sums[count] += value * value
-    spot = lanes(1)
-    line = gram[...]
-    for m in range(count + 1):
-        total = jnp.sum(jnp.sum(sums[m], axis=0, keepdims=True), axis=1, keepdims=True)
-        line = jnp.where(spot == m, total, line)
+    line = write_sums(jnp.broadcast_to(gram[...], (8, 128)), sums, range(count + 1))[:1]
     for device in range(message.shape[0]):
         message[device] = line
 
@@ -691,45 +687,101 @@
     )
 
 
+def two_sum(a, b):
+    total = a + b
+    part = total - a
+    return total, (a - (total - part)) + (b - part)
+
+
+def split(a):
+    scaled = 4097.0 * a
+    high = scaled - (scaled - a)
+    return high, a - high
+
+
+def two_product(a, b, a_parts, b_parts):
+    product = a * b
+    (a_high, a_low), (b_high, b_low) = a_parts, b_parts
+    rest = ((a_high * b_high - product) + a_high * b_low + a_low * b_high) + a_low * b_low
+    return product, rest
+
+
+def write_sums(line, sums, places):
+    spot = lanes(8)
+    ones = jnp.ones((128, 128), jnp.bfloat16)
+    stacked = jnp.concatenate(sums, axis=0)
+    parts = []
+    for _ in range(3):
+        part = stacked.astype(jnp.bfloat16)
+        stacked = stacked - part.astype(jnp.float32)
+        parts.append(jnp.dot(part, ones, preferred_element_type=jnp.float32))
+    large, small = parts[0], parts[1] + parts[2]
+    for index, place in enumerate(places):
+        rows = slice(8 * index, 8 * index + 8)
+        total, rest = two_sum(large[rows], small[rows])
+        for step in (4, 2, 1):
+            total, error = two_sum(total, pltpu.roll(total, step, 0))
+            rest = rest + pltpu.roll(rest, step, 0) + error
+        line = jnp.where(spot == place, total, jnp.where(spot == place + 64, rest, line))
+    return line
+
+
 def gram_place(m, n):
     return 16 + m * (m + 1) // 2 + n
 
 
 def gram_kernel(basis, out):
     count = basis.shape[0] // 192
-    spot = lanes(1)
-    line = jnp.zeros((1, 128), jnp.float32)
+    line = jnp.zeros((8, 128), jnp.float32)
     for m in range(count):
         sums = [jnp.zeros((8, 128), jnp.float32) for _ in range(m + 1)]
         for tile in range(24):
             value = basis[pl.ds(192 * m + 8 * tile, 8), :]
             for n in range(m + 1):
                 sums[n] += value * basis[pl.ds(192 * n + 8 * tile, 8), :]
-        for n in range(m + 1):
-            total = jnp.sum(jnp.sum(sums[n], axis=0, keepdims=True), axis=1, keepdims=True)
-            line = jnp.where(spot == gram_place(m, n), total, line)
-    out[...] = line
+        line = write_sums(line, sums, [gram_place(m, n) for n in range(m + 1)])
+    out[...] = line[:1]
 
 
 def finish_kernel(cell_count, messages, advanced, basis, out, hessenberg):
     count = basis.shape[0] // 192
-    total = messages[0]
-    for device in range(1, messages.shape[0]):
-        total = total + messages[device]
+    terms = [messages[device] for device in range(messages.shape[0])]
+    errors = []
+    while len(terms) > 1:
+        pairs = [two_sum(a, b) for a, b in zip(terms[::2], terms[1::2])]
+        errors += [error for _, error in pairs]
+        terms = [total for total, _ in pairs] + terms[len(terms) // 2 * 2 :]
+    while len(errors) > 1:
+        errors = [a + b for a, b in zip(errors[::2], errors[1::2])] + errors[len(errors) // 2 * 2 :]
+    total = terms[0]
+    rest = pltpu.roll(jnp.broadcast_to(total, (8, 128)), 64, 1)
+    rest = rest + errors[0] if errors else rest
 
     def entry(index):
-        return jnp.broadcast_to(total[:, index : index + 1], (8, 128))
-
-    pending = [entry(m) for m in range(count)]
-    energy = entry(count)
+        high = jnp.broadcast_to(total[:, index : index + 1], (8, 128))
+        return high, jnp.broadcast_to(rest[:1, index : index + 1], (8, 128))
+
+    pending, pending_rest = [list(part) for part in zip(*[entry(m) for m in range(count)])]
+    energy, energy_rest = entry(count)
     weights = []
+    diagonals = [entry(gram_place(m, m)) for m in range(count)]
+    inverses = [1.0 / diagonal for diagonal, _ in diagonals]
     for m in range(count):
-        diagonal = entry(gram_place(m, m))
-        weight = pending[m] / diagonal
+        weight = pending[m] * inverses[m]
         weights.append(weight)
-        energy = energy - weight * (2.0 * pending[m] - weight * diagonal)
+        parts = split(weight)
+        diagonal, diagonal_rest = diagonals[m]
+        product, error = two_product(weight, diagonal, parts, split(diagonal))
+        left = (pending[m] - product) + (pending_rest[m] - error - weight * diagonal_rest)
+        product, error = two_product(weight, pending[m], parts, split(pending[m]))
+        energy, lost = two_sum(energy, -product)
+        energy_rest = energy_rest + (lost - error - weight * (pending_rest[m] + left))
         for n in range(m + 1, count):
-            pending[n] = pending[n] - weight * entry(gram_place(n, m))
+            factor, factor_rest = entry(gram_place(n, m))
+            product, error = two_product(weight, factor, parts, split(factor))
+            pending[n], lost = two_sum(pending[n], -product)
+            pending_rest[n] = pending_rest[n] + (lost - error - weight * factor_rest)
+    energy = energy + energy_rest
     spread = jnp.sqrt(jnp.maximum(energy, 0.0) / cell_count + epsilon)
     scale = 1.0 / spread
     for tile in range(24):

time: 28.1 us -> 28.3 us (level)
  Pallas kernels: 3.82 us -> 4.25 us
where the time goes in v8:
time: 28.3 us; the launch traced here: 28.1 us
  blocking collectives  9.53 us (34%)
  starting transfers between devices  8.37 us (30%)
  Pallas kernels  4.25 us (15%)
  waiting for transfers between devices  4.14 us (15%)
  local copies, waits for them, and re-layouts  1.14 us (4%)
  between operations  0.67 us (2%)
    all_to_all x1, blocking collectives, local(): messages = lax.all_to_all(message, axes, 0, 0, tiled=True)  9.53 us
    ppermute x4, starting transfers between devices, exchange(): return lax.ppermute(value, axes, pairs)  6.84 us
    ppermute x4, waiting for transfers between devices, exchange(): return lax.ppermute(value, axes, pairs)  2.61 us
    pallas_call x1, Pallas kernels, compact_plan(): pl.pallas_call(compact_kernel, in_specs=vmem(12), out_specs=vmem(2), out_...  1.45 us
    unnamed x4, local copies, waits for them, and re-layouts  1.14 us
    ppermute x1, waiting for transfers between devices, compact_plan(): shared = lax.ppermute(share, 'row', swap)  1.08 us
    pallas_call x1, Pallas kernels, local(): pl.pallas_call(functools.partial(finish_kernel, float(field.size * device...  1.01 us
    pallas_call x1, Pallas kernels, compact_plan(): pl.pallas_call(load_kernel, in_specs=[pl.BlockSpec(memory_space=pltpu.SME...  0.98 us
  transfers between devices with their start and end apart: 7, of which 4 were waited for; matrix products, arithmetic and copies ran while one was open for 0% of the time, Pallas kernels for 5%

profile of v8, /device:TPU:0, one launch (start us, length us, event | category | flops | bytes accessed | tf_op | source)
XLA Modules:
  0.0 28.1 jit_solution(3742292508007149426)
XLA Ops:
  0.6 0.5 %collective-permute-start = (f32[192,128]{1,0:T(8,128)}, f32[192,128]{1,0:T(8,128)S(1)}, u32[]{:S(2)}, u32[]{:S(2)}) collective-permute-start(f32[192,128]{1,0:T(8,128)} %bitcast.7), channel_id=1, source_target_pairs={{0,1},{1,0},{2,3},{3,2},{4,5},{5,4},{6,7},{7,6},{8,9},{9,8},{10,11... | collective-permute-start | bytes 294920 | tf_op jit(solution)/shard_map/ppermute | solution.py:904
  1.1 0.1 collective-permute-start.1
  1.2 1.0 %shard_map.68 = (f32[8,128]{1,0:T(8,128)S(1)}, f32[192,128]{1,0:T(8,128)S(1)}, f32[192,128]{1,0:T(8,128)S(1)}) custom-call(f32[8]{0:T(128)} %conductance.1, s32[8,128]{1,0:T(8,128)} %region.1, f32[192,128]{1,0:T(8,128)} %bitcast.8, f32[192,128]{1,0:T(8,128)} %bitcast.10), custom_call_target="tpu_custom_call" | custom-call | tf_op jit(solution)/shard_map/pallas_call | solution.py:906
  2.2 0.1 collective-permute-done.far_field
  2.3 0.4 %collective-permute-done.1.far_flow = f32[192,128]{1,0:T(8,128)S(1)} collective-permute-done((f32[192,128]{1,0:T(8,128)}, f32[192,128]{1,0:T(8,128)S(1)}, u32[]{:S(2)}, u32[]{:S(2)}) %collective-permute-start.1) | collective-permute-done | bytes 98336 | tf_op jit(solution)/shard_map/ppermute | solution.py:905
  2.7 0.3 shard_map.69
  2.9 2.8 %collective-permute-start.2 = (f32[288,128]{1,0:T(8,128)S(1)}, f32[288,128]{1,0:T(8,128)S(1)}, u32[]{:S(2)}, u32[]{:S(2)}) collective-permute-start(f32[288,128]{1,0:T(8,128)S(1)} %get-tuple-element.22), channel_id=1, source_target_pairs={{0,4},{1,13},{2,6},{3,15},{4,0},{5,9},{6,2},{7,11},{8,12},{9,5},{1... | collective-permute-start | bytes 442376 | tf_op jit(solution)/shard_map/ppermute | solution.py:898
  5.7 1.1 %collective-permute-start.3 = (f32[120,128]{1,0:T(8,128)S(1)}, f32[120,128]{1,0:T(8,128)S(1)}, u32[]{:S(2)}, u32[]{:S(2)}) collective-permute-start(f32[120,128]{1,0:T(8,128)S(1)} %get-tuple-element.23), channel_id=1, source_target_pairs={{0,9},{1,0},{2,11},{3,2},{4,13},{5,4},{6,15},{7,6},{8,1},{9,8},{10... | collective-permute-start | bytes 184328 | tf_op jit(solution)/shard_map/ppermute | solution.py:898
  6.9 2.5 %collective-permute-start.5 = (f32[56,128]{1,0:T(8,128)S(1)}, f32[56,128]{1,0:T(8,128)S(1)}, u32[]{:S(2)}, u32[]{:S(2)}) collective-permute-start(f32[56,128]{1,0:T(8,128)S(1)} %get-tuple-element.21.strip), channel_id=1, source_target_pairs={{0,11},{1,2},{2,9},{3,0},{4,15},{5,6},{6,13},{7,4},{8,3},{9,10},{1... | collective-permute-start | bytes 86024 | tf_op jit(solution)/shard_map/ppermute | solution.py:898
  9.3 0.4 %collective-permute-start.4 = (f32[32,128]{1,0:T(8,128)S(1)}, f32[32,128]{1,0:T(8,128)S(1)}, u32[]{:S(2)}, u32[]{:S(2)}) collective-permute-start(f32[32,128]{1,0:T(8,128)S(1)} %get-tuple-element.24), channel_id=1, source_target_pairs={{0,6},{1,15},{2,4},{3,13},{4,2},{5,11},{6,0},{7,9},{8,14},{9,7},{1... | collective-permute-start | bytes 49160 | tf_op jit(solution)/shard_map/ppermute | solution.py:898
  9.8 0.0 copy-start
  9.8 1.1 %copy-done = f32[8,3,8,8,128]{4,3,2,1,0:T(8,128)S(1)} copy-done((f32[8,3,8,8,128]{4,3,2,1,0:T(8,128)S(1)}, f32[8,3,8,8,128]{4,3,2,1,0:T(8,128)}, u32[]{:S(2)}) %copy-start) | copy-done | bytes 786456
  10.9 0.0 copy-start.1
  10.9 0.5 %shard_map.70.gram = f32[1,128]{1,0:T(1,128)S(1)} custom-call(f32[1536,128]{1,0:T(8,128)S(1)} %bitcast.4), custom_call_target="tpu_custom_call" | custom-call | tf_op jit(solution)/shard_map/pallas_call | solution.py:929
  11.4 2.6 %collective-permute-done.4.diagonal = f32[32,128]{1,0:T(8,128)S(1)} collective-permute-done((f32[32,128]{1,0:T(8,128)S(1)}, f32[32,128]{1,0:T(8,128)S(1)}, u32[]{:S(2)}, u32[]{:S(2)}) %collective-permute-start.4) | collective-permute-done | bytes 16416 | tf_op jit(solution)/shard_map/ppermute | solution.py:898
  14.0 0.0 collective-permute-done.5.opposite
  14.0 0.0 collective-permute-done.3.turn
  14.0 0.0 collective-permute-done.2.side
  14.1 0.9 %collective-permute-start.6 = (f32[400,128]{1,0:T(8,128)S(1)}, f32[400,128]{1,0:T(8,128)S(1)}, u32[]{:S(2)}, u32[]{:S(2)}) collective-permute-start(f32[400,128]{1,0:T(8,128)S(1)} %shard_map.71), channel_id=1, source_target_pairs={{0,1},{1,0},{2,3},{3,2},{4,5},{5,4},{6,7},{7,6},{8,9},{9,8},{10,11... | collective-permute-start | bytes 614408 | tf_op jit(solution)/shard_map/ppermute | solution.py:938
  15.0 1.1 %collective-permute-done.6.shared = f32[400,128]{1,0:T(8,128)S(1)} collective-permute-done((f32[400,128]{1,0:T(8,128)S(1)}, f32[400,128]{1,0:T(8,128)S(1)}, u32[]{:S(2)}, u32[]{:S(2)}) %collective-permute-start.6) | collective-permute-done | bytes 204832 | tf_op jit(solution)/shard_map/ppermute | solution.py:938
  16.1 0.0 copy-done.1
  16.1 1.5 %shard_map.72 = (f32[16,1,128]{2,1,0:T(1,128)S(1)}, f32[192,128]{1,0:T(8,128)S(1)}) custom-call(f32[192,128]{1,0:T(8,128)S(1)} %get-tuple-element.18.field, f32[192,128]{1,0:T(8,128)S(1)} %get-tuple-element.19.velocity, f32[192,128]{1,0:T(8,128)S(1)} %collective-permute-done.far_field, f32[192,128]{1,0:T(8,128)S(1)} %collective-permute-done.1.far_flow, ...), custom_call_target="tpu_custom_call" | custom-call | tf_op jit(solution)/shard_map/pallas_call | solution.py:940
  17.6 9.5 %all_to_all.5.messages = f32[16,1,128]{2,1,0:T(1,128)S(1)} all-to-all(f32[16,1,128]{2,1,0:T(1,128)S(1)} %get-tuple-element.30), channel_id=1, replica_groups=mesh['groups'=2,'phi'=4,'gz'=2,'row'=2] {'phi','gz','row'}, dimensions={0} | all-to-all | bytes 16384 | tf_op jit(solution)/shard_map/all_to_all | solution.py:962
  27.1 1.0 %shard_map.73 = (f32[192,128]{1,0:T(8,128)}, f32[9]{0:T(128)}) custom-call(f32[16,1,128]{2,1,0:T(1,128)S(1)} %all_to_all.5.messages, f32[192,128]{1,0:T(8,128)S(1)} %get-tuple-element.31.advanced, f32[1536,128]{1,0:T(8,128)S(1)} %bitcast.6), custom_call_target="tpu_custom_call" | custom-call | tf_op jit(solution)/shard_map/pallas_call | solution.py:964
  (1 shorter events, 0.0 us)
Async XLA Ops:
  0.6 1.7 %collective-permute-start = (f32[192,128]{1,0:T(8,128)}, f32[192,128]{1,0:T(8,128)S(1)}, u32[]{:S(2)}, u32[]{:S(2)}) collective-permute-start(f32[192,128]{1,0:T(8,128)} %bitcast.7), channel_id=1, source_target_pairs={{0,1},{1,0},{2,3},{3,2},{4,5},{5,4},{6,7},{7,6},{8,9},{9,8},{10,11... | collective-permute-start | bytes 294920 | tf_op jit(solution)/shard_map/ppermute | solution.py:904
  1.1 1.5 %collective-permute-start.1 = (f32[192,128]{1,0:T(8,128)}, f32[192,128]{1,0:T(8,128)S(1)}, u32[]{:S(2)}, u32[]{:S(2)}) collective-permute-start(f32[192,128]{1,0:T(8,128)} %bitcast.9), channel_id=1, source_target_pairs={{0,1},{1,0},{2,3},{3,2},{4,5},{5,4},{6,7},{7,6},{8,9},{9,8},{10,11... | collective-permute-start | bytes 294920 | tf_op jit(solution)/shard_map/ppermute | solution.py:905
  2.9 11.1 %collective-permute-start.2 = (f32[288,128]{1,0:T(8,128)S(1)}, f32[288,128]{1,0:T(8,128)S(1)}, u32[]{:S(2)}, u32[]{:S(2)}) collective-permute-start(f32[288,128]{1,0:T(8,128)S(1)} %get-tuple-element.22), channel_id=1, source_target_pairs={{0,4},{1,13},{2,6},{3,15},{4,0},{5,9},{6,2},{7,11},{8,12},{9,5},{1... | collective-permute-start | bytes 442376 | tf_op jit(solution)/shard_map/ppermute | solution.py:898
  5.7 8.3 %collective-permute-start.3 = (f32[120,128]{1,0:T(8,128)S(1)}, f32[120,128]{1,0:T(8,128)S(1)}, u32[]{:S(2)}, u32[]{:S(2)}) collective-permute-start(f32[120,128]{1,0:T(8,128)S(1)} %get-tuple-element.23), channel_id=1, source_target_pairs={{0,9},{1,0},{2,11},{3,2},{4,13},{5,4},{6,15},{7,6},{8,1},{9,8},{10... | collective-permute-start | bytes 184328 | tf_op jit(solution)/shard_map/ppermute | solution.py:898
  6.9 7.2 %collective-permute-start.5 = (f32[56,128]{1,0:T(8,128)S(1)}, f32[56,128]{1,0:T(8,128)S(1)}, u32[]{:S(2)}, u32[]{:S(2)}) collective-permute-start(f32[56,128]{1,0:T(8,128)S(1)} %get-tuple-element.21.strip), channel_id=1, source_target_pairs={{0,11},{1,2},{2,9},{3,0},{4,15},{5,6},{6,13},{7,4},{8,3},{9,10},{1... | collective-permute-start | bytes 86024 | tf_op jit(solution)/shard_map/ppermute | solution.py:898
  9.3 4.7 %collective-permute-start.4 = (f32[32,128]{1,0:T(8,128)S(1)}, f32[32,128]{1,0:T(8,128)S(1)}, u32[]{:S(2)}, u32[]{:S(2)}) collective-permute-start(f32[32,128]{1,0:T(8,128)S(1)} %get-tuple-element.24), channel_id=1, source_target_pairs={{0,6},{1,15},{2,4},{3,13},{4,2},{5,11},{6,0},{7,9},{8,14},{9,7},{1... | collective-permute-start | bytes 49160 | tf_op jit(solution)/shard_map/ppermute | solution.py:898
  9.8 1.1 %copy-start = (f32[8,3,8,8,128]{4,3,2,1,0:T(8,128)S(1)}, f32[8,3,8,8,128]{4,3,2,1,0:T(8,128)}, u32[]{:S(2)}) copy-start(f32[8,3,8,8,128]{4,3,2,1,0:T(8,128)} %param.7) | copy-start | bytes 2359300
  10.9 5.2 %copy-start.1 = (f32[8,3,8,8,128]{4,3,2,1,0:T(8,128)S(1)}, f32[8,3,8,8,128]{4,3,2,1,0:T(8,128)}, u32[]{:S(2)}) copy-start(f32[8,3,8,8,128]{4,3,2,1,0:T(8,128)} %param.7) | copy-start | bytes 2359300
  14.1 2.0 %collective-permute-start.6 = (f32[400,128]{1,0:T(8,128)S(1)}, f32[400,128]{1,0:T(8,128)S(1)}, u32[]{:S(2)}, u32[]{:S(2)}) collective-permute-start(f32[400,128]{1,0:T(8,128)S(1)} %shard_map.71), channel_id=1, source_target_pairs={{0,1},{1,0},{2,3},{3,2},{4,5},{5,4},{6,7},{7,6},{8,9},{9,8},{10,11... | collective-permute-start | bytes 614408 | tf_op jit(solution)/shard_map/ppermute | solution.py:938

commit v9 on v8

--- a/solution.py
+++ b/solution.py
@@ -448,7 +448,18 @@
     return (lax.axis_index("phi") + lax.axis_index("row")) % 2 == 0
 
 
-def load_kernel(conductance, region, field, velocity, reflect, field_copy, flow_copy):
+def own_strip(source, c):
+    slot = lanes(8) // 8
+    part = jnp.zeros((8, 128), jnp.float32)
+    for r in range(8):
+        moved = pltpu.roll(layer(source, c, r), (8 * r + 4) % 128, 1)
+        part = jnp.where(slot == r, moved, part)
+    return part
+
+
+def load_kernel(
+    conductance, region, field, velocity, reflect, field_copy, flow_copy, turn, own_ends
+):
     kinds = region[...]
     value = jnp.zeros(kinds.shape, jnp.float32)
     for kind in range(conductance.shape[0]):
@@ -456,9 +467,20 @@
     reflect[...] = 1.0 - 2.0 * value / (1.0 + value)
     field_copy[...] = field[...]
     flow_copy[...] = velocity[...]
-
-
-def send_kernel(field, velocity, far_field, far_flow, reflect, side, turn, diagonal, strip):
+    carry = (diffuse * 2.0 / 1.5) - advect * jnp.minimum(layer(velocity, 0, 1), 0.0)
+    stretch = (0.5 * advect) * layer(field, 0, 1)
+    for c in range(3):
+        for r in range(2):
+            turn[pl.ds(8 * (6 * r + c), 8), :] = layer(field, c, r)
+            turn[pl.ds(8 * (6 * r + 3 + c), 8), :] = layer(velocity, c, r)
+        turn[pl.ds(8 * (12 + c), 8), :] = carry * layer(field, c, 2) + stretch * layer(
+            velocity, c, 2
+        )
+    for c in range(6):
+        own_ends[pl.ds(8 * c, 8), :] = own_strip(field if c < 3 else velocity, c % 3)
+
+
+def send_kernel(field, velocity, far_field, far_flow, reflect, own_ends, side, diagonal, strip):
     top = lax.axis_index("row")
     upper = faces_up()
     slot = lanes(8) // 8
@@ -498,17 +520,10 @@
         diagonal[pl.ds(diagonal_wall + depth - 1, 1), :] = wall
 
     for c in range(6):
-        own, far = (field, far_field) if c < 3 else (velocity, far_flow)
-        parts = []
-        for source in (own, far):
-            part = jnp.zeros((8, 128), jnp.float32)
-            for r in range(8):
-                part = jnp.where(
-                    slot == r, pltpu.roll(layer(source, c % 3, r), (8 * r + 4) % 128, 1), part
-                )
-            parts.append(part)
-        low = jnp.where(top == 0, parts[0], parts[1])
-        high = jnp.where(top == 0, parts[1], parts[0])
+        own = own_ends[pl.ds(8 * c, 8), :]
+        far = own_strip(far_field if c < 3 else far_flow, c % 3)
+        low = jnp.where(top == 0, own, far)
+        high = jnp.where(top == 0, far, own)
         strip[pl.ds(8 * c, 8), :] = jnp.where(slot < 8, low, pltpu.roll(high, 64, 1))
     for depth in (1, 2):
         edge = facing(lambda q: strip[pl.ds(q, 6, stride=8), :], depth)
@@ -529,15 +544,6 @@
                 inner_cell(own, far, r * 8 + depth - 1, 3, 64),
                 inner_cell(own, far, r * 8 + 8 - depth, 3, 64),
             )
-    carry = (diffuse * 2.0 / 1.5) - advect * jnp.minimum(layer(velocity, 0, 1), 0.0)
-    stretch = (0.5 * advect) * layer(field, 0, 1)
-    for c in range(3):
-        for r in range(2):
-            turn[pl.ds(8 * (6 * r + c), 8), :] = layer(field, c, r)
-            turn[pl.ds(8 * (6 * r + 3 + c), 8), :] = layer(velocity, c, r)
-        turn[pl.ds(8 * (12 + c), 8), :] = carry * layer(field, c, 2) + stretch * layer(
-            velocity, c, 2
-        )
     strip[pl.ds(48, 8), :] = reflect[...]
 
 
@@ -745,7 +751,9 @@
 
 def finish_kernel(cell_count, messages, advanced, basis, out, hessenberg):
     count = basis.shape[0] // 192
-    terms = [messages[device] for device in range(messages.shape[0])]
+    terms = [
+        jnp.broadcast_to(messages[device], (8, 128)) for device in range(messages.shape[0])
+    ]
     errors = []
     while len(terms) > 1:
         pairs = [two_sum(a, b) for a, b in zip(terms[::2], terms[1::2])]
@@ -754,12 +762,12 @@
     while len(errors) > 1:
         errors = [a + b for a, b in zip(errors[::2], errors[1::2])] + errors[len(errors) // 2 * 2 :]
     total = terms[0]
-    rest = pltpu.roll(jnp.broadcast_to(total, (8, 128)), 64, 1)
+    rest = pltpu.roll(total, 64, 1)
     rest = rest + errors[0] if errors else rest
 
     def entry(index):
         high = jnp.broadcast_to(total[:, index : index + 1], (8, 128))
-        return high, jnp.broadcast_to(rest[:1, index : index + 1], (8, 128))
+        return high, jnp.broadcast_to(rest[:, index : index + 1], (8, 128))
 
     pending, pending_rest = [list(part) for part in zip(*[entry(m) for m in range(count)])]
     energy, energy_rest = entry(count)
@@ -903,24 +911,29 @@
     swap = [(0, 1), (1, 0)]
     far_field = lax.ppermute(field_rows, "row", swap)
     far_flow = lax.ppermute(flow_rows, "row", swap)
-    reflect, field_rows, flow_rows = pl.pallas_call(
+    reflect, field_rows, flow_rows, turn, own_ends = pl.pallas_call(
         load_kernel,
         in_specs=[pl.BlockSpec(memory_space=pltpu.SMEM)] + vmem(3),
-        out_specs=vmem(3),
-        out_shape=[shape(8, 128), shape(192, 128), shape(192, 128)],
+        out_specs=vmem(5),
+        out_shape=[
+            shape(8, 128),
+            shape(192, 128),
+            shape(192, 128),
+            shape(8 * tiles, 128),
+            shape(48, 128),
+        ],
     )(wall_conductance, wall_region, field_rows, flow_rows)
     blocks = near(field_rows, flow_rows, far_field, far_flow, reflect)
-    side, turn, diagonal, strip = pl.pallas_call(
+    side, diagonal, strip = pl.pallas_call(
         send_kernel,
-        in_specs=vmem(5),
-        out_specs=vmem(4),
+        in_specs=vmem(6),
+        out_specs=vmem(3),
         out_shape=[
             shape(side_length, 128),
-            shape(8 * tiles, 128),
             shape(diagonal_length, 128),
             shape(strip_length, 128),
         ],
-    )(*blocks)
+    )(*blocks, *near(own_ends))
     opposite = exchange(strip, lambda p, g, r: (p + 2, 1 - g, 1) if r == 0 else (p, 1 - g, 0))
     turn = exchange(turn, lambda p, g, r: (p + 2, g, 1) if r == 0 else (p, g, 0))
     diagonal = exchange(diagonal, lambda p, g, r: (beside(p, r), 1 - g, r))

time: 28.3 us -> 28.2 us (level)
  transfers between devices with their start and end apart: 7 -> 7, of which waited for: 4 -> 3; matrix products, arithmetic and copies ran while one was open for 0% -> 0% of each run, Pallas kernels for 5% -> 6%
where the time goes in v9:
time: 28.2 us; the launch traced here: 28 us
  blocking collectives  9.53 us (34%)
  starting transfers between devices  8.38 us (30%)
  Pallas kernels  4.24 us (15%)
  waiting for transfers between devices  4.03 us (14%)
  local copies, waits for them, and re-layouts  1.14 us (4%)
  between operations  0.68 us (2%)
    all_to_all x1, blocking collectives, local(): messages = lax.all_to_all(message, axes, 0, 0, tiled=True)  9.53 us
    ppermute x4, starting transfers between devices, exchange(): return lax.ppermute(value, axes, pairs)  6.84 us
    ppermute x4, waiting for transfers between devices, exchange(): return lax.ppermute(value, axes, pairs)  2.6 us
    pallas_call x1, Pallas kernels, compact_plan(): pl.pallas_call(compact_kernel, in_specs=vmem(12), out_specs=vmem(2), out_...  1.45 us
    unnamed x4, local copies, waits for them, and re-layouts  1.14 us
    ppermute x1, waiting for transfers between devices, compact_plan(): shared = lax.ppermute(share, 'row', swap)  1.08 us
    pallas_call x1, Pallas kernels, compact_plan(): pl.pallas_call(load_kernel, in_specs=[pl.BlockSpec(memory_space=pltpu.SME...  1.08 us
    pallas_call x1, Pallas kernels, local(): pl.pallas_call(functools.partial(finish_kernel, float(field.size * device...  0.98 us
  transfers between devices with their start and end apart: 7, of which 3 were waited for; matrix products, arithmetic and copies ran while one was open for 0% of the time, Pallas kernels for 6%

profile of v9, /device:TPU:0, one launch (start us, length us, event | category | flops | bytes accessed | tf_op | source)
XLA Modules:
  0.0 28.0 jit_solution(4932952286696136949)
XLA Ops:
  0.6 0.5 %collective-permute-start = (f32[192,128]{1,0:T(8,128)}, f32[192,128]{1,0:T(8,128)S(1)}, u32[]{:S(2)}, u32[]{:S(2)}) collective-permute-start(f32[192,128]{1,0:T(8,128)} %bitcast.7), channel_id=1, source_target_pairs={{0,1},{1,0},{2,3},{3,2},{4,5},{5,4},{6,7},{7,6},{8,9},{9,8},{10,11... | collective-permute-start | bytes 294920 | tf_op jit(solution)/shard_map/ppermute | solution.py:912
  1.1 0.1 collective-permute-start.1
  1.2 1.1 %shard_map.68 = (f32[8,128]{1,0:T(8,128)S(1)}, f32[192,128]{1,0:T(8,128)S(1)}, f32[192,128]{1,0:T(8,128)S(1)}, f32[120,128]{1,0:T(8,128)S(1)}, f32[48,128]{1,0:T(8,128)S(1)}) custom-call(f32[8]{0:T(128)} %conductance.1, s32[8,128]{1,0:T(8,128)} %region.1, f32[192,128]{1,0:T(8,128)} %bitcast.8, f32[192,128]{1,0:T(8,128)} %bitcast.10), custom_call_target="tpu_custom_call" | custom-call | tf_op jit(solution)/shard_map/pallas_call | solution.py:914
  2.3 0.0 collective-permute-done.far_field
  2.3 0.3 %collective-permute-done.1.far_flow = f32[192,128]{1,0:T(8,128)S(1)} collective-permute-done((f32[192,128]{1,0:T(8,128)}, f32[192,128]{1,0:T(8,128)S(1)}, u32[]{:S(2)}, u32[]{:S(2)}) %collective-permute-start.1) | collective-permute-done | bytes 98336 | tf_op jit(solution)/shard_map/ppermute | solution.py:913
  2.7 0.2 shard_map.69
  2.9 2.8 %collective-permute-start.2 = (f32[288,128]{1,0:T(8,128)S(1)}, f32[288,128]{1,0:T(8,128)S(1)}, u32[]{:S(2)}, u32[]{:S(2)}) collective-permute-start(f32[288,128]{1,0:T(8,128)S(1)} %get-tuple-element.24), channel_id=1, source_target_pairs={{0,4},{1,13},{2,6},{3,15},{4,0},{5,9},{6,2},{7,11},{8,12},{9,5},{1... | collective-permute-start | bytes 442376 | tf_op jit(solution)/shard_map/ppermute | solution.py:906
  5.7 1.1 %collective-permute-start.3 = (f32[120,128]{1,0:T(8,128)S(1)}, f32[120,128]{1,0:T(8,128)S(1)}, u32[]{:S(2)}, u32[]{:S(2)}) collective-permute-start(f32[120,128]{1,0:T(8,128)S(1)} %get-tuple-element.25), channel_id=1, source_target_pairs={{0,9},{1,0},{2,11},{3,2},{4,13},{5,4},{6,15},{7,6},{8,1},{9,8},{10... | collective-permute-start | bytes 184328 | tf_op jit(solution)/shard_map/ppermute | solution.py:906
  6.8 2.5 %collective-permute-start.5 = (f32[56,128]{1,0:T(8,128)S(1)}, f32[56,128]{1,0:T(8,128)S(1)}, u32[]{:S(2)}, u32[]{:S(2)}) collective-permute-start(f32[56,128]{1,0:T(8,128)S(1)} %get-tuple-element.23.strip), channel_id=1, source_target_pairs={{0,11},{1,2},{2,9},{3,0},{4,15},{5,6},{6,13},{7,4},{8,3},{9,10},{1... | collective-permute-start | bytes 86024 | tf_op jit(solution)/shard_map/ppermute | solution.py:906
  9.3 0.4 %collective-permute-start.4 = (f32[32,128]{1,0:T(8,128)S(1)}, f32[32,128]{1,0:T(8,128)S(1)}, u32[]{:S(2)}, u32[]{:S(2)}) collective-permute-start(f32[32,128]{1,0:T(8,128)S(1)} %get-tuple-element.26), channel_id=1, source_target_pairs={{0,6},{1,15},{2,4},{3,13},{4,2},{5,11},{6,0},{7,9},{8,14},{9,7},{1... | collective-permute-start | bytes 49160 | tf_op jit(solution)/shard_map/ppermute | solution.py:906
  9.7 0.0 copy-start
  9.7 1.1 %copy-done = f32[8,3,8,8,128]{4,3,2,1,0:T(8,128)S(1)} copy-done((f32[8,3,8,8,128]{4,3,2,1,0:T(8,128)S(1)}, f32[8,3,8,8,128]{4,3,2,1,0:T(8,128)}, u32[]{:S(2)}) %copy-start) | copy-done | bytes 786456
  10.8 0.0 copy-start.1
  10.8 0.5 %shard_map.70.gram = f32[1,128]{1,0:T(1,128)S(1)} custom-call(f32[1536,128]{1,0:T(8,128)S(1)} %bitcast.4), custom_call_target="tpu_custom_call" | custom-call | tf_op jit(solution)/shard_map/pallas_call | solution.py:942
  11.4 0.0 collective-permute-done.3.turn
  11.4 2.6 %collective-permute-done.4.diagonal = f32[32,128]{1,0:T(8,128)S(1)} collective-permute-done((f32[32,128]{1,0:T(8,128)S(1)}, f32[32,128]{1,0:T(8,128)S(1)}, u32[]{:S(2)}, u32[]{:S(2)}) %collective-permute-start.4) | collective-permute-done | bytes 16416 | tf_op jit(solution)/shard_map/ppermute | solution.py:906
  14.0 0.0 collective-permute-done.5.opposite
  14.0 0.0 collective-permute-done.2.side
  14.0 0.9 %collective-permute-start.6 = (f32[400,128]{1,0:T(8,128)S(1)}, f32[400,128]{1,0:T(8,128)S(1)}, u32[]{:S(2)}, u32[]{:S(2)}) collective-permute-start(f32[400,128]{1,0:T(8,128)S(1)} %shard_map.71), channel_id=1, source_target_pairs={{0,1},{1,0},{2,3},{3,2},{4,5},{5,4},{6,7},{7,6},{8,9},{9,8},{10,11... | collective-permute-start | bytes 614408 | tf_op jit(solution)/shard_map/ppermute | solution.py:951
  14.9 1.1 %collective-permute-done.6.shared = f32[400,128]{1,0:T(8,128)S(1)} collective-permute-done((f32[400,128]{1,0:T(8,128)S(1)}, f32[400,128]{1,0:T(8,128)S(1)}, u32[]{:S(2)}, u32[]{:S(2)}) %collective-permute-start.6) | collective-permute-done | bytes 204832 | tf_op jit(solution)/shard_map/ppermute | solution.py:951
  16.0 0.0 copy-done.1
  16.0 1.5 %shard_map.72 = (f32[16,1,128]{2,1,0:T(1,128)S(1)}, f32[192,128]{1,0:T(8,128)S(1)}) custom-call(f32[192,128]{1,0:T(8,128)S(1)} %get-tuple-element.19.field, f32[192,128]{1,0:T(8,128)S(1)} %get-tuple-element.20.velocity, f32[192,128]{1,0:T(8,128)S(1)} %collective-permute-done.far_field, f32[192,128]{1,0:T(8,128)S(1)} %collective-permute-done.1.far_flow, ...), custom_call_target="tpu_custom_call" | custom-call | tf_op jit(solution)/shard_map/pallas_call | solution.py:953
  17.5 9.5 %all_to_all.5.messages = f32[16,1,128]{2,1,0:T(1,128)S(1)} all-to-all(f32[16,1,128]{2,1,0:T(1,128)S(1)} %get-tuple-element.32), channel_id=1, replica_groups=mesh['groups'=2,'phi'=4,'gz'=2,'row'=2] {'phi','gz','row'}, dimensions={0} | all-to-all | bytes 16384 | tf_op jit(solution)/shard_map/all_to_all | solution.py:975
  27.0 1.0 %shard_map.73 = (f32[192,128]{1,0:T(8,128)}, f32[9]{0:T(128)}) custom-call(f32[16,1,128]{2,1,0:T(1,128)S(1)} %all_to_all.5.messages, f32[192,128]{1,0:T(8,128)S(1)} %get-tuple-element.33.advanced, f32[1536,128]{1,0:T(8,128)S(1)} %bitcast.6), custom_call_target="tpu_custom_call" | custom-call | tf_op jit(solution)/shard_map/pallas_call | solution.py:977
  (1 shorter events, 0.0 us)
Async XLA Ops:
  0.6 1.7 %collective-permute-start = (f32[192,128]{1,0:T(8,128)}, f32[192,128]{1,0:T(8,128)S(1)}, u32[]{:S(2)}, u32[]{:S(2)}) collective-permute-start(f32[192,128]{1,0:T(8,128)} %bitcast.7), channel_id=1, source_target_pairs={{0,1},{1,0},{2,3},{3,2},{4,5},{5,4},{6,7},{7,6},{8,9},{9,8},{10,11... | collective-permute-start | bytes 294920 | tf_op jit(solution)/shard_map/ppermute | solution.py:912
  1.1 1.5 %collective-permute-start.1 = (f32[192,128]{1,0:T(8,128)}, f32[192,128]{1,0:T(8,128)S(1)}, u32[]{:S(2)}, u32[]{:S(2)}) collective-permute-start(f32[192,128]{1,0:T(8,128)} %bitcast.9), channel_id=1, source_target_pairs={{0,1},{1,0},{2,3},{3,2},{4,5},{5,4},{6,7},{7,6},{8,9},{9,8},{10,11... | collective-permute-start | bytes 294920 | tf_op jit(solution)/shard_map/ppermute | solution.py:913
  2.9 11.1 %collective-permute-start.2 = (f32[288,128]{1,0:T(8,128)S(1)}, f32[288,128]{1,0:T(8,128)S(1)}, u32[]{:S(2)}, u32[]{:S(2)}) collective-permute-start(f32[288,128]{1,0:T(8,128)S(1)} %get-tuple-element.24), channel_id=1, source_target_pairs={{0,4},{1,13},{2,6},{3,15},{4,0},{5,9},{6,2},{7,11},{8,12},{9,5},{1... | collective-permute-start | bytes 442376 | tf_op jit(solution)/shard_map/ppermute | solution.py:906
  5.7 5.7 %collective-permute-start.3 = (f32[120,128]{1,0:T(8,128)S(1)}, f32[120,128]{1,0:T(8,128)S(1)}, u32[]{:S(2)}, u32[]{:S(2)}) collective-permute-start(f32[120,128]{1,0:T(8,128)S(1)} %get-tuple-element.25), channel_id=1, source_target_pairs={{0,9},{1,0},{2,11},{3,2},{4,13},{5,4},{6,15},{7,6},{8,1},{9,8},{10... | collective-permute-start | bytes 184328 | tf_op jit(solution)/shard_map/ppermute | solution.py:906
  6.8 7.2 %collective-permute-start.5 = (f32[56,128]{1,0:T(8,128)S(1)}, f32[56,128]{1,0:T(8,128)S(1)}, u32[]{:S(2)}, u32[]{:S(2)}) collective-permute-start(f32[56,128]{1,0:T(8,128)S(1)} %get-tuple-element.23.strip), channel_id=1, source_target_pairs={{0,11},{1,2},{2,9},{3,0},{4,15},{5,6},{6,13},{7,4},{8,3},{9,10},{1... | collective-permute-start | bytes 86024 | tf_op jit(solution)/shard_map/ppermute | solution.py:906
  9.3 4.7 %collective-permute-start.4 = (f32[32,128]{1,0:T(8,128)S(1)}, f32[32,128]{1,0:T(8,128)S(1)}, u32[]{:S(2)}, u32[]{:S(2)}) collective-permute-start(f32[32,128]{1,0:T(8,128)S(1)} %get-tuple-element.26), channel_id=1, source_target_pairs={{0,6},{1,15},{2,4},{3,13},{4,2},{5,11},{6,0},{7,9},{8,14},{9,7},{1... | collective-permute-start | bytes 49160 | tf_op jit(solution)/shard_map/ppermute | solution.py:906
  9.7 1.1 %copy-start = (f32[8,3,8,8,128]{4,3,2,1,0:T(8,128)S(1)}, f32[8,3,8,8,128]{4,3,2,1,0:T(8,128)}, u32[]{:S(2)}) copy-start(f32[8,3,8,8,128]{4,3,2,1,0:T(8,128)} %param.7) | copy-start | bytes 2359300
  10.8 5.2 %copy-start.1 = (f32[8,3,8,8,128]{4,3,2,1,0:T(8,128)S(1)}, f32[8,3,8,8,128]{4,3,2,1,0:T(8,128)}, u32[]{:S(2)}) copy-start(f32[8,3,8,8,128]{4,3,2,1,0:T(8,128)} %param.7) | copy-start | bytes 2359300
  14.0 2.0 %collective-permute-start.6 = (f32[400,128]{1,0:T(8,128)S(1)}, f32[400,128]{1,0:T(8,128)S(1)}, u32[]{:S(2)}, u32[]{:S(2)}) collective-permute-start(f32[400,128]{1,0:T(8,128)S(1)} %shard_map.71), channel_id=1, source_target_pairs={{0,1},{1,0},{2,3},{3,2},{4,5},{5,4},{6,7},{7,6},{8,9},{9,8},{10,11... | collective-permute-start | bytes 614408 | tf_op jit(solution)/shard_map/ppermute | solution.py:951

commit v10 on v8

--- a/solution.py
+++ b/solution.py
@@ -745,7 +745,9 @@
 
 def finish_kernel(cell_count, messages, advanced, basis, out, hessenberg):
     count = basis.shape[0] // 192
-    terms = [messages[device] for device in range(messages.shape[0])]
+    terms = [
+        jnp.broadcast_to(messages[device], (8, 128)) for device in range(messages.shape[0])
+    ]
     errors = []
     while len(terms) > 1:
         pairs = [two_sum(a, b) for a, b in zip(terms[::2], terms[1::2])]
@@ -754,12 +756,12 @@
     while len(errors) > 1:
         errors = [a + b for a, b in zip(errors[::2], errors[1::2])] + errors[len(errors) // 2 * 2 :]
     total = terms[0]
-    rest = pltpu.roll(jnp.broadcast_to(total, (8, 128)), 64, 1)
+    rest = pltpu.roll(total, 64, 1)
     rest = rest + errors[0] if errors else rest
 
     def entry(index):
         high = jnp.broadcast_to(total[:, index : index + 1], (8, 128))
-        return high, jnp.broadcast_to(rest[:1, index : index + 1], (8, 128))
+        return high, jnp.broadcast_to(rest[:, index : index + 1], (8, 128))
 
     pending, pending_rest = [list(part) for part in zip(*[entry(m) for m in range(count)])]
     energy, energy_rest = entry(count)

time: 28.3 us -> 28.3 us (level)
  no operation moved by 1% of the time
where the time goes in v10:
time: 28.3 us; the launch traced here: 28.1 us
  blocking collectives  9.53 us (34%)
  starting transfers between devices  8.37 us (30%)
  Pallas kernels  4.22 us (15%)
  waiting for transfers between devices  4.14 us (15%)
  local copies, waits for them, and re-layouts  1.14 us (4%)
  between operations  0.67 us (2%)
    all_to_all x1, blocking collectives, local(): messages = lax.all_to_all(message, axes, 0, 0, tiled=True)  9.53 us
    ppermute x4, starting transfers between devices, exchange(): return lax.ppermute(value, axes, pairs)  6.84 us
    ppermute x4, waiting for transfers between devices, exchange(): return lax.ppermute(value, axes, pairs)  2.61 us
    pallas_call x1, Pallas kernels, compact_plan(): pl.pallas_call(compact_kernel, in_specs=vmem(12), out_specs=vmem(2), out_...  1.45 us
    unnamed x4, local copies, waits for them, and re-layouts  1.14 us
    ppermute x1, waiting for transfers between devices, compact_plan(): shared = lax.ppermute(share, 'row', swap)  1.08 us
    pallas_call x1, Pallas kernels, local(): pl.pallas_call(functools.partial(finish_kernel, float(field.size * device...  0.98 us
    pallas_call x1, Pallas kernels, compact_plan(): pl.pallas_call(load_kernel, in_specs=[pl.BlockSpec(memory_space=pltpu.SME...  0.98 us
  transfers between devices with their start and end apart: 7, of which 4 were waited for; matrix products, arithmetic and copies ran while one was open for 0% of the time, Pallas kernels for 5%

profile of v10, /device:TPU:0, one launch (start us, length us, event | category | flops | bytes accessed | tf_op | source)
XLA Modules:
  0.0 28.1 jit_solution(14621802068340733278)
XLA Ops:
  0.6 0.5 %collective-permute-start = (f32[192,128]{1,0:T(8,128)}, f32[192,128]{1,0:T(8,128)S(1)}, u32[]{:S(2)}, u32[]{:S(2)}) collective-permute-start(f32[192,128]{1,0:T(8,128)} %bitcast.7), channel_id=1, source_target_pairs={{0,1},{1,0},{2,3},{3,2},{4,5},{5,4},{6,7},{7,6},{8,9},{9,8},{10,11... | collective-permute-start | bytes 294920 | tf_op jit(solution)/shard_map/ppermute | solution.py:906
  1.1 0.1 collective-permute-start.1
  1.2 1.0 %shard_map.68 = (f32[8,128]{1,0:T(8,128)S(1)}, f32[192,128]{1,0:T(8,128)S(1)}, f32[192,128]{1,0:T(8,128)S(1)}) custom-call(f32[8]{0:T(128)} %conductance.1, s32[8,128]{1,0:T(8,128)} %region.1, f32[192,128]{1,0:T(8,128)} %bitcast.8, f32[192,128]{1,0:T(8,128)} %bitcast.10), custom_call_target="tpu_custom_call" | custom-call | tf_op jit(solution)/shard_map/pallas_call | solution.py:908
  2.2 0.1 collective-permute-done.far_field
  2.3 0.4 %collective-permute-done.1.far_flow = f32[192,128]{1,0:T(8,128)S(1)} collective-permute-done((f32[192,128]{1,0:T(8,128)}, f32[192,128]{1,0:T(8,128)S(1)}, u32[]{:S(2)}, u32[]{:S(2)}) %collective-permute-start.1) | collective-permute-done | bytes 98336 | tf_op jit(solution)/shard_map/ppermute | solution.py:907
  2.7 0.3 shard_map.69
  2.9 2.8 %collective-permute-start.2 = (f32[288,128]{1,0:T(8,128)S(1)}, f32[288,128]{1,0:T(8,128)S(1)}, u32[]{:S(2)}, u32[]{:S(2)}) collective-permute-start(f32[288,128]{1,0:T(8,128)S(1)} %get-tuple-element.22), channel_id=1, source_target_pairs={{0,4},{1,13},{2,6},{3,15},{4,0},{5,9},{6,2},{7,11},{8,12},{9,5},{1... | collective-permute-start | bytes 442376 | tf_op jit(solution)/shard_map/ppermute | solution.py:900
  5.7 1.1 %collective-permute-start.3 = (f32[120,128]{1,0:T(8,128)S(1)}, f32[120,128]{1,0:T(8,128)S(1)}, u32[]{:S(2)}, u32[]{:S(2)}) collective-permute-start(f32[120,128]{1,0:T(8,128)S(1)} %get-tuple-element.23), channel_id=1, source_target_pairs={{0,9},{1,0},{2,11},{3,2},{4,13},{5,4},{6,15},{7,6},{8,1},{9,8},{10... | collective-permute-start | bytes 184328 | tf_op jit(solution)/shard_map/ppermute | solution.py:900
  6.9 2.5 %collective-permute-start.5 = (f32[56,128]{1,0:T(8,128)S(1)}, f32[56,128]{1,0:T(8,128)S(1)}, u32[]{:S(2)}, u32[]{:S(2)}) collective-permute-start(f32[56,128]{1,0:T(8,128)S(1)} %get-tuple-element.21.strip), channel_id=1, source_target_pairs={{0,11},{1,2},{2,9},{3,0},{4,15},{5,6},{6,13},{7,4},{8,3},{9,10},{1... | collective-permute-start | bytes 86024 | tf_op jit(solution)/shard_map/ppermute | solution.py:900
  9.3 0.4 %collective-permute-start.4 = (f32[32,128]{1,0:T(8,128)S(1)}, f32[32,128]{1,0:T(8,128)S(1)}, u32[]{:S(2)}, u32[]{:S(2)}) collective-permute-start(f32[32,128]{1,0:T(8,128)S(1)} %get-tuple-element.24), channel_id=1, source_target_pairs={{0,6},{1,15},{2,4},{3,13},{4,2},{5,11},{6,0},{7,9},{8,14},{9,7},{1... | collective-permute-start | bytes 49160 | tf_op jit(solution)/shard_map/ppermute | solution.py:900
  9.8 0.0 copy-start
  9.8 1.1 %copy-done = f32[8,3,8,8,128]{4,3,2,1,0:T(8,128)S(1)} copy-done((f32[8,3,8,8,128]{4,3,2,1,0:T(8,128)S(1)}, f32[8,3,8,8,128]{4,3,2,1,0:T(8,128)}, u32[]{:S(2)}) %copy-start) | copy-done | bytes 786456
  10.9 0.0 copy-start.1
  10.9 0.5 %shard_map.70.gram = f32[1,128]{1,0:T(1,128)S(1)} custom-call(f32[1536,128]{1,0:T(8,128)S(1)} %bitcast.4), custom_call_target="tpu_custom_call" | custom-call | tf_op jit(solution)/shard_map/pallas_call | solution.py:931
  11.4 2.6 %collective-permute-done.4.diagonal = f32[32,128]{1,0:T(8,128)S(1)} collective-permute-done((f32[32,128]{1,0:T(8,128)S(1)}, f32[32,128]{1,0:T(8,128)S(1)}, u32[]{:S(2)}, u32[]{:S(2)}) %collective-permute-start.4) | collective-permute-done | bytes 16416 | tf_op jit(solution)/shard_map/ppermute | solution.py:900
  14.0 0.0 collective-permute-done.5.opposite
  14.0 0.0 collective-permute-done.3.turn
  14.0 0.0 collective-permute-done.2.side
  14.1 0.9 %collective-permute-start.6 = (f32[400,128]{1,0:T(8,128)S(1)}, f32[400,128]{1,0:T(8,128)S(1)}, u32[]{:S(2)}, u32[]{:S(2)}) collective-permute-start(f32[400,128]{1,0:T(8,128)S(1)} %shard_map.71), channel_id=1, source_target_pairs={{0,1},{1,0},{2,3},{3,2},{4,5},{5,4},{6,7},{7,6},{8,9},{9,8},{10,11... | collective-permute-start | bytes 614408 | tf_op jit(solution)/shard_map/ppermute | solution.py:940
  15.0 1.1 %collective-permute-done.6.shared = f32[400,128]{1,0:T(8,128)S(1)} collective-permute-done((f32[400,128]{1,0:T(8,128)S(1)}, f32[400,128]{1,0:T(8,128)S(1)}, u32[]{:S(2)}, u32[]{:S(2)}) %collective-permute-start.6) | collective-permute-done | bytes 204832 | tf_op jit(solution)/shard_map/ppermute | solution.py:940
  16.1 0.0 copy-done.1
  16.1 1.5 %shard_map.72 = (f32[16,1,128]{2,1,0:T(1,128)S(1)}, f32[192,128]{1,0:T(8,128)S(1)}) custom-call(f32[192,128]{1,0:T(8,128)S(1)} %get-tuple-element.18.field, f32[192,128]{1,0:T(8,128)S(1)} %get-tuple-element.19.velocity, f32[192,128]{1,0:T(8,128)S(1)} %collective-permute-done.far_field, f32[192,128]{1,0:T(8,128)S(1)} %collective-permute-done.1.far_flow, ...), custom_call_target="tpu_custom_call" | custom-call | tf_op jit(solution)/shard_map/pallas_call | solution.py:942
  17.6 9.5 %all_to_all.5.messages = f32[16,1,128]{2,1,0:T(1,128)S(1)} all-to-all(f32[16,1,128]{2,1,0:T(1,128)S(1)} %get-tuple-element.30), channel_id=1, replica_groups=mesh['groups'=2,'phi'=4,'gz'=2,'row'=2] {'phi','gz','row'}, dimensions={0} | all-to-all | bytes 16384 | tf_op jit(solution)/shard_map/all_to_all | solution.py:964
  27.1 1.0 %shard_map.73 = (f32[192,128]{1,0:T(8,128)}, f32[9]{0:T(128)}) custom-call(f32[16,1,128]{2,1,0:T(1,128)S(1)} %all_to_all.5.messages, f32[192,128]{1,0:T(8,128)S(1)} %get-tuple-element.31.advanced, f32[1536,128]{1,0:T(8,128)S(1)} %bitcast.6), custom_call_target="tpu_custom_call" | custom-call | tf_op jit(solution)/shard_map/pallas_call | solution.py:966
  (1 shorter events, 0.0 us)
Async XLA Ops:
  0.6 1.7 %collective-permute-start = (f32[192,128]{1,0:T(8,128)}, f32[192,128]{1,0:T(8,128)S(1)}, u32[]{:S(2)}, u32[]{:S(2)}) collective-permute-start(f32[192,128]{1,0:T(8,128)} %bitcast.7), channel_id=1, source_target_pairs={{0,1},{1,0},{2,3},{3,2},{4,5},{5,4},{6,7},{7,6},{8,9},{9,8},{10,11... | collective-permute-start | bytes 294920 | tf_op jit(solution)/shard_map/ppermute | solution.py:906
  1.1 1.5 %collective-permute-start.1 = (f32[192,128]{1,0:T(8,128)}, f32[192,128]{1,0:T(8,128)S(1)}, u32[]{:S(2)}, u32[]{:S(2)}) collective-permute-start(f32[192,128]{1,0:T(8,128)} %bitcast.9), channel_id=1, source_target_pairs={{0,1},{1,0},{2,3},{3,2},{4,5},{5,4},{6,7},{7,6},{8,9},{9,8},{10,11... | collective-permute-start | bytes 294920 | tf_op jit(solution)/shard_map/ppermute | solution.py:907
  2.9 11.1 %collective-permute-start.2 = (f32[288,128]{1,0:T(8,128)S(1)}, f32[288,128]{1,0:T(8,128)S(1)}, u32[]{:S(2)}, u32[]{:S(2)}) collective-permute-start(f32[288,128]{1,0:T(8,128)S(1)} %get-tuple-element.22), channel_id=1, source_target_pairs={{0,4},{1,13},{2,6},{3,15},{4,0},{5,9},{6,2},{7,11},{8,12},{9,5},{1... | collective-permute-start | bytes 442376 | tf_op jit(solution)/shard_map/ppermute | solution.py:900
  5.7 8.3 %collective-permute-start.3 = (f32[120,128]{1,0:T(8,128)S(1)}, f32[120,128]{1,0:T(8,128)S(1)}, u32[]{:S(2)}, u32[]{:S(2)}) collective-permute-start(f32[120,128]{1,0:T(8,128)S(1)} %get-tuple-element.23), channel_id=1, source_target_pairs={{0,9},{1,0},{2,11},{3,2},{4,13},{5,4},{6,15},{7,6},{8,1},{9,8},{10... | collective-permute-start | bytes 184328 | tf_op jit(solution)/shard_map/ppermute | solution.py:900
  6.9 7.2 %collective-permute-start.5 = (f32[56,128]{1,0:T(8,128)S(1)}, f32[56,128]{1,0:T(8,128)S(1)}, u32[]{:S(2)}, u32[]{:S(2)}) collective-permute-start(f32[56,128]{1,0:T(8,128)S(1)} %get-tuple-element.21.strip), channel_id=1, source_target_pairs={{0,11},{1,2},{2,9},{3,0},{4,15},{5,6},{6,13},{7,4},{8,3},{9,10},{1... | collective-permute-start | bytes 86024 | tf_op jit(solution)/shard_map/ppermute | solution.py:900
  9.3 4.7 %collective-permute-start.4 = (f32[32,128]{1,0:T(8,128)S(1)}, f32[32,128]{1,0:T(8,128)S(1)}, u32[]{:S(2)}, u32[]{:S(2)}) collective-permute-start(f32[32,128]{1,0:T(8,128)S(1)} %get-tuple-element.24), channel_id=1, source_target_pairs={{0,6},{1,15},{2,4},{3,13},{4,2},{5,11},{6,0},{7,9},{8,14},{9,7},{1... | collective-permute-start | bytes 49160 | tf_op jit(solution)/shard_map/ppermute | solution.py:900
  9.8 1.1 %copy-start = (f32[8,3,8,8,128]{4,3,2,1,0:T(8,128)S(1)}, f32[8,3,8,8,128]{4,3,2,1,0:T(8,128)}, u32[]{:S(2)}) copy-start(f32[8,3,8,8,128]{4,3,2,1,0:T(8,128)} %param.7) | copy-start | bytes 2359300
  10.9 5.2 %copy-start.1 = (f32[8,3,8,8,128]{4,3,2,1,0:T(8,128)S(1)}, f32[8,3,8,8,128]{4,3,2,1,0:T(8,128)}, u32[]{:S(2)}) copy-start(f32[8,3,8,8,128]{4,3,2,1,0:T(8,128)} %param.7) | copy-start | bytes 2359300
  14.1 2.0 %collective-permute-start.6 = (f32[400,128]{1,0:T(8,128)S(1)}, f32[400,128]{1,0:T(8,128)S(1)}, u32[]{:S(2)}, u32[]{:S(2)}) collective-permute-start(f32[400,128]{1,0:T(8,128)S(1)} %shard_map.71), channel_id=1, source_target_pairs={{0,1},{1,0},{2,3},{3,2},{4,5},{5,4},{6,7},{7,6},{8,9},{9,8},{10,11... | collective-permute-start | bytes 614408 | tf_op jit(solution)/shard_map/ppermute | solution.py:940
